TPU v7x, 32 devices: a whole 2x2x4 slice. The times are simulated.
32 devices in a mesh: groups: 2 (over y), dp: 16 (over z, x, core).
Axes of the slice: x: 2, y: 2, z: 4, core: 2. Of those that a mesh axis runs over, the one named last changes fastest.
Arguments:
- particles: bfloat16 [2048, 128, 128], P(('groups', 'dp')), parts along dimension 0, may hold values from -20 to 20
- refs: bfloat16 [128, 256, 128], P('dp', 'groups'), parts along dimension 1, may hold values from -0.5 to 0.5
- ctf_group: int32 [2048], P(('groups', 'dp')), parts along dimension 0, may hold values from 0 to 31, as said below
- defocus: float32 [64], P('groups'), parts along dimension 0, may hold values from 0.5 to 2
- class_prior: float32 [256], P('groups'), parts along dimension 0, may hold values from 0.25 to 4
- cycle_weight: float32 [64], replicated, may hold values from 0.5 to 2
Outputs:
- new_refs: float32 [128, 256, 128], P('dp', 'groups'), parts along dimension 1
- log_evidence: float32 [2048], P(('groups', 'dp')), parts along dimension 0
There are 2 independent parts, one for each index of `groups`. A program takes and returns all parts, laid end to end along the dimension named above; an argument that names none is the same for every part. Nothing has to cross between parts.
Inputs may be any that keep to these rules, and one draw needn't show every extreme that they name: `ctf_group`: CTF groups follow the particle order: particle n belongs to group n * 32 // 1024 or the next one, capped at 31.
All inputs are finite; a program needn't handle non-finite values.
Results may differ from a plain program's by a relative error of at most 0.0045.
Values may be sent and summed in bfloat16 or wider, within the bound.
No kernel may reach another device: no remote copies, remote signals or barrier semaphores. Data moves between devices by JAX's collectives and lax.ppermute only.
A program may use at most 64 MiB of HBM per device.

v0:
```python
import math

import jax
import jax.numpy as jnp
from jax import lax
from jax.sharding import PartitionSpec as P

M = 128
R = 64
ROT = 36
G = 32


def ctf_table(defocus):
    radius = (jnp.arange(R, dtype=jnp.float32) + 1.0) / R
    phase = 20.0 * defocus[:, None] * radius[None, :] ** 2
    return -(0.995 * jnp.sin(phase) + 0.1 * jnp.cos(phase))


def angle_tables():
    harmonic = jnp.arange(M, dtype=jnp.float32)[:, None]
    turning = jnp.arange(ROT, dtype=jnp.float32)[None, :]
    theta = 2.0 * math.pi * harmonic * turning / ROT
    return (jnp.cos(theta), jnp.sin(theta))


def shards(particles, refs, ctf_group, defocus, class_prior, cycle_weight):
    highest = lax.Precision.HIGHEST
    ctf = ctf_table(defocus)
    cos_table, sin_table = angle_tables()
    onehot = (ctf_group[:, None] == jnp.arange(G, dtype=jnp.int32)[None, :]).astype(jnp.float32)
    gain_table = jnp.concatenate([cycle_weight[None, :] * ctf, cycle_weight[None, :] * ctf], axis=1)
    gain = jnp.dot(onehot, gain_table, precision=highest)
    weighted = (particles.astype(jnp.float32) * gain[:, None, :]).astype(jnp.bfloat16)
    turned = jnp.concatenate([weighted[:, :, R:], -weighted[:, :, :R]], axis=2)
    all_refs = lax.all_gather(refs, "dp", axis=0, tiled=True)
    part_weighted = weighted
    part_turned = turned
    part_cos = cos_table
    part_sin = sin_table
    cross_real = jnp.einsum(
        "nmq,mkq->mnk", part_weighted, all_refs, preferred_element_type=jnp.float32
    )
    cross_imag = jnp.einsum(
        "nmq,mkq->mnk", part_turned, all_refs, preferred_element_type=jnp.float32
    )
    corr = jnp.einsum("mnk,mj->jnk", cross_real, part_cos, precision=highest)
    corr = corr - jnp.einsum("mnk,mj->jnk", cross_imag, part_sin, precision=highest)
    wide_refs = all_refs.astype(jnp.float32)
    energy = jnp.sum(wide_refs[:, :, :R] ** 2 + wide_refs[:, :, R:] ** 2, axis=0)
    corr, energy = (corr, energy)
    quadratic = jnp.dot(cycle_weight[None, :] * ctf * ctf, energy.T, precision=highest)
    norm_term = jnp.dot(onehot, quadratic, precision=highest)
    scores = corr - 0.5 * norm_term[None, :, :] + jnp.log(class_prior)[None, None, :]
    top = jnp.max(scores, axis=(0, 2), keepdims=True)
    expo = jnp.exp(scores - top)
    total = jnp.sum(expo, axis=(0, 2), keepdims=True)
    posterior = expo / total
    log_evidence = top[0, :, 0] + jnp.log(total[0, :, 0])
    local_mass = jnp.dot(onehot.T, jnp.sum(posterior, axis=0), precision=highest)
    mass = lax.psum(local_mass, "dp")
    part_cos = cos_table
    part_sin = sin_table
    post_real = jnp.einsum("jnk,mj->mnk", posterior, part_cos, precision=highest).astype(
        jnp.bfloat16
    )
    post_imag = jnp.einsum("jnk,mj->mnk", posterior, part_sin, precision=highest).astype(
        jnp.bfloat16
    )
    part_weighted = weighted
    part_turned = turned
    term = jnp.einsum("mnk,nmq->mkq", post_real, part_weighted, preferred_element_type=jnp.float32)
    numer = lax.psum_scatter(
        term
        - jnp.einsum("mnk,nmq->mkq", post_imag, part_turned, preferred_element_type=jnp.float32),
        "dp",
        scatter_dimension=0,
        tiled=True,
    )
    denom = 1.0 + jnp.dot(mass.T, cycle_weight[None, :] * ctf * ctf, precision=highest)
    denom_wide = jnp.concatenate([denom, denom], axis=1)
    new_refs = numer / denom_wide[None, :, :]
    return (new_refs, log_evidence)


def solution(mesh):
    in_specs = (
        P(("groups", "dp"), None, None),
        P("dp", "groups", None),
        P(("groups", "dp")),
        P("groups"),
        P("groups"),
        P(),
    )
    out_specs = (P("dp", "groups", None), P(("groups", "dp")))
    return jax.shard_map(shards, mesh=mesh, in_specs=in_specs, out_specs=out_specs, check_vma=False)
```

profile of v0, /device:TPU:0, one launch (start us, length us, event | category | flops | bytes accessed | tf_op | source)
XLA Modules:
  0.0 216.0 jit_solution(5967293046546979658)
XLA Ops:
  7.2 0.0 all-gather.2.cloned.1.call-start
  7.2 0.7 all-gather.2.cloned.1.call-update
  7.9 0.0 reduce-scatter.2.cloned.1.call-start
  7.9 0.7 log.6
  8.6 0.7 broadcast_multiply_fusion
  9.3 0.8 fusion.38
  10.1 0.9 fusion.20
  11.0 2.9 %multiply_convert_fusion = bf16[64,128,128]{2,0,1:T(8,128)(2,1)S(1)} fusion(bf16[64,128,128]{2,1,0:T(8,128)(2,1)} %param.6, f32[64,128]{1,0:T(8,128)S(1)} %fusion.20), kind=kLoop, calls=%fused_computation.10 | loop fusion | flops 3145728 | bytes 4227072 | tf_op jit(solution)/shard_map/convert_element_type | solution.py:34
  13.9 2.7 %fusion.70 = (bf16[64,128,64]{2,0,1:T(8,128)(2,1)}, bf16[64,128,64]{2,0,1:T(8,128)(2,1)}) fusion(bf16[64,128,128]{2,0,1:T(8,128)(2,1)S(1)} %multiply_convert_fusion), kind=kLoop, calls=%fused_computation.77 | loop fusion | flops 524288 | bytes 4194304 | tf_op jit(solution)/shard_map/slice | solution.py:35
  16.6 46.8 %all-gather.2.cloned.1.call-done = bf16[128,128,128]{2,1,0:T(8,128)(2,1)} async-done(((bf16[8,128,128]{2,1,0:T(8,128)(2,1)}), bf16[128,128,128]{2,1,0:T(8,128)(2,1)}) %all-gather.2.cloned.1.call-update) | async-done | bytes 4194320 | tf_op jit(solution)/shard_map/all_gather | solution.py:36
  63.5 3.2 %convert_element_type.18 = f32[128,128,128]{2,1,0:T(8,128)S(1)} convert(bf16[128,128,128]{2,1,0:T(8,128)(2,1)} %all-gather.2.cloned.1.call-done) | non-fusion elementwise | flops 2097152 | bytes 12582912 | tf_op jit(solution)/shard_map/convert_element_type | solution.py:49
  66.8 2.5 %fusion.1 = f32[128,64]{1,0:T(8,128)S(1)} fusion(f32[128,128,128]{2,1,0:T(8,128)S(1)} %convert_element_type.18), kind=kLoop, calls=%fused_computation.2 | loop fusion | flops 4186112 | bytes 8421376 | tf_op jit(solution)/shard_map/reduce_sum | solution.py:50
  69.3 0.3 fusion.54
  69.6 0.2 convolution_multiply_fusion
  69.9 0.3 copy-done.2
  70.2 3.0 %fusion.18 = f32[128,64,128]{2,1,0:T(8,128)S(1)} fusion(bf16[128,128,128]{2,1,0:T(8,128)(2,1)S(1)} %copy-done, bf16[64,128,64]{2,0,1:T(8,128)(2,1)S(1)} %copy-done.2, bf16[64,128,64]{2,0,1:T(8,128)(2,1)S(1)} %copy-done.1), kind=kOutput, calls=%fused_computation.23 | convolution fusion | flops 272629760 | bytes 10485760 | tf_op jit(solution)/shard_map/nmq,mkq->mnk/dot_general | solution.py:44
  73.2 4.7 %fusion.2 = f32[36,64,128]{2,0,1:T(8,128)S(1)} fusion(f32[128,64,128]{2,1,0:T(8,128)S(1)} %fusion.18, f32[128]{0:T(128)S(1)} %iota_multiply_fusion), kind=kOutput, calls=%fused_computation.6 | convolution fusion | flops 452994048 | bytes 5374464 | tf_op jit(solution)/shard_map/mnk,mj->jnk/dot_general | solution.py:48
  77.9 3.0 %fusion.72 = f32[128,64,128]{2,1,0:T(8,128)S(1)} fusion(bf16[64,128,128]{2,0,1:T(8,128)(2,1)S(1)} %multiply_convert_fusion, bf16[128,128,128]{2,1,0:T(8,128)(2,1)S(1)} %copy-done), kind=kOutput, calls=%fused_computation.79 | convolution fusion | flops 268435456 | bytes 10485760 | tf_op jit(solution)/shard_map/nmq,mkq->mnk/dot_general | solution.py:41
  80.8 5.3 %fusion.71 = (f32[64]{0:T(128)S(1)}, f32[36,64,128]{2,0,1:T(8,128)S(1)}) fusion(f32[128]{0:T(128)S(1)} %log.6, f32[64,128]{1,0:T(8,128)S(1)} %convolution_multiply_fusion, f32[36,64,128]{2,0,1:T(8,128)S(1)} %fusion.2, f32[128,64,128]{2,1,0:T(8,128)S(1)} %fusion.72, f32[128]{0:T(128)S(1)} %iota_multiply_fusion), kind=kOutput, calls=%fused_computation.78 | convolution fusion | flops 454173632 | bytes 6587648 | tf_op jit(solution)/shard_map/mnk,mj->jnk/dot_general | solution.py:47
  86.1 1.0 fusion.17
  87.1 3.9 %fusion.24 = bf16[128,64,128]{2,0,1:T(8,128)(2,1)S(1)} fusion(f32[128]{0:T(128)S(1)} %iota_multiply_fusion, f32[36,64,128]{2,0,1:T(8,128)S(1)} %get-tuple-element.5, f32[64]{0:T(128)S(1)} %fusion.17, f32[64]{0:T(128)S(1)} %get-tuple-element.4), kind=kOutput, calls=%fused_computation.34 | convolution fusion | flops 453583872 | bytes 3277824 | tf_op jit(solution)/shard_map/jnk,mj->mnk/dot_general | solution.py:64
  91.0 3.9 %fusion.21 = bf16[128,64,128]{2,0,1:T(8,128)(2,1)S(1)} fusion(f32[128]{0:T(128)S(1)} %iota_multiply_fusion, f32[36,64,128]{2,0,1:T(8,128)S(1)} %get-tuple-element.5, f32[64]{0:T(128)S(1)} %fusion.17, f32[64]{0:T(128)S(1)} %get-tuple-element.4), kind=kOutput, calls=%fused_computation.31 | convolution fusion | flops 453583872 | bytes 3277824 | tf_op jit(solution)/shard_map/jnk,mj->mnk/dot_general | solution.py:67
  94.9 2.0 fusion.6
  96.9 6.8 %convolution_subtract_fusion = f32[128,128,128]{2,1,0:T(8,128)} fusion(f32[128,128,128]{2,1,0:T(8,128)S(1)} %fusion.6, bf16[128,64,128]{2,0,1:T(8,128)(2,1)S(1)} %fusion.21, bf16[64,128,64]{2,0,1:T(8,128)(2,1)S(1)} %copy-done.2, bf16[64,128,64]{2,0,1:T(8,128)(2,1)S(1)} %copy-done.1), kind=kOutput, calls=%fused_computation.11 | convolution fusion | flops 274726912 | bytes 20971520 | tf_op jit(solution)/shard_map/mnk,nmq->mkq/dot_general | solution.py:75
  103.7 0.4 fusion.67
  104.1 0.3 fusion.19
  104.3 61.1 %psum.7 = f32[32,128]{1,0:T(8,128)S(1)} all-reduce(f32[32,128]{1,0:T(8,128)S(1)} %fusion.19), channel_id=1, replica_groups=mesh['groups'=2,'dp'=16] {'dp'}, use_global_device_ids=true, to_apply=%region_5.0 | all-reduce | flops 4096 | bytes 32768 | tf_op jit(solution)/shard_map/psum | solution.py:61
  165.4 0.4 convolution_add_fusion
  165.8 0.1 copy.11
  165.9 0.5 log_add_fusion
  166.4 40.8 %reduce-scatter.2.cloned.1.call-done = f32[8,128,128]{2,1,0:T(8,128)} async-done(((f32[128,128,128]{2,1,0:T(8,128)}), f32[8,128,128]{2,1,0:T(8,128)}) %reduce-scatter.2.cloned.1.call-update) | async-done | bytes 524304 | tf_op jit(solution)/shard_map/reduce_scatter | solution.py:73
  207.2 1.9 broadcast_divide_fusion
  (13 shorter events, 0.1 us)
Async XLA Ops:
  7.2 56.3 %all-gather.2.cloned.1.call-start = ((), (), s32[]{:S(2)}) async-start(), calls=%async_computation.1 | async-start | bytes 4456448 | tf_op jit(solution)/shard_map/all_gather | solution.py:36
  7.9 199.3 %reduce-scatter.2.cloned.1.call-start = ((), (), s32[]{:S(2)}) async-start(), calls=%async_computation.2 | async-start | bytes 8912896 | tf_op jit(solution)/shard_map/reduce_scatter | solution.py:73
  66.7 2.6 %copy-start.3 = (f32[64]{0:T(128)S(1)}, f32[64]{0:T(128)}, u32[]{:S(2)}) copy-start(f32[64]{0:T(128)} %param.11) | copy-start | bytes 772
  66.7 2.9 %copy-start.4 = (s32[64]{0:T(128)S(1)}, s32[64]{0:T(128)}, u32[]{:S(2)}) copy-start(s32[64]{0:T(128)} %param.8) | copy-start | bytes 772
  66.7 3.1 %copy-start = (bf16[128,128,128]{2,1,0:T(8,128)(2,1)S(1)}, bf16[128,128,128]{2,1,0:T(8,128)(2,1)}, u32[]{:S(2)}) copy-start(bf16[128,128,128]{2,1,0:T(8,128)(2,1)} %all-gather.2.cloned.1.call-done) | copy-start | bytes 12582916
  66.7 3.1 %copy-start.1 = (bf16[64,128,64]{2,0,1:T(8,128)(2,1)S(1)}, bf16[64,128,64]{2,0,1:T(8,128)(2,1)}, u32[]{:S(2)}) copy-start(bf16[64,128,64]{2,0,1:T(8,128)(2,1)} %get-tuple-element.2) | copy-start | bytes 3145732
  66.7 3.5 %copy-start.2 = (bf16[64,128,64]{2,0,1:T(8,128)(2,1)S(1)}, bf16[64,128,64]{2,0,1:T(8,128)(2,1)}, u32[]{:S(2)}) copy-start(bf16[64,128,64]{2,0,1:T(8,128)(2,1)} %get-tuple-element.3) | copy-start | bytes 3145732
Sparse Core Ops, SparseCore 0:
  10.2 53.2 all-gather.1
  103.8 103.3 reduce-scatter.1
where the time goes:
time: 216 us
  waiting for transfers between devices  88.4 us (41%)
  blocking collectives  61.1 us (28%)
  matrix products  34.5 us (16%)
  other arithmetic  16.6 us (8%)
  between operations  14.2 us (7%)
    psum x1, blocking collectives, shards(): mass = lax.psum(local_mass, 'dp')  61.1 us
    all_gather x1, waiting for transfers between devices, shards(): all_refs = lax.all_gather(refs, 'dp', axis=0, tiled=True)  46.8 us
    reduce_scatter x1, waiting for transfers between devices, shards(): lax.psum_scatter(term - jnp.einsum('mnk,nmq->mkq', post_imag, part_turned...  40.8 us
    dot_general x1, matrix products, shards(): jnp.einsum('mnk,nmq->mkq', post_imag, part_turned, preferred_element_type...  6.76 us
    dot_general x1, matrix products, shards(): corr = jnp.einsum('mnk,mj->jnk', cross_real, part_cos, precision=highest)  5.31 us
    dot_general x1, matrix products, shards(): jnp.einsum('mnk,mj->jnk', cross_imag, part_sin, precision=highest)  4.69 us
  transfers between devices with their start and end apart: 2, of which 2 were waited for; matrix products, arithmetic and copies ran while one was open for 5% of the time, Pallas kernels for 0%

commit v1 on v0

v1 whole, which is shorter than its diff:
```python
import functools
import math

import jax
import jax.numpy as jnp
import numpy as np
from jax import lax
from jax.experimental import pallas as pl
from jax.experimental.pallas import tpu as pltpu
from jax.sharding import PartitionSpec as P

ROT = 36
HALF = ROT // 2
HIGHEST = lax.Precision.HIGHEST
F32 = jnp.float32
BF16 = jnp.bfloat16
VMEM_LIMIT = 40 * 1024 * 1024


def chip_ring(mesh):
    chips = mesh.shape["dp"] // 2
    wide = 2
    coords = [getattr(d, "coords", None) for d in mesh.devices.reshape(-1, chips * 2)[0]]
    if all(c is not None for c in coords):
        wide = len({c[0] for c in coords})
    if chips % wide:
        wide = 1
    deep = chips // wide
    if wide == 1:
        return list(range(chips))
    ring = []
    for z in range(deep):
        xs = range(1, wide) if z % 2 == 0 else range(wide - 1, 0, -1)
        ring += [z * wide + x for x in xs]
    ring += [z * wide for z in range(deep - 1, -1, -1)]
    return ring


def ring_perm(ring, shift, cross):
    n = len(ring)
    pairs = []
    for at, chip in enumerate(ring):
        to = ring[(at + shift) % n]
        pairs += [(2 * chip + c, 2 * to + (c ^ cross)) for c in (0, 1)]
    return pairs


def _combine(terms):
    by = {}
    for k, v in terms:
        k %= ROT
        k = min(k, ROT - k)
        sign = 1
        if k > 9:
            k, sign = HALF - k, -1
        if k == 9:
            continue
        by.setdefault(k, []).append((sign, v))
    total = None
    for k, vs in sorted(by.items()):
        part, psign = None, 1
        for sign, v in vs:
            if part is None:
                part, psign = v, sign
            else:
                part = part + v if sign == psign else part - v
        if k:
            part = part * math.cos(k * math.pi / HALF)
        if total is None:
            total = part if psign > 0 else -part
        else:
            total = total + part if psign > 0 else total - part
    return total


def cos_transform(a):
    plus = [a[t] + a[HALF - t] for t in range(9)] + [a[9]]
    minus = [a[t] - a[HALF - t] for t in range(9)]
    out = [None] * 19
    for j in range(10):
        side = plus if j % 2 == 0 else minus
        even = _combine([(t * j, side[t]) for t in range(0, len(side), 2)])
        odd = _combine([(t * j, side[t]) for t in range(1, len(side), 2)])
        if odd is None:
            out[j] = out[HALF - j] = even
        else:
            out[j] = even + odd
            out[HALF - j] = even - odd
    return out


def sin_transform(b):
    plus = {t: b[t] + b[HALF - t] for t in range(1, 9)}
    plus[9] = b[9]
    minus = {t: b[t] - b[HALF - t] for t in range(1, 9)}
    out = [None] * 18
    for j in range(1, 10):
        side = plus if j % 2 else minus
        even = _combine([(9 - t * j, v) for t, v in side.items() if t % 2 == 0])
        odd = _combine([(9 - t * j, v) for t, v in side.items() if t % 2])
        if odd is None:
            odd = jnp.zeros_like(even)
        if even is None:
            even = jnp.zeros_like(odd)
        out[j] = odd + even
        if j != 9:
            out[HALF - j] = odd - even
    return out


def _residue(m):
    r = lax.rem(m, ROT)
    flip = r > HALF
    return jnp.where(flip, ROT - r, r), jnp.where(flip, -1.0, 1.0).astype(F32)


def _half_sign(shape):
    lane = lax.broadcasted_iota(jnp.int32, shape, len(shape) - 1)
    return jnp.where(lane < shape[-1] // 2, -1.0, 1.0).astype(F32)


def _forward(base, piece, wo, ws, acc, energy):
    mp, kh, q = piece.shape
    sign = _half_sign((kh, q))
    squares = jnp.zeros((kh, q), F32)
    for j in range(mp):
        t, s = _residue(base * mp + j)
        x = piece[j]
        wide = x.astype(F32)
        squares = squares + wide * wide
        swapped = (pltpu.roll(wide, q // 2, 1) * sign).astype(BF16)
        both = jnp.concatenate([x, swapped], axis=0)
        w = jnp.concatenate([wo[j], ws[j]], axis=0)
        y = lax.dot_general(both, w, (((1,), (1,)), ((), ())), preferred_element_type=F32)
        acc[t, :kh, :] += y[:kh]
        acc[t, kh:, :] += s * y[kh:]
    energy[...] += squares


def _backward(base, table, wo, ws, j, mp):
    t, s = _residue(base * mp + j)
    w = jnp.concatenate([wo[j], ws[j]], axis=0)
    y = jnp.dot(table[t], w, preferred_element_type=F32)
    kh = y.shape[0] // 2
    turned = pltpu.roll(y[kh:], y.shape[1] // 2, 1) * (_half_sign((kh, y.shape[1])) * s)
    return y[:kh] + turned


def forward_kernel(count, first, ids, *refs):
    pieces, rest = refs[:count], refs[count:]
    wos, wss, rest = rest[:count], rest[count : 2 * count], rest[2 * count :]
    if first:
        acc, energy = rest
        acc[...] = jnp.zeros_like(acc)
        energy[...] = jnp.zeros_like(energy)
    else:
        acc_in, energy_in, acc, energy = rest
        acc[...] = acc_in[...]
        energy[...] = energy_in[...]
    for i in range(count):
        _forward(ids[i], pieces[i], wos[i], wss[i], acc, energy)


def score_kernel(count, ids, *refs):
    pieces, rest = refs[:count], refs[count:]
    wos, wss, rest = rest[:count], rest[count : 2 * count], rest[2 * count :]
    acc_in, energy_in, w2, prior, real_out, imag_out, stats, acc, energy, scores = rest
    acc[...] = acc_in[...]
    energy[...] = energy_in[...]
    for i in range(count):
        _forward(ids[i], pieces[i], wos[i], wss[i], acc, energy)
    kh, n = scores.shape[1:]
    norm = lax.dot_general(
        energy[...], w2[...], (((1,), (1,)), ((), ())), precision=HIGHEST, preferred_element_type=F32
    )
    energy[...] = jnp.log(prior[...]) - 0.5 * norm
    tile = 8

    def scan_scores(i, top):
        at = pl.multiple_of(i * tile, tile)
        rows, rows_imag = pl.ds(at, tile), pl.ds(pl.multiple_of(kh + i * tile, tile), tile)
        p = cos_transform([acc[t, rows, :] for t in range(19)])
        q = sin_transform([None] + [acc[t, rows_imag, :] for t in range(1, HALF)])
        base = energy[rows, :]
        for j in range(19):
            pj = p[j] + base
            if j in (0, HALF):
                scores[j, rows, :] = pj
                top = jnp.maximum(top, pj)
            else:
                lo, hi = pj - q[j], pj + q[j]
                scores[j, rows, :] = lo
                scores[ROT - j, rows, :] = hi
                top = jnp.maximum(top, jnp.maximum(lo, hi))
        return top

    top = lax.fori_loop(0, kh // tile, scan_scores, jnp.full((tile, n), -jnp.inf, F32))
    top = jnp.max(top, axis=0, keepdims=True)

    def scan_exp(i, total):
        rows = pl.ds(pl.multiple_of(i * tile, tile), tile)
        u = [jnp.exp(scores[j, rows, :] - top) for j in range(ROT)]
        plus = [u[0]] + [u[j] + u[ROT - j] for j in range(1, HALF)] + [u[HALF]]
        minus = [None] + [u[j] - u[ROT - j] for j in range(1, HALF)]
        real = cos_transform(plus)
        imag = sin_transform(minus)
        for t in range(19):
            real_out[t, rows, :] = real[t]
        for t in range(1, HALF):
            imag_out[t - 1, rows, :] = imag[t]
        return total + real[0]

    total = lax.fori_loop(0, kh // tile, scan_exp, jnp.zeros((tile, n), F32))
    stats[0:1, :] = top
    stats[1:2, :] = jnp.sum(total, axis=0, keepdims=True)


def table_kernel(count, ids, real, imag, mine, other, w2, *refs):
    wos, wss, rest = refs[:count], refs[count : 2 * count], refs[2 * count :]
    table, evidence, dpart, outs = rest[0], rest[1], rest[2], rest[3:]
    kh, n = real.shape[1:]
    theirs = pltpu.roll(jnp.broadcast_to(other[...].reshape(2, 1, n), (2, 8, n)).reshape(16, n), n // 2, 1)
    top_a, total_a = mine[0:1, :], mine[1:2, :]
    top_b, total_b = theirs[0:1, :], theirs[8:9, :]
    top = jnp.maximum(top_a, top_b)
    scale = jnp.exp(top_a - top)
    total = total_a * scale + total_b * jnp.exp(top_b - top)
    evidence[...] = top + jnp.log(total)
    scale = scale / total
    for t in range(19):
        table[t, :kh, :] = (real[t] * scale).astype(BF16)
        if 0 < t < HALF:
            table[t, kh:, :] = (imag[t - 1] * scale).astype(BF16)
        else:
            table[t, kh:, :] = jnp.zeros((kh, n), BF16)
    dpart[...] = jnp.dot(real[0] * scale, w2[...], precision=HIGHEST, preferred_element_type=F32)
    for i in range(count):
        mp = outs[i].shape[0]
        for j in range(mp):
            outs[i][j] = _backward(ids[i], table, wos[i], wss[i], j, mp).astype(outs[i].dtype)


def numer_kernel(count, init, ids, table, *refs):
    wos, wss, rest = refs[:count], refs[count : 2 * count], refs[2 * count :]
    inits, outs = (rest[:count], rest[count:]) if init else (None, rest)
    for i in range(count):
        mp = outs[i].shape[0]
        for j in range(mp):
            y = _backward(ids[i], table, wos[i], wss[i], j, mp)
            if init:
                y = y + inits[i][j].astype(F32)
            outs[i][j] = y.astype(outs[i].dtype)


def final_kernel(ids, own, left, right, own_x, left_x, right_x, dsum, dsum_x, out):
    kh = own.shape[1]
    c = ids[0]
    near = pl.ds(pl.multiple_of(c * kh, kh), kh)
    far = pl.ds(pl.multiple_of((1 - c) * kh, kh), kh)
    inv, inv_x = 1.0 / (1.0 + dsum[...]), 1.0 / (1.0 + dsum_x[...])
    for j in range(own.shape[0]):
        out[j, near, :] = (own[j] + left[j].astype(F32) + right[j].astype(F32)) * inv
        out[j, far, :] = (own_x[j].astype(F32) + left_x[j].astype(F32) + right_x[j].astype(F32)) * inv_x


def _call(kernel, ids, operands, w_at, w, outs, scratch=(), cost=1_000_000, aliases=None):
    wo, ws = w
    mp = None
    specs = []
    full = lambda a: pl.BlockSpec(a.shape, lambda g, s, nd=a.ndim: (0,) * nd)
    args = []
    for a in operands[:w_at[0]]:
        specs.append(full(a))
        args.append(a)
    count = w_at[1]
    if count:
        mp = w_at[2]
        for arr in (wo, ws):
            for i in range(count):
                specs.append(pl.BlockSpec((mp,) + arr.shape[1:], lambda g, s, i=i: (s[i], 0, 0)))
                args.append(arr)
    for a in operands[w_at[0] :]:
        specs.append(full(a))
        args.append(a)
    nbytes = sum(math.prod(o.shape) * o.dtype.itemsize for o in outs)
    return pl.pallas_call(
        kernel,
        out_shape=outs,
        grid_spec=pltpu.PrefetchScalarGridSpec(
            num_scalar_prefetch=1,
            grid=(1,),
            in_specs=specs,
            out_specs=[pl.BlockSpec(o.shape, lambda g, s, nd=len(o.shape): (0,) * nd) for o in outs],
            scratch_shapes=scratch,
        ),
        compiler_params=pltpu.CompilerParams(vmem_limit_bytes=VMEM_LIMIT),
        cost_estimate=pl.CostEstimate(flops=cost, bytes_accessed=2 * nbytes, transcendentals=0),
    )(ids, *args)


def ctf_table(defocus, radial):
    radius = (jnp.arange(radial, dtype=F32) + 1.0) / radial
    phase = 20.0 * defocus[:, None] * radius[None, :] ** 2
    return -(0.995 * jnp.sin(phase) + 0.1 * jnp.cos(phase))


def shards(ring, particles, refs, ctf_group, defocus, class_prior, cycle_weight):
    chips = len(ring)
    opposite = chips // 2
    nl, _, q = particles.shape
    mp, k, _ = refs.shape
    kh = k // 2
    n2 = 2 * nl
    me = lax.axis_index("dp")
    c = lax.rem(me, 2)
    chip_at = np.zeros((2 * chips, chips), np.int32)
    for at, chip in enumerate(ring):
        for core in (0, 1):
            chip_at[2 * chip + core] = [ring[(at + s) % chips] for s in range(chips)]
    at_distance = lax.dynamic_index_in_dim(jnp.asarray(chip_at), me, 0, keepdims=False)

    def dev(s, cross):
        return 2 * at_distance[s % chips] + (c ^ cross)

    def ids_of(pairs):
        return jnp.stack([dev(s, x) for s, x in pairs]).astype(jnp.int32)

    swap = [(i, i ^ 1) for i in range(2 * chips)]
    send = lambda a, shift, cross: lax.ppermute(a, "dp", ring_perm(ring, shift, cross))
    core_swap = lambda a: lax.ppermute(a, "dp", swap)

    near = lax.dynamic_slice_in_dim(refs, c * kh, kh, axis=1)
    far = lax.dynamic_slice_in_dim(refs, (1 - c) * kh, kh, axis=1)
    from_left = [send(near, 1, 0), send(far, 1, 1)]
    from_right = [send(near, -1, 0), send(far, -1, 1)]
    sister = core_swap(far)

    group_x = core_swap(ctf_group)
    ctf = ctf_table(defocus, q // 2)
    gains = cycle_weight[None, :] * ctf
    gain_table = jnp.concatenate([gains, gains], axis=1)
    square_table = jnp.concatenate([gains * ctf, gains * ctf], axis=1)
    groups = jnp.concatenate([ctf_group, group_x])
    index = jnp.arange(defocus.shape[0], dtype=jnp.int32)[None, :]
    onehot = (ctf_group[:, None] == index).astype(F32)
    gain = jnp.dot(onehot, gain_table, precision=HIGHEST)
    onehot_all = (groups[:, None] == index).astype(F32)
    w2 = jnp.dot(onehot_all, square_table, precision=HIGHEST)
    wo = jnp.transpose((particles.astype(F32) * gain[:, None, :]).astype(BF16), (1, 0, 2))
    ws = core_swap(wo)
    w = (wo, ws)
    prior = lax.dynamic_slice_in_dim(class_prior, c * kh, kh, axis=0)[:, None]
    prior = jnp.broadcast_to(prior, (kh, n2))

    shape = jax.ShapeDtypeStruct
    acc_shapes = [shape((19, 2 * kh, n2), F32), shape((kh, q), F32)]
    pieces, where = [near, sister], [(0, 0), (0, 1)]
    acc = None
    for step in range(1, opposite + 1):
        pieces += from_left + from_right
        if step < opposite:
            where += [(-step, 0), (-step, 1), (step, 0), (step, 1)]
        else:
            where += [(step, 0), (step, 1)]
        if step < opposite - 1:
            from_left_next = [send(a, 1, 0) for a in from_left]
            from_right_next = [send(a, -1, 0) for a in from_right]
        elif step == opposite - 1:
            from_left_next = [send(from_left[0], 1, 0)]
            from_right_next = [send(from_right[1], -1, 0)]
        if step == opposite:
            break
        from_left, from_right = from_left_next, from_right_next
        count = len(pieces)
        body = functools.partial(forward_kernel, count, acc is None)
        acc = _call(
            body,
            ids_of(where),
            pieces + ([] if acc is None else list(acc)),
            (count, count, mp),
            w,
            acc_shapes,
            cost=count * mp * 2 * q * n2 * 2 * kh * 4,
        )
        pieces, where = [], []

    count = len(pieces)
    table_f32 = [shape((19, kh, n2), F32), shape((17, kh, n2), F32), shape((2, n2), F32)]
    real, imag, stats = _call(
        functools.partial(score_kernel, count),
        ids_of(where),
        pieces + list(acc) + [w2, prior],
        (count, count, mp),
        w,
        table_f32,
        scratch=[
            pltpu.VMEM((19, 2 * kh, n2), F32),
            pltpu.VMEM((kh, q), F32),
            pltpu.VMEM((ROT, kh, n2), F32),
        ],
        cost=100_000_000,
    )
    stats_x = core_swap(stats)

    piece = shape((mp, kh, q), BF16)
    wide_piece = shape((mp, kh, q), F32)
    table, evidence, dsum, to_right, to_left = _call(
        functools.partial(table_kernel, 2),
        ids_of([(opposite, 0), (opposite, 1)]),
        [real, imag, stats, stats_x, w2],
        (5, 2, mp),
        w,
        [shape((19, 2 * kh, n2), BF16), shape((1, n2), F32), shape((kh, q), F32), piece, piece],
        cost=50_000_000,
    )
    sent_right, sent_left = [to_right], [to_left]
    here = None
    for step in range(1, opposite + 1):
        if step < opposite or opposite == 1:
            pass
        if step == 1:
            got_left = [send(sent_right[0], 1, 0)]
            got_right = [send(sent_left[0], -1, 0)]
        elif step < opposite:
            got_left = [send(a, 1, 0) for a in sent_right]
            got_right = [send(a, -1, 0) for a in sent_left]
        dist = opposite - step
        if dist == 0:
            break
        new_right, new_left = [None, None], [None, None]
        for x in (0, 1):
            spots, inits = [(dist, x), (-dist, x)], [None, None]
            if step == 1:
                if x == 0:
                    inits[0] = got_left[0]
                else:
                    inits[1] = got_right[0]
            else:
                inits = [got_left[x], got_right[x]]
            with_init = [i for i in (0, 1) if inits[i] is not None]
            if len(with_init) == 2:
                res = _call(
                    functools.partial(numer_kernel, 2, True),
                    ids_of(spots),
                    [table] + inits,
                    (1, 2, mp),
                    w,
                    [piece, piece],
                )
            else:
                res = [None, None]
                for i in (0, 1):
                    ini = inits[i] is not None
                    res[i] = _call(
                        functools.partial(numer_kernel, 1, ini),
                        ids_of([spots[i]]),
                        [table] + ([inits[i]] if ini else []),
                        (1, 1, mp),
                        w,
                        [piece],
                    )[0]
            new_right[x], new_left[x] = res
        sent_right, sent_left = new_right, new_left
    own, own_far = _call(
        functools.partial(numer_kernel, 2, False),
        ids_of([(0, 0), (0, 1)]),
        [table],
        (1, 2, mp),
        w,
        [wide_piece, piece],
    )
    own_x = core_swap(own_far)
    left, left_x = send(sent_right[0], 1, 0), send(sent_right[1], 1, 1)
    right, right_x = send(sent_left[0], -1, 0), send(sent_left[1], -1, 1)

    if chips & (chips - 1) == 0:
        bit = 2
        while bit < 2 * chips:
            dsum = dsum + lax.ppermute(dsum, "dp", [(i, i ^ bit) for i in range(2 * chips)])
            bit *= 2
    else:
        halves = [[2 * i + core for i in range(chips)] for core in (0, 1)]
        dsum = lax.psum(dsum, "dp", axis_index_groups=halves)
    dsum_x = core_swap(dsum)

    new_refs = _call(
        final_kernel,
        c[None].astype(jnp.int32),
        [own, left, right, own_x, left_x, right_x, dsum, dsum_x],
        (8, 0, mp),
        w,
        [shape((mp, k, q), F32)],
    )[0]
    return new_refs, evidence[0, :nl]


def solution(mesh):
    in_specs = (
        P(("groups", "dp"), None, None),
        P("dp", "groups", None),
        P(("groups", "dp")),
        P("groups"),
        P("groups"),
        P(),
    )
    out_specs = (P("dp", "groups", None), P(("groups", "dp")))
    body = functools.partial(shards, chip_ring(mesh))
    return jax.shard_map(body, mesh=mesh, in_specs=in_specs, out_specs=out_specs, check_vma=False)
```

time: 216 us -> 94.2 us (0.44)
  waiting for transfers between devices: 88.4 us -> 12.6 us
  blocking collectives: 61.1 us -> 0 us
  starting transfers between devices: 0.08 us -> 37.9 us
  matrix products: 34.5 us -> 1.1 us
  Pallas kernels: 0 us -> 28.8 us
  other arithmetic: 16.6 us -> 5.15 us
  between operations: 14.2 us -> 5.91 us
    psum x1 -> x0, blocking collectives: 61.1 us -> none  [shards(): mass = lax.psum(local_mass, 'dp')]
    all_gather x1 -> x0, waiting for transfers between devices: 46.8 us -> none  [shards(): all_refs = lax.all_gather(refs, 'dp', axis=0, tiled=True)]
    reduce_scatter x1 -> x0, waiting for transfers between devices: 40.8 us -> none  [shards(): lax.psum_scatter(term - jnp.einsum('mnk,nmq->mkq', post_imag, part_turned...]
    ppermute x0 -> x37, starting transfers between devices: none -> 37.9 us  [the longest x28 31.1 us: shards(): lax.ppermute(a, 'dp', ring_perm(ring, shift, cross))]
    dot_general x13 -> x2, matrix products: 34.5 us -> 1.1 us  [the longest x1 0.87 us: shards(): gain = jnp.dot(onehot, gain_table, precision=HIGHEST)]
    pallas_call x0 -> x15, Pallas kernels: none -> 28.8 us  [_call(): pl.pallas_call(kernel, out_shape=outs, grid_spec=pltpu.PrefetchScalarGrid...]
    ppermute x0 -> x37, waiting for transfers between devices: none -> 12.6 us  [the longest x28 8.42 us: shards(): lax.ppermute(a, 'dp', ring_perm(ring, shift, cross))]
    convert_element_type x2 -> x0, other arithmetic: 6.18 us -> none  [the longest x1 3.23 us: shards(): wide_refs = all_refs.astype(jnp.float32)]
  transfers between devices with their start and end apart: 2 -> 37, of which waited for: 2 -> 6; matrix products, arithmetic and copies ran while one was open for 5% -> 3% of each run, Pallas kernels for 0% -> 24%
where the time goes in v1:
time: 94.2 us; the launch traced here: 93.7 us
  starting transfers between devices  37.9 us (40%)
  Pallas kernels  28.8 us (31%)
  waiting for transfers between devices  12.6 us (13%)
  between operations  5.91 us (6%)
  other arithmetic  5.15 us (5%)
  local copies, waits for them, and re-layouts  2.16 us (2%)
  matrix products  1.1 us (1%)
    ppermute x28, starting transfers between devices, shards(): lax.ppermute(a, 'dp', ring_perm(ring, shift, cross))  31.1 us
    pallas_call x15, Pallas kernels, _call(): pl.pallas_call(kernel, out_shape=outs, grid_spec=pltpu.PrefetchScalarGrid...  28.8 us
    ppermute x28, waiting for transfers between devices, shards(): lax.ppermute(a, 'dp', ring_perm(ring, shift, cross))  8.42 us
    ppermute x3, starting transfers between devices, shards(): lax.ppermute(dsum, 'dp', [(i, i ^ bit) for i in range(2 * chips)])  5.04 us
    ppermute x3, waiting for transfers between devices, shards(): lax.ppermute(dsum, 'dp', [(i, i ^ bit) for i in range(2 * chips)])  3.07 us
    transpose x1, other arithmetic, shards(): jnp.transpose((particles.astype(F32) * gain[:, None, :]).astype(BF16), (1...  2.98 us
  transfers between devices with their start and end apart: 37, of which 6 were waited for; matrix products, arithmetic and copies ran while one was open for 3% of the time, Pallas kernels for 24%

profile of v1, /device:TPU:0, one launch (start us, length us, event | category | flops | bytes accessed | tf_op | source)
XLA Modules:
  0.0 93.7 jit_solution(3655646351406386459)
XLA Ops:
  3.0 3.0 %fusion.refs_6_.refs_7_.refs_8_.refs_9_.refs_10_.refs_11_.refs_4_.refs_5_.refs_2_.refs_3_.refs_0_.refs_1_ = bf16[128,64,128]{2,1,0:T(8,128)(2,1)S(1)} fusion(bf16[64,128,128]{2,1,0:T(8,128)(2,1)} %param.7, f32[64,128]{1,0:T(8,128)S(1)} %fusion.3), kind=kLoop, calls=%fused_computation.1 | loop fusion | flops 3145728 | bytes 4227072 | tf_op jit(solution)/shard_map/transpose | solution.py:349
  6.5 2.6 %collective-permute-start = (bf16[8,64,128]{2,1,0:T(8,128)(2,1)S(1)}, bf16[8,64,128]{2,1,0:T(8,128)(2,1)S(1)}, u32[]{:S(2)}, u32[]{:S(2)}) collective-permute-start(bf16[8,64,128]{2,1,0:T(8,128)(2,1)S(1)} %get-tuple-element.51.refs_0_), channel_id=1, source_target_pairs={{2,6},{3,7},{6,10},{7,11},{10,14},{11,15},{14,12},{15,13},{12,8},{... | collective-permute-start | bytes 393224 | tf_op jit(solution)/shard_map/ppermute | solution.py:329
  11.8 1.6 %collective-permute-start.4 = (bf16[8,64,128]{2,1,0:T(8,128)(2,1)S(1)}, bf16[8,64,128]{2,1,0:T(8,128)(2,1)S(1)}, u32[]{:S(2)}, u32[]{:S(2)}) collective-permute-start(bf16[8,64,128]{2,1,0:T(8,128)(2,1)S(1)} %get-tuple-element.50), channel_id=1, source_target_pairs={{2,1},{3,0},{6,3},{7,2},{10,7},{11,6},{14,11},{15,10},{12,15},{13,... | collective-permute-start | bytes 393224 | tf_op jit(solution)/shard_map/ppermute | solution.py:329
  17.0 1.6 %collective-permute-start.1 = (bf16[8,64,128]{2,1,0:T(8,128)(2,1)S(1)}, bf16[8,64,128]{2,1,0:T(8,128)(2,1)S(1)}, u32[]{:S(2)}, u32[]{:S(2)}) collective-permute-start(bf16[8,64,128]{2,1,0:T(8,128)(2,1)S(1)} %collective-permute-done.refs_2_), channel_id=1, source_target_pairs={{2,6},{3,7},{6,10},{7,11},{10,14},{11,15},{14,12},{15,13},{12,8},{... | collective-permute-start | bytes 393224 | tf_op jit(solution)/shard_map/ppermute | solution.py:329
  18.6 2.1 %collective-permute-start.10 = (bf16[8,64,128]{2,1,0:T(8,128)(2,1)S(1)}, bf16[8,64,128]{2,1,0:T(8,128)(2,1)S(1)}, u32[]{:S(2)}, u32[]{:S(2)}) collective-permute-start(bf16[8,64,128]{2,1,0:T(8,128)(2,1)S(1)} %collective-permute-done.9.refs_3_), channel_id=1, source_target_pairs={{2,6},{3,7},{6,10},{7,11},{10,14},{11,15},{14,12},{15,13},{12,8},{... | collective-permute-start | bytes 393224 | tf_op jit(solution)/shard_map/ppermute | solution.py:329
  20.7 1.8 %collective-permute-start.5 = (bf16[8,64,128]{2,1,0:T(8,128)(2,1)S(1)}, bf16[8,64,128]{2,1,0:T(8,128)(2,1)S(1)}, u32[]{:S(2)}, u32[]{:S(2)}) collective-permute-start(bf16[8,64,128]{2,1,0:T(8,128)(2,1)S(1)} %collective-permute-done.4.refs_5_), channel_id=1, source_target_pairs={{2,0},{3,1},{6,2},{7,3},{10,6},{11,7},{14,10},{15,11},{12,14},{13,... | collective-permute-start | bytes 393224 | tf_op jit(solution)/shard_map/ppermute | solution.py:329
  26.1 1.6 %collective-permute-start.11 = (bf16[8,64,128]{2,1,0:T(8,128)(2,1)S(1)}, bf16[8,64,128]{2,1,0:T(8,128)(2,1)S(1)}, u32[]{:S(2)}, u32[]{:S(2)}) collective-permute-start(bf16[8,64,128]{2,1,0:T(8,128)(2,1)S(1)} %collective-permute-done.10.refs_1_), channel_id=1, source_target_pairs={{2,6},{3,7},{6,10},{7,11},{10,14},{11,15},{14,12},{15,13},{12,8},{... | collective-permute-start | bytes 393224 | tf_op jit(solution)/shard_map/ppermute | solution.py:329
  28.1 1.6 %collective-permute-start.2 = (bf16[8,64,128]{2,1,0:T(8,128)(2,1)S(1)}, bf16[8,64,128]{2,1,0:T(8,128)(2,1)S(1)}, u32[]{:S(2)}, u32[]{:S(2)}) collective-permute-start(bf16[8,64,128]{2,1,0:T(8,128)(2,1)S(1)} %collective-permute-done.1.refs_0_), channel_id=1, source_target_pairs={{2,6},{3,7},{6,10},{7,11},{10,14},{11,15},{14,12},{15,13},{12,8},{... | collective-permute-start | bytes 393224 | tf_op jit(solution)/shard_map/ppermute | solution.py:329
  30.4 3.9 %collective-permute-done.2.refs_0_ = bf16[8,64,128]{2,1,0:T(8,128)(2,1)S(1)} collective-permute-done((bf16[8,64,128]{2,1,0:T(8,128)(2,1)S(1)}, bf16[8,64,128]{2,1,0:T(8,128)(2,1)S(1)}, u32[]{:S(2)}, u32[]{:S(2)}) %collective-permute-start.2) | collective-permute-done | bytes 131104 | tf_op jit(solution)/shard_map/ppermute | solution.py:329
  34.2 1.6 %collective-permute-start.3 = (bf16[8,64,128]{2,1,0:T(8,128)(2,1)S(1)}, bf16[8,64,128]{2,1,0:T(8,128)(2,1)S(1)}, u32[]{:S(2)}, u32[]{:S(2)}) collective-permute-start(bf16[8,64,128]{2,1,0:T(8,128)(2,1)S(1)} %collective-permute-done.2.refs_0_), channel_id=1, source_target_pairs={{2,6},{3,7},{6,10},{7,11},{10,14},{11,15},{14,12},{15,13},{12,8},{... | collective-permute-start | bytes 393224 | tf_op jit(solution)/shard_map/ppermute | solution.py:329
  36.3 3.0 %shard_map.86 = (f32[19,128,128]{2,1,0:T(8,128)S(1)}, f32[64,128]{1,0:T(8,128)S(1)}) custom-call(s32[6]{0:T(128)S(1)} %stack.112.ids, bf16[8,64,128]{2,1,0:T(8,128)(2,1)S(1)} %get-tuple-element.51.refs_0_, bf16[8,64,128]{2,1,0:T(8,128)(2,1)S(1)} %collective-permute-done.15.refs_1_, bf16[8,64,128]{2,1,0:T(8,128)(2,1)S(1)} %collective-permute-done.refs_2_, ...), custom_call_target="tpu_custom_call" | custom-call | flops 805306368 | bytes 2555904 | tf_op jit(solution)/shard_map/pallas_call | solution.py:286
  39.3 2.6 %shard_map.87 = (f32[19,128,128]{2,1,0:T(8,128)S(1)}, f32[64,128]{1,0:T(8,128)S(1)}) custom-call(s32[4]{0:T(128)S(1)} %pad_add_fusion.3.ids, bf16[8,64,128]{2,1,0:T(8,128)(2,1)S(1)} %collective-permute-done.1.refs_0_, bf16[8,64,128]{2,1,0:T(8,128)(2,1)S(1)} %collective-permute-done.10.refs_1_, bf16[8,64,128]{2,1,0:T(8,128)(2,1)S(1)} %collective-permute-done.13.refs_2_, ...), custom_call_target="tpu_custom_call" | custom-call | flops 536870912 | bytes 2555904 | tf_op jit(solution)/shard_map/pallas_call | solution.py:286
  41.9 2.6 %shard_map.88 = (f32[19,128,128]{2,1,0:T(8,128)S(1)}, f32[64,128]{1,0:T(8,128)S(1)}) custom-call(s32[4]{0:T(128)S(1)} %pad_add_fusion.2.ids, bf16[8,64,128]{2,1,0:T(8,128)(2,1)S(1)} %collective-permute-done.2.refs_0_, bf16[8,64,128]{2,1,0:T(8,128)(2,1)S(1)} %collective-permute-done.11.refs_1_, bf16[8,64,128]{2,1,0:T(8,128)(2,1)S(1)} %collective-permute-done.14.refs_2_, ...), custom_call_target="tpu_custom_call" | custom-call | flops 536870912 | bytes 2555904 | tf_op jit(solution)/shard_map/pallas_call | solution.py:286
  44.6 3.4 %shard_map.89 = (f32[19,64,128]{2,1,0:T(8,128)S(1)}, f32[17,64,128]{2,1,0:T(8,128)S(1)}, f32[2,128]{1,0:T(2,128)S(1)}) custom-call(s32[2]{0:T(128)S(1)} %pad_add_fusion.1.ids, bf16[8,64,128]{2,1,0:T(8,128)(2,1)S(1)} %collective-permute-done.3.refs_0_, bf16[8,64,128]{2,1,0:T(8,128)(2,1)S(1)} %collective-permute-done.7.refs_1_, ...), custom_call_target="tpu_custom_call" | custom-call | flops 100000000 | bytes 2361344 | tf_op jit(solution)/shard_map/pallas_call | solution.py:286
  49.2 2.1 %shard_map.90 = (bf16[19,128,128]{2,1,0:T(8,128)(2,1)S(1)}, f32[1,128]{1,0:T(1,128)S(1)}, f32[64,128]{1,0:T(8,128)S(1)}, bf16[8,64,128]{2,1,0:T(8,128)(2,1)S(1)}, bf16[8,64,128]{2,1,0:T(8,128)(2,1)S(1)}) custom-call(s32[2]{0:T(128)S(1)} %pad_add_fusion.1.ids, f32[19,64,128]{2,1,0:T(8,128)S(1)} %get-tuple-element.32.real, ...), custom_call_target="tpu_custom_call" | custom-call | flops 50000000 | bytes 1836032 | tf_op jit(solution)/shard_map/pallas_call | solution.py:286
  51.7 1.7 %collective-permute-start.18 = (bf16[8,64,128]{2,1,0:T(8,128)(2,1)S(1)}, bf16[8,64,128]{2,1,0:T(8,128)(2,1)S(1)}, u32[]{:S(2)}, u32[]{:S(2)}) collective-permute-start(bf16[8,64,128]{2,1,0:T(8,128)(2,1)S(1)} %get-tuple-element.37), channel_id=1, source_target_pairs={{2,6},{3,7},{6,10},{7,11},{10,14},{11,15},{14,12},{15,13},{12,8},{... | collective-permute-start | bytes 393224 | tf_op jit(solution)/shard_map/ppermute | solution.py:329
  53.4 1.6 %collective-permute-start.33 = (f32[64,128]{1,0:T(8,128)S(1)}, f32[64,128]{1,0:T(8,128)S(1)}, u32[]{:S(2)}, u32[]{:S(2)}) collective-permute-start(f32[64,128]{1,0:T(8,128)S(1)} %get-tuple-element.48), channel_id=1, source_target_pairs={{0,2},{1,3},{2,0},{3,1},{4,6},{5,7},{6,4},{7,5},{8,10},{9,11},{10,... | collective-permute-start | bytes 98312 | tf_op jit(solution)/shard_map/ppermute | solution.py:479
  57.9 1.6 %collective-permute-start.20 = (bf16[8,64,128]{2,1,0:T(8,128)(2,1)S(1)}, bf16[8,64,128]{2,1,0:T(8,128)(2,1)S(1)}, u32[]{:S(2)}, u32[]{:S(2)}) collective-permute-start(bf16[8,64,128]{2,1,0:T(8,128)(2,1)S(1)} %shard_map.93), channel_id=1, source_target_pairs={{2,0},{3,1},{6,2},{7,3},{10,6},{11,7},{14,10},{15,11},{12,14},{13,... | collective-permute-start | bytes 393224 | tf_op jit(solution)/shard_map/ppermute | solution.py:329
  60.8 1.6 %collective-permute-start.28 = (bf16[8,64,128]{2,1,0:T(8,128)(2,1)S(1)}, bf16[8,64,128]{2,1,0:T(8,128)(2,1)S(1)}, u32[]{:S(2)}, u32[]{:S(2)}) collective-permute-start(bf16[8,64,128]{2,1,0:T(8,128)(2,1)S(1)} %shard_map.97), channel_id=1, source_target_pairs={{2,0},{3,1},{6,2},{7,3},{10,6},{11,7},{14,10},{15,11},{12,14},{13,... | collective-permute-start | bytes 393224 | tf_op jit(solution)/shard_map/ppermute | solution.py:329
  64.2 1.6 %collective-permute-start.34 = (f32[64,128]{1,0:T(8,128)S(1)}, f32[64,128]{1,0:T(8,128)S(1)}, u32[]{:S(2)}, u32[]{:S(2)}) collective-permute-start(f32[64,128]{1,0:T(8,128)S(1)} %add.119), channel_id=1, source_target_pairs={{0,4},{1,5},{2,6},{3,7},{4,0},{5,1},{6,2},{7,3},{8,12},{9,13},{10,... | collective-permute-start | bytes 98312 | tf_op jit(solution)/shard_map/ppermute | solution.py:479
  65.9 3.1 %collective-permute-done.34 = f32[64,128]{1,0:T(8,128)S(1)} collective-permute-done((f32[64,128]{1,0:T(8,128)S(1)}, f32[64,128]{1,0:T(8,128)S(1)}, u32[]{:S(2)}, u32[]{:S(2)}) %collective-permute-start.34) | collective-permute-done | bytes 32800 | tf_op jit(solution)/shard_map/ppermute | solution.py:479
  69.0 1.8 %collective-permute-start.35 = (f32[64,128]{1,0:T(8,128)S(1)}, f32[64,128]{1,0:T(8,128)S(1)}, u32[]{:S(2)}, u32[]{:S(2)}) collective-permute-start(f32[64,128]{1,0:T(8,128)S(1)} %add.120), channel_id=1, source_target_pairs={{0,8},{1,9},{2,10},{3,11},{4,12},{5,13},{6,14},{7,15},{8,0},{9,1},... | collective-permute-start | bytes 98312 | tf_op jit(solution)/shard_map/ppermute | solution.py:479
  70.8 1.9 %shard_map.98 = (bf16[8,64,128]{2,1,0:T(8,128)(2,1)S(1)}, bf16[8,64,128]{2,1,0:T(8,128)(2,1)S(1)}) custom-call(s32[2]{0:T(128)S(1)} %pad_add_fusion.8.ids, bf16[19,128,128]{2,1,0:T(8,128)(2,1)S(1)} %get-tuple-element.35.table, bf16[128,64,128]{2,1,0:T(8,128)(2,1)S(1)} %fusion.refs_6_.refs_7_.refs_8_.refs_9_.refs_10_.refs_11_.refs_4_.refs_5_.refs_2_.refs_3_.refs_0_.refs_1_, ...), custom_call_target="tpu_custom_call" | custom-call | flops 1000000 | bytes 524288 | tf_op jit(solution)/shard_map/pallas_call | solution.py:286
  72.8 2.0 %collective-permute-start.30 = (bf16[8,64,128]{2,1,0:T(8,128)(2,1)S(1)}, bf16[8,64,128]{2,1,0:T(8,128)(2,1)S(1)}, u32[]{:S(2)}, u32[]{:S(2)}) collective-permute-start(bf16[8,64,128]{2,1,0:T(8,128)(2,1)S(1)} %get-tuple-element.45), channel_id=1, source_target_pairs={{2,0},{3,1},{6,2},{7,3},{10,6},{11,7},{14,10},{15,11},{12,14},{13,... | collective-permute-start | bytes 393224 | tf_op jit(solution)/shard_map/ppermute | solution.py:329
  74.8 1.9 %shard_map.94 = (bf16[8,64,128]{2,1,0:T(8,128)(2,1)S(1)}, bf16[8,64,128]{2,1,0:T(8,128)(2,1)S(1)}) custom-call(s32[2]{0:T(128)S(1)} %pad_add_fusion.6.ids, bf16[19,128,128]{2,1,0:T(8,128)(2,1)S(1)} %get-tuple-element.35.table, bf16[128,64,128]{2,1,0:T(8,128)(2,1)S(1)} %fusion.refs_6_.refs_7_.refs_8_.refs_9_.refs_10_.refs_11_.refs_4_.refs_5_.refs_2_.refs_3_.refs_0_.refs_1_, ...), custom_call_target="tpu_custom_call" | custom-call | flops 1000000 | bytes 524288 | tf_op jit(solution)/shard_map/pallas_call | solution.py:286
  76.8 2.0 %collective-permute-start.22 = (bf16[8,64,128]{2,1,0:T(8,128)(2,1)S(1)}, bf16[8,64,128]{2,1,0:T(8,128)(2,1)S(1)}, u32[]{:S(2)}, u32[]{:S(2)}) collective-permute-start(bf16[8,64,128]{2,1,0:T(8,128)(2,1)S(1)} %get-tuple-element.39), channel_id=1, source_target_pairs={{2,0},{3,1},{6,2},{7,3},{10,6},{11,7},{14,10},{15,11},{12,14},{13,... | collective-permute-start | bytes 393224 | tf_op jit(solution)/shard_map/ppermute | solution.py:329
  79.0 1.9 %shard_map.91 = (f32[8,64,128]{2,1,0:T(8,128)S(1)}, bf16[8,64,128]{2,1,0:T(8,128)(2,1)S(1)}) custom-call(s32[2]{0:T(128)S(1)} %pad_add_fusion.ids, bf16[19,128,128]{2,1,0:T(8,128)(2,1)S(1)} %get-tuple-element.35.table, bf16[128,64,128]{2,1,0:T(8,128)(2,1)S(1)} %fusion.refs_6_.refs_7_.refs_8_.refs_9_.refs_10_.refs_11_.refs_4_.refs_5_.refs_2_.refs_3_.refs_0_.refs_1_, ...), custom_call_target="tpu_custom_call" | custom-call | flops 1000000 | bytes 786432 | tf_op jit(solution)/shard_map/pallas_call | solution.py:286
  81.5 1.9 %shard_map.99 = (bf16[8,64,128]{2,1,0:T(8,128)(2,1)S(1)}, bf16[8,64,128]{2,1,0:T(8,128)(2,1)S(1)}) custom-call(s32[2]{0:T(128)S(1)} %pad_add_fusion.7.ids, bf16[19,128,128]{2,1,0:T(8,128)(2,1)S(1)} %get-tuple-element.35.table, bf16[128,64,128]{2,1,0:T(8,128)(2,1)S(1)} %fusion.refs_6_.refs_7_.refs_8_.refs_9_.refs_10_.refs_11_.refs_4_.refs_5_.refs_2_.refs_3_.refs_0_.refs_1_, ...), custom_call_target="tpu_custom_call" | custom-call | flops 1000000 | bytes 524288 | tf_op jit(solution)/shard_map/pallas_call | solution.py:286
  83.5 1.7 %collective-permute-start.32 = (bf16[8,64,128]{2,1,0:T(8,128)(2,1)S(1)}, bf16[8,64,128]{2,1,0:T(8,128)(2,1)S(1)}, u32[]{:S(2)}, u32[]{:S(2)}) collective-permute-start(bf16[8,64,128]{2,1,0:T(8,128)(2,1)S(1)} %get-tuple-element.47), channel_id=1, source_target_pairs={{2,1},{3,0},{6,3},{7,2},{10,7},{11,6},{14,11},{15,10},{12,15},{13,... | collective-permute-start | bytes 393224 | tf_op jit(solution)/shard_map/ppermute | solution.py:329
  85.2 1.9 %shard_map.95 = (bf16[8,64,128]{2,1,0:T(8,128)(2,1)S(1)}, bf16[8,64,128]{2,1,0:T(8,128)(2,1)S(1)}) custom-call(s32[2]{0:T(128)S(1)} %pad_add_fusion.5.ids, bf16[19,128,128]{2,1,0:T(8,128)(2,1)S(1)} %get-tuple-element.35.table, bf16[128,64,128]{2,1,0:T(8,128)(2,1)S(1)} %fusion.refs_6_.refs_7_.refs_8_.refs_9_.refs_10_.refs_11_.refs_4_.refs_5_.refs_2_.refs_3_.refs_0_.refs_1_, ...), custom_call_target="tpu_custom_call" | custom-call | flops 1000000 | bytes 524288 | tf_op jit(solution)/shard_map/pallas_call | solution.py:286
  87.2 2.0 %collective-permute-start.24 = (bf16[8,64,128]{2,1,0:T(8,128)(2,1)S(1)}, bf16[8,64,128]{2,1,0:T(8,128)(2,1)S(1)}, u32[]{:S(2)}, u32[]{:S(2)}) collective-permute-start(bf16[8,64,128]{2,1,0:T(8,128)(2,1)S(1)} %get-tuple-element.41), channel_id=1, source_target_pairs={{2,0},{3,1},{6,2},{7,3},{10,6},{11,7},{14,10},{15,11},{12,14},{13,... | collective-permute-start | bytes 393224 | tf_op jit(solution)/shard_map/ppermute | solution.py:329
  89.7 2.9 %collective-permute-done.23.left = bf16[8,64,128]{2,1,0:T(8,128)(2,1)S(1)} collective-permute-done((bf16[8,64,128]{2,1,0:T(8,128)(2,1)S(1)}, bf16[8,64,128]{2,1,0:T(8,128)(2,1)S(1)}, u32[]{:S(2)}, u32[]{:S(2)}) %collective-permute-start.23) | collective-permute-done | bytes 131104 | tf_op jit(solution)/shard_map/ppermute | solution.py:329
  (88 shorter events, 19.8 us)
Async XLA Ops:
  6.0 30.3 %collective-permute-start.8 = (bf16[128,64,128]{2,1,0:T(8,128)(2,1)S(1)}, bf16[128,64,128]{2,1,0:T(8,128)(2,1)}, u32[]{:S(2)}, u32[]{:S(2)}) collective-permute-start(bf16[128,64,128]{2,1,0:T(8,128)(2,1)S(1)} %fusion.refs_6_.refs_7_.refs_8_.refs_9_.refs_10_.refs_11_.refs_4_.refs_5_.refs_2_.refs_3_.refs_0_.refs_1_), channel_id=1, source_target_pairs={{0,1},{1,0},{2,3},{3,2},{4,5},{5,4},{6,7},{7,6},{8,9},{9,8},{10,11... | collective-permute-start | bytes 6291464 | tf_op jit(solution)/shard_map/ppermute | solution.py:330
  6.5 6.8 %collective-permute-start = (bf16[8,64,128]{2,1,0:T(8,128)(2,1)S(1)}, bf16[8,64,128]{2,1,0:T(8,128)(2,1)S(1)}, u32[]{:S(2)}, u32[]{:S(2)}) collective-permute-start(bf16[8,64,128]{2,1,0:T(8,128)(2,1)S(1)} %get-tuple-element.51.refs_0_), channel_id=1, source_target_pairs={{2,6},{3,7},{6,10},{7,11},{10,14},{11,15},{14,12},{15,13},{12,8},{... | collective-permute-start | bytes 393224 | tf_op jit(solution)/shard_map/ppermute | solution.py:329
  9.1 7.9 %collective-permute-start.12 = (bf16[8,64,128]{2,1,0:T(8,128)(2,1)S(1)}, bf16[8,64,128]{2,1,0:T(8,128)(2,1)S(1)}, u32[]{:S(2)}, u32[]{:S(2)}) collective-permute-start(bf16[8,64,128]{2,1,0:T(8,128)(2,1)S(1)} %get-tuple-element.51.refs_0_), channel_id=1, source_target_pairs={{2,0},{3,1},{6,2},{7,3},{10,6},{11,7},{14,10},{15,11},{12,14},{13,... | collective-permute-start | bytes 393224 | tf_op jit(solution)/shard_map/ppermute | solution.py:329
  9.5 11.2 %collective-permute-start.15 = (bf16[8,64,128]{2,1,0:T(8,128)(2,1)S(1)}, bf16[8,64,128]{2,1,0:T(8,128)(2,1)S(1)}, u32[]{:S(2)}, u32[]{:S(2)}) collective-permute-start(bf16[8,64,128]{2,1,0:T(8,128)(2,1)S(1)} %get-tuple-element.50), channel_id=1, source_target_pairs={{0,1},{1,0},{2,3},{3,2},{4,5},{5,4},{6,7},{7,6},{8,9},{9,8},{10,11... | collective-permute-start | bytes 393224 | tf_op jit(solution)/shard_map/ppermute | solution.py:330
  11.8 8.9 %collective-permute-start.4 = (bf16[8,64,128]{2,1,0:T(8,128)(2,1)S(1)}, bf16[8,64,128]{2,1,0:T(8,128)(2,1)S(1)}, u32[]{:S(2)}, u32[]{:S(2)}) collective-permute-start(bf16[8,64,128]{2,1,0:T(8,128)(2,1)S(1)} %get-tuple-element.50), channel_id=1, source_target_pairs={{2,1},{3,0},{6,3},{7,2},{10,7},{11,6},{14,11},{15,10},{12,15},{13,... | collective-permute-start | bytes 393224 | tf_op jit(solution)/shard_map/ppermute | solution.py:329
  17.0 11.1 %collective-permute-start.1 = (bf16[8,64,128]{2,1,0:T(8,128)(2,1)S(1)}, bf16[8,64,128]{2,1,0:T(8,128)(2,1)S(1)}, u32[]{:S(2)}, u32[]{:S(2)}) collective-permute-start(bf16[8,64,128]{2,1,0:T(8,128)(2,1)S(1)} %collective-permute-done.refs_2_), channel_id=1, source_target_pairs={{2,6},{3,7},{6,10},{7,11},{10,14},{11,15},{14,12},{15,13},{12,8},{... | collective-permute-start | bytes 393224 | tf_op jit(solution)/shard_map/ppermute | solution.py:329
  18.6 7.5 %collective-permute-start.10 = (bf16[8,64,128]{2,1,0:T(8,128)(2,1)S(1)}, bf16[8,64,128]{2,1,0:T(8,128)(2,1)S(1)}, u32[]{:S(2)}, u32[]{:S(2)}) collective-permute-start(bf16[8,64,128]{2,1,0:T(8,128)(2,1)S(1)} %collective-permute-done.9.refs_3_), channel_id=1, source_target_pairs={{2,6},{3,7},{6,10},{7,11},{10,14},{11,15},{14,12},{15,13},{12,8},{... | collective-permute-start | bytes 393224 | tf_op jit(solution)/shard_map/ppermute | solution.py:329
  20.7 7.0 %collective-permute-start.13 = (bf16[8,64,128]{2,1,0:T(8,128)(2,1)S(1)}, bf16[8,64,128]{2,1,0:T(8,128)(2,1)S(1)}, u32[]{:S(2)}, u32[]{:S(2)}) collective-permute-start(bf16[8,64,128]{2,1,0:T(8,128)(2,1)S(1)} %collective-permute-done.12.refs_4_), channel_id=1, source_target_pairs={{2,0},{3,1},{6,2},{7,3},{10,6},{11,7},{14,10},{15,11},{12,14},{13,... | collective-permute-start | bytes 393224 | tf_op jit(solution)/shard_map/ppermute | solution.py:329
  20.7 9.0 %collective-permute-start.5 = (bf16[8,64,128]{2,1,0:T(8,128)(2,1)S(1)}, bf16[8,64,128]{2,1,0:T(8,128)(2,1)S(1)}, u32[]{:S(2)}, u32[]{:S(2)}) collective-permute-start(bf16[8,64,128]{2,1,0:T(8,128)(2,1)S(1)} %collective-permute-done.4.refs_5_), channel_id=1, source_target_pairs={{2,0},{3,1},{6,2},{7,3},{10,6},{11,7},{14,10},{15,11},{12,14},{13,... | collective-permute-start | bytes 393224 | tf_op jit(solution)/shard_map/ppermute | solution.py:329
  26.1 15.9 %collective-permute-start.11 = (bf16[8,64,128]{2,1,0:T(8,128)(2,1)S(1)}, bf16[8,64,128]{2,1,0:T(8,128)(2,1)S(1)}, u32[]{:S(2)}, u32[]{:S(2)}) collective-permute-start(bf16[8,64,128]{2,1,0:T(8,128)(2,1)S(1)} %collective-permute-done.10.refs_1_), channel_id=1, source_target_pairs={{2,6},{3,7},{6,10},{7,11},{10,14},{11,15},{14,12},{15,13},{12,8},{... | collective-permute-start | bytes 393224 | tf_op jit(solution)/shard_map/ppermute | solution.py:329
  27.6 14.3 %collective-permute-start.14 = (bf16[8,64,128]{2,1,0:T(8,128)(2,1)S(1)}, bf16[8,64,128]{2,1,0:T(8,128)(2,1)S(1)}, u32[]{:S(2)}, u32[]{:S(2)}) collective-permute-start(bf16[8,64,128]{2,1,0:T(8,128)(2,1)S(1)} %collective-permute-done.13.refs_2_), channel_id=1, source_target_pairs={{2,0},{3,1},{6,2},{7,3},{10,6},{11,7},{14,10},{15,11},{12,14},{13,... | collective-permute-start | bytes 393224 | tf_op jit(solution)/shard_map/ppermute | solution.py:329
  28.1 6.2 %collective-permute-start.2 = (bf16[8,64,128]{2,1,0:T(8,128)(2,1)S(1)}, bf16[8,64,128]{2,1,0:T(8,128)(2,1)S(1)}, u32[]{:S(2)}, u32[]{:S(2)}) collective-permute-start(bf16[8,64,128]{2,1,0:T(8,128)(2,1)S(1)} %collective-permute-done.1.refs_0_), channel_id=1, source_target_pairs={{2,6},{3,7},{6,10},{7,11},{10,14},{11,15},{14,12},{15,13},{12,8},{... | collective-permute-start | bytes 393224 | tf_op jit(solution)/shard_map/ppermute | solution.py:329
  29.7 6.2 %collective-permute-start.6 = (bf16[8,64,128]{2,1,0:T(8,128)(2,1)S(1)}, bf16[8,64,128]{2,1,0:T(8,128)(2,1)S(1)}, u32[]{:S(2)}, u32[]{:S(2)}) collective-permute-start(bf16[8,64,128]{2,1,0:T(8,128)(2,1)S(1)} %collective-permute-done.5.refs_3_), channel_id=1, source_target_pairs={{2,0},{3,1},{6,2},{7,3},{10,6},{11,7},{14,10},{15,11},{12,14},{13,... | collective-permute-start | bytes 393224 | tf_op jit(solution)/shard_map/ppermute | solution.py:329
  34.2 10.3 %collective-permute-start.3 = (bf16[8,64,128]{2,1,0:T(8,128)(2,1)S(1)}, bf16[8,64,128]{2,1,0:T(8,128)(2,1)S(1)}, u32[]{:S(2)}, u32[]{:S(2)}) collective-permute-start(bf16[8,64,128]{2,1,0:T(8,128)(2,1)S(1)} %collective-permute-done.2.refs_0_), channel_id=1, source_target_pairs={{2,6},{3,7},{6,10},{7,11},{10,14},{11,15},{14,12},{15,13},{12,8},{... | collective-permute-start | bytes 393224 | tf_op jit(solution)/shard_map/ppermute | solution.py:329
  35.8 8.7 %collective-permute-start.7 = (bf16[8,64,128]{2,1,0:T(8,128)(2,1)S(1)}, bf16[8,64,128]{2,1,0:T(8,128)(2,1)S(1)}, u32[]{:S(2)}, u32[]{:S(2)}) collective-permute-start(bf16[8,64,128]{2,1,0:T(8,128)(2,1)S(1)} %collective-permute-done.6.refs_3_), channel_id=1, source_target_pairs={{2,0},{3,1},{6,2},{7,3},{10,6},{11,7},{14,10},{15,11},{12,14},{13,... | collective-permute-start | bytes 393224 | tf_op jit(solution)/shard_map/ppermute | solution.py:329
  51.3 8.3 %collective-permute-start.27 = (bf16[8,64,128]{2,1,0:T(8,128)(2,1)S(1)}, bf16[8,64,128]{2,1,0:T(8,128)(2,1)S(1)}, u32[]{:S(2)}, u32[]{:S(2)}) collective-permute-start(bf16[8,64,128]{2,1,0:T(8,128)(2,1)S(1)} %get-tuple-element.43), channel_id=1, source_target_pairs={{2,0},{3,1},{6,2},{7,3},{10,6},{11,7},{14,10},{15,11},{12,14},{13,... | collective-permute-start | bytes 393224 | tf_op jit(solution)/shard_map/ppermute | solution.py:329
  51.7 10.8 %collective-permute-start.18 = (bf16[8,64,128]{2,1,0:T(8,128)(2,1)S(1)}, bf16[8,64,128]{2,1,0:T(8,128)(2,1)S(1)}, u32[]{:S(2)}, u32[]{:S(2)}) collective-permute-start(bf16[8,64,128]{2,1,0:T(8,128)(2,1)S(1)} %get-tuple-element.37), channel_id=1, source_target_pairs={{2,6},{3,7},{6,10},{7,11},{10,14},{11,15},{14,12},{15,13},{12,8},{... | collective-permute-start | bytes 393224 | tf_op jit(solution)/shard_map/ppermute | solution.py:329
  53.4 10.8 %collective-permute-start.33 = (f32[64,128]{1,0:T(8,128)S(1)}, f32[64,128]{1,0:T(8,128)S(1)}, u32[]{:S(2)}, u32[]{:S(2)}) collective-permute-start(f32[64,128]{1,0:T(8,128)S(1)} %get-tuple-element.48), channel_id=1, source_target_pairs={{0,2},{1,3},{2,0},{3,1},{4,6},{5,7},{6,4},{7,5},{8,10},{9,11},{10,... | collective-permute-start | bytes 98312 | tf_op jit(solution)/shard_map/ppermute | solution.py:479
  56.2 14.6 %collective-permute-start.26 = (bf16[8,64,128]{2,1,0:T(8,128)(2,1)S(1)}, bf16[8,64,128]{2,1,0:T(8,128)(2,1)S(1)}, u32[]{:S(2)}, u32[]{:S(2)}) collective-permute-start(bf16[8,64,128]{2,1,0:T(8,128)(2,1)S(1)} %shard_map.96), channel_id=1, source_target_pairs={{2,6},{3,7},{6,10},{7,11},{10,14},{11,15},{14,12},{15,13},{12,8},{... | collective-permute-start | bytes 393224 | tf_op jit(solution)/shard_map/ppermute | solution.py:329
  57.9 16.9 %collective-permute-start.20 = (bf16[8,64,128]{2,1,0:T(8,128)(2,1)S(1)}, bf16[8,64,128]{2,1,0:T(8,128)(2,1)S(1)}, u32[]{:S(2)}, u32[]{:S(2)}) collective-permute-start(bf16[8,64,128]{2,1,0:T(8,128)(2,1)S(1)} %shard_map.93), channel_id=1, source_target_pairs={{2,0},{3,1},{6,2},{7,3},{10,6},{11,7},{14,10},{15,11},{12,14},{13,... | collective-permute-start | bytes 393224 | tf_op jit(solution)/shard_map/ppermute | solution.py:329
  60.8 10.0 %collective-permute-start.28 = (bf16[8,64,128]{2,1,0:T(8,128)(2,1)S(1)}, bf16[8,64,128]{2,1,0:T(8,128)(2,1)S(1)}, u32[]{:S(2)}, u32[]{:S(2)}) collective-permute-start(bf16[8,64,128]{2,1,0:T(8,128)(2,1)S(1)} %shard_map.97), channel_id=1, source_target_pairs={{2,0},{3,1},{6,2},{7,3},{10,6},{11,7},{14,10},{15,11},{12,14},{13,... | collective-permute-start | bytes 393224 | tf_op jit(solution)/shard_map/ppermute | solution.py:329
  63.6 11.2 %collective-permute-start.19 = (bf16[8,64,128]{2,1,0:T(8,128)(2,1)S(1)}, bf16[8,64,128]{2,1,0:T(8,128)(2,1)S(1)}, u32[]{:S(2)}, u32[]{:S(2)}) collective-permute-start(bf16[8,64,128]{2,1,0:T(8,128)(2,1)S(1)} %shard_map.92), channel_id=1, source_target_pairs={{2,6},{3,7},{6,10},{7,11},{10,14},{11,15},{14,12},{15,13},{12,8},{... | collective-permute-start | bytes 393224 | tf_op jit(solution)/shard_map/ppermute | solution.py:329
  69.0 9.8 %collective-permute-start.35 = (f32[64,128]{1,0:T(8,128)S(1)}, f32[64,128]{1,0:T(8,128)S(1)}, u32[]{:S(2)}, u32[]{:S(2)}) collective-permute-start(f32[64,128]{1,0:T(8,128)S(1)} %add.120), channel_id=1, source_target_pairs={{0,8},{1,9},{2,10},{3,11},{4,12},{5,13},{6,14},{7,15},{8,0},{9,1},... | collective-permute-start | bytes 98312 | tf_op jit(solution)/shard_map/ppermute | solution.py:479
  72.7 8.2 %collective-permute-start.29 = (bf16[8,64,128]{2,1,0:T(8,128)(2,1)S(1)}, bf16[8,64,128]{2,1,0:T(8,128)(2,1)S(1)}, u32[]{:S(2)}, u32[]{:S(2)}) collective-permute-start(bf16[8,64,128]{2,1,0:T(8,128)(2,1)S(1)} %get-tuple-element.44), channel_id=1, source_target_pairs={{2,6},{3,7},{6,10},{7,11},{10,14},{11,15},{14,12},{15,13},{12,8},{... | collective-permute-start | bytes 393224 | tf_op jit(solution)/shard_map/ppermute | solution.py:329
  72.8 8.7 %collective-permute-start.30 = (bf16[8,64,128]{2,1,0:T(8,128)(2,1)S(1)}, bf16[8,64,128]{2,1,0:T(8,128)(2,1)S(1)}, u32[]{:S(2)}, u32[]{:S(2)}) collective-permute-start(bf16[8,64,128]{2,1,0:T(8,128)(2,1)S(1)} %get-tuple-element.45), channel_id=1, source_target_pairs={{2,0},{3,1},{6,2},{7,3},{10,6},{11,7},{14,10},{15,11},{12,14},{13,... | collective-permute-start | bytes 393224 | tf_op jit(solution)/shard_map/ppermute | solution.py:329
  76.7 6.7 %collective-permute-start.21 = (bf16[8,64,128]{2,1,0:T(8,128)(2,1)S(1)}, bf16[8,64,128]{2,1,0:T(8,128)(2,1)S(1)}, u32[]{:S(2)}, u32[]{:S(2)}) collective-permute-start(bf16[8,64,128]{2,1,0:T(8,128)(2,1)S(1)} %get-tuple-element.38), channel_id=1, source_target_pairs={{2,6},{3,7},{6,10},{7,11},{10,14},{11,15},{14,12},{15,13},{12,8},{... | collective-permute-start | bytes 393224 | tf_op jit(solution)/shard_map/ppermute | solution.py:329
  76.8 8.4 %collective-permute-start.22 = (bf16[8,64,128]{2,1,0:T(8,128)(2,1)S(1)}, bf16[8,64,128]{2,1,0:T(8,128)(2,1)S(1)}, u32[]{:S(2)}, u32[]{:S(2)}) collective-permute-start(bf16[8,64,128]{2,1,0:T(8,128)(2,1)S(1)} %get-tuple-element.39), channel_id=1, source_target_pairs={{2,0},{3,1},{6,2},{7,3},{10,6},{11,7},{14,10},{15,11},{12,14},{13,... | collective-permute-start | bytes 393224 | tf_op jit(solution)/shard_map/ppermute | solution.py:329
  78.9 8.3 %collective-permute-start.36 = (f32[64,128]{1,0:T(8,128)S(1)}, f32[64,128]{1,0:T(8,128)S(1)}, u32[]{:S(2)}, u32[]{:S(2)}) collective-permute-start(f32[64,128]{1,0:T(8,128)S(1)} %add.121.dsum), channel_id=1, source_target_pairs={{0,1},{1,0},{2,3},{3,2},{4,5},{5,4},{6,7},{7,6},{8,9},{9,8},{10,11... | collective-permute-start | bytes 98312 | tf_op jit(solution)/shard_map/ppermute | solution.py:330
  80.9 8.7 %collective-permute-start.25 = (bf16[8,64,128]{2,1,0:T(8,128)(2,1)S(1)}, bf16[8,64,128]{2,1,0:T(8,128)(2,1)S(1)}, u32[]{:S(2)}, u32[]{:S(2)}) collective-permute-start(bf16[8,64,128]{2,1,0:T(8,128)(2,1)S(1)} %get-tuple-element.42), channel_id=1, source_target_pairs={{0,1},{1,0},{2,3},{3,2},{4,5},{5,4},{6,7},{7,6},{8,9},{9,8},{10,11... | collective-permute-start | bytes 393224 | tf_op jit(solution)/shard_map/ppermute | solution.py:330
  83.4 6.3 %collective-permute-start.31 = (bf16[8,64,128]{2,1,0:T(8,128)(2,1)S(1)}, bf16[8,64,128]{2,1,0:T(8,128)(2,1)S(1)}, u32[]{:S(2)}, u32[]{:S(2)}) collective-permute-start(bf16[8,64,128]{2,1,0:T(8,128)(2,1)S(1)} %get-tuple-element.46), channel_id=1, source_target_pairs={{2,7},{3,6},{6,11},{7,10},{10,15},{11,14},{14,13},{15,12},{12,9},{... | collective-permute-start | bytes 393224 | tf_op jit(solution)/shard_map/ppermute | solution.py:329
  83.5 6.2 %collective-permute-start.32 = (bf16[8,64,128]{2,1,0:T(8,128)(2,1)S(1)}, bf16[8,64,128]{2,1,0:T(8,128)(2,1)S(1)}, u32[]{:S(2)}, u32[]{:S(2)}) collective-permute-start(bf16[8,64,128]{2,1,0:T(8,128)(2,1)S(1)} %get-tuple-element.47), channel_id=1, source_target_pairs={{2,1},{3,0},{6,3},{7,2},{10,7},{11,6},{14,11},{15,10},{12,15},{13,... | collective-permute-start | bytes 393224 | tf_op jit(solution)/shard_map/ppermute | solution.py:329
  87.2 5.6 %collective-permute-start.24 = (bf16[8,64,128]{2,1,0:T(8,128)(2,1)S(1)}, bf16[8,64,128]{2,1,0:T(8,128)(2,1)S(1)}, u32[]{:S(2)}, u32[]{:S(2)}) collective-permute-start(bf16[8,64,128]{2,1,0:T(8,128)(2,1)S(1)} %get-tuple-element.41), channel_id=1, source_target_pairs={{2,0},{3,1},{6,2},{7,3},{10,6},{11,7},{14,10},{15,11},{12,14},{13,... | collective-permute-start | bytes 393224 | tf_op jit(solution)/shard_map/ppermute | solution.py:329
  (8 other events, 50.4 us)

commit v2 on v1

v2 whole, which is shorter than its diff:
```python
import functools
import math

import jax
import jax.numpy as jnp
from jax import lax
from jax.experimental import pallas as pl
from jax.experimental.layout import Layout, with_layout_constraint
from jax.experimental.pallas import tpu as pltpu
from jax.sharding import PartitionSpec as P

ROT = 36
HALF = ROT // 2
HIGHEST = lax.Precision.HIGHEST
F32 = jnp.float32
BF16 = jnp.bfloat16
VMEM_LIMIT = 40 * 1024 * 1024


class Ring:
    def __init__(self, mesh):
        self.chips = mesh.shape["dp"] // 2
        wide = 2
        coords = [getattr(d, "coords", None) for d in mesh.devices.reshape(-1, 2 * self.chips)[0]]
        if all(c is not None for c in coords):
            wide = len({c[0] for c in coords})
        self.wide = wide if self.chips % wide == 0 else 1
        self.deep = self.chips // self.wide

    def chip(self, pos, div=lambda a, b: a // b, pick=lambda c, a, b: a if c else b):
        if self.wide == 1:
            return pos
        row = self.wide - 1
        z = div(pos, row)
        i = pos - z * row
        x = pick(z - 2 * div(z, 2) == 0, 1 + i, row - i)
        back = self.deep - 1 - (pos - self.deep * row)
        return pick(pos < self.deep * row, z * self.wide + x, back * self.wide)

    def pos(self, chip, div=lambda a, b: a // b, pick=lambda c, a, b: a if c else b):
        if self.wide == 1:
            return chip
        row = self.wide - 1
        z = div(chip, self.wide)
        x = chip - z * self.wide
        i = pick(z - 2 * div(z, 2) == 0, x - 1, row - x)
        return pick(x == 0, self.deep * row + self.deep - 1 - z, z * row + i)

    def order(self):
        return [self.chip(p) for p in range(self.chips)]

    def devices(self, spots):
        me = lax.axis_index("dp")
        at = self.pos(lax.div(me, 2), lax.div, jnp.where)
        core = me - 2 * lax.div(me, 2)
        found = []
        for dist, other in spots:
            chip = self.chip(lax.rem(at + dist % self.chips, self.chips), lax.div, jnp.where)
            found.append(2 * chip + (1 - core if other else core))
        return found, core


def ring_perm(ring, shift, cross):
    n = len(ring)
    pairs = []
    for at, chip in enumerate(ring):
        to = ring[(at + shift) % n]
        pairs += [(2 * chip + c, 2 * to + (c ^ cross)) for c in (0, 1)]
    return pairs


def _combine(terms):
    by = {}
    for k, v in terms:
        k %= ROT
        k = min(k, ROT - k)
        sign = 1
        if k > 9:
            k, sign = HALF - k, -1
        if k == 9:
            continue
        by.setdefault(k, []).append((sign, v))
    total = None
    for k, vs in sorted(by.items()):
        part, psign = None, 1
        for sign, v in vs:
            if part is None:
                part, psign = v, sign
            else:
                part = part + v if sign == psign else part - v
        if k:
            part = part * math.cos(k * math.pi / HALF)
        if total is None:
            total = part if psign > 0 else -part
        else:
            total = total + part if psign > 0 else total - part
    return total


def cos_transform(a):
    plus = [a[t] + a[HALF - t] for t in range(9)] + [a[9]]
    minus = [a[t] - a[HALF - t] for t in range(9)]
    out = [None] * 19
    for j in range(10):
        side = plus if j % 2 == 0 else minus
        even = _combine([(t * j, side[t]) for t in range(0, len(side), 2)])
        odd = _combine([(t * j, side[t]) for t in range(1, len(side), 2)])
        if odd is None:
            out[j] = out[HALF - j] = even
        else:
            out[j] = even + odd
            out[HALF - j] = even - odd
    return out


def sin_transform(b):
    plus = {t: b[t] + b[HALF - t] for t in range(1, 9)}
    plus[9] = b[9]
    minus = {t: b[t] - b[HALF - t] for t in range(1, 9)}
    out = [None] * 18
    for j in range(1, 10):
        side = plus if j % 2 else minus
        even = _combine([(9 - t * j, v) for t, v in side.items() if t % 2 == 0])
        odd = _combine([(9 - t * j, v) for t, v in side.items() if t % 2])
        if odd is None:
            odd = jnp.zeros_like(even)
        if even is None:
            even = jnp.zeros_like(odd)
        out[j] = odd + even
        if j != 9:
            out[HALF - j] = odd - even
    return out


def _residue(m):
    r = lax.rem(m, ROT)
    flip = r > HALF
    return jnp.where(flip, ROT - r, r), jnp.where(flip, -1.0, 1.0).astype(F32)


def _half_sign(shape):
    lane = lax.broadcasted_iota(jnp.int32, shape, len(shape) - 1)
    return jnp.where(lane < shape[-1] // 2, -1.0, 1.0).astype(F32)


def _forward(base, mp, piece, row, wo, ws, acc, energy):
    kh, q = piece.shape[1:]
    sign = _half_sign((kh, q))
    first = base * mp
    squares = jnp.zeros((kh, q), F32)
    for j in range(mp):
        m = first + j
        t, s = _residue(m)
        x = piece[row + j]
        wide = x.astype(F32)
        squares = squares + wide * wide
        swapped = (pltpu.roll(wide, q // 2, 1) * sign).astype(BF16)
        both = jnp.concatenate([x, swapped], axis=0)
        w = jnp.concatenate([wo[m], ws[m]], axis=0)
        y = lax.dot_general(both, w, (((1,), (1,)), ((), ())), preferred_element_type=F32)
        acc[t, :kh, :] += y[:kh]
        acc[t, kh:, :] += s * y[kh:]
    energy[...] += squares


def _backward(m, table, wo, ws):
    t, s = _residue(m)
    w = jnp.concatenate([wo[m], ws[m]], axis=0)
    y = jnp.dot(table[t], w, preferred_element_type=F32)
    kh = y.shape[0] // 2
    turned = pltpu.roll(y[kh:], y.shape[1] // 2, 1) * (_half_sign((kh, y.shape[1])) * s)
    return y[:kh] + turned


def forward_kernel(ring, spots, mp, first, wo, ws, *refs):
    acc, energy = refs[-2:]
    if first:
        acc[...] = jnp.zeros_like(acc)
        energy[...] = jnp.zeros_like(energy)
    at, _ = ring.devices([place for _, _, place in spots])
    for base, (operand, row, _) in zip(at, spots):
        _forward(base, mp, refs[operand], row, wo, ws, acc, energy)


def score_kernel(ring, spots, mp, wo, ws, *refs):
    at, _ = ring.devices([place for _, _, place in spots])
    w2, prior, _, _, acc, energy, real_out, imag_out, stats, scores = refs[2:]
    for base, (operand, row, _) in zip(at, spots):
        _forward(base, mp, refs[operand], row, wo, ws, acc, energy)
    kh, n = scores.shape[1:]
    norm = lax.dot_general(
        energy[...], w2[...], (((1,), (1,)), ((), ())), precision=HIGHEST, preferred_element_type=F32
    )
    energy[...] = jnp.log(prior[...]) - 0.5 * norm
    tile = 8

    def scan_scores(i, top):
        at = pl.multiple_of(i * tile, tile)
        rows, rows_imag = pl.ds(at, tile), pl.ds(pl.multiple_of(kh + i * tile, tile), tile)
        p = cos_transform([acc[t, rows, :] for t in range(19)])
        q = sin_transform([None] + [acc[t, rows_imag, :] for t in range(1, HALF)])
        base = energy[rows, :]
        for j in range(19):
            pj = p[j] + base
            if j in (0, HALF):
                scores[j, rows, :] = pj
                top = jnp.maximum(top, pj)
            else:
                lo, hi = pj - q[j], pj + q[j]
                scores[j, rows, :] = lo
                scores[ROT - j, rows, :] = hi
                top = jnp.maximum(top, jnp.maximum(lo, hi))
        return top

    top = lax.fori_loop(0, kh // tile, scan_scores, jnp.full((tile, n), -jnp.inf, F32))
    top = jnp.max(top, axis=0, keepdims=True)

    def scan_exp(i, total):
        rows = pl.ds(pl.multiple_of(i * tile, tile), tile)
        u = [jnp.exp(scores[j, rows, :] - top) for j in range(ROT)]
        plus = [u[0]] + [u[j] + u[ROT - j] for j in range(1, HALF)] + [u[HALF]]
        minus = [None] + [u[j] - u[ROT - j] for j in range(1, HALF)]
        real = cos_transform(plus)
        imag = sin_transform(minus)
        for t in range(19):
            real_out[t, rows, :] = real[t]
        for t in range(1, HALF):
            imag_out[t - 1, rows, :] = imag[t]
        return total + real[0]

    total = lax.fori_loop(0, kh // tile, scan_exp, jnp.zeros((tile, n), F32))
    stats[0:1, :] = top
    stats[1:2, :] = jnp.sum(total, axis=0, keepdims=True)


def table_kernel(ring, spots, mp, wo, ws, real, imag, mine, other, w2, table, evidence, dpart, *outs):
    kh, n = real.shape[1:]
    theirs = pltpu.roll(jnp.broadcast_to(other[...].reshape(2, 1, n), (2, 8, n)).reshape(16, n), n // 2, 1)
    top_a, total_a = mine[0:1, :], mine[1:2, :]
    top_b, total_b = theirs[0:1, :], theirs[8:9, :]
    top = jnp.maximum(top_a, top_b)
    scale = jnp.exp(top_a - top)
    total = total_a * scale + total_b * jnp.exp(top_b - top)
    evidence[...] = top + jnp.log(total)
    scale = scale / total
    for t in range(19):
        table[t, :kh, :] = (real[t] * scale).astype(BF16)
        if 0 < t < HALF:
            table[t, kh:, :] = (imag[t - 1] * scale).astype(BF16)
        else:
            table[t, kh:, :] = jnp.zeros((kh, n), BF16)
    dpart[...] = jnp.dot(real[0] * scale, w2[...], precision=HIGHEST, preferred_element_type=F32)
    at, _ = ring.devices(spots)
    for base, out in zip(at, outs):
        for j in range(mp):
            out[j] = _backward(base * mp + j, table, wo, ws).astype(out.dtype)
        out[mp] = _split(dpart[...])


def numer_kernel(ring, spots, mp, wo, ws, table, *outs):
    at, _ = ring.devices(spots)
    for i, base in enumerate(at):
        for j in range(mp):
            outs[i // 2][i % 2 * mp + j] = _backward(base * mp + j, table, wo, ws)


def _split(x):
    lead = x.astype(BF16)
    rest = (x - lead.astype(F32)).astype(BF16)
    lane = lax.broadcasted_iota(jnp.int32, x.shape, 1)
    return jnp.where(lane < x.shape[1] // 2, lead.astype(F32), rest.astype(F32)).astype(BF16)


def _join(row):
    wide = row.astype(F32)
    return wide + pltpu.roll(wide, row.shape[1] // 2, 1)


def add_kernel(mp, half, part_r, part_l, got_r, got_l, dsum, out_r, out_l, total):
    for side, (part, got, out) in enumerate(((part_r, got_r, out_r), (part_l, got_l, out_l))):
        for i in (0, 1):
            rows = slice(i * mp, (i + 1) * mp)
            y = part[rows]
            if not half:
                y = y + got[rows].astype(F32)
            elif i == side:
                y = y + got[:mp].astype(F32)
            out[rows] = y.astype(BF16)
        out[2 * mp] = got[got.shape[0] - 1]
    total[...] = dsum[...] + (_join(got_r[got_r.shape[0] - 1]) + _join(got_l[got_l.shape[0] - 1]))


def own_kernel(part, got_r, got_l, dsum, own, far):
    mp = own.shape[0]
    denom = 1.0 + dsum[...] + _join(got_r[2 * mp])
    inv = 1.0 / denom
    for j in range(2 * mp):
        y = (part[j] + got_r[j].astype(F32) + got_l[j].astype(F32)) * inv
        if j < mp:
            own[j] = y
        else:
            far[j - mp] = y.astype(BF16)


def final_kernel(ring, own, own_x, out):
    kh = own.shape[1]
    _, c = ring.devices([])
    out[:, pl.ds(pl.multiple_of(c * kh, kh), kh), :] = own[...]
    out[:, pl.ds(pl.multiple_of((1 - c) * kh, kh), kh), :] = own_x[...].astype(F32)


def _call(kernel, operands, outs, scratch=(), aliases=None, keep=True):
    return pl.pallas_call(
        kernel,
        out_shape=[pltpu.VMEM(o.shape, o.dtype) for o in outs] if keep else outs,
        in_specs=[pl.BlockSpec(memory_space=pltpu.VMEM)] * len(operands),
        out_specs=[pl.BlockSpec(memory_space=pltpu.VMEM)] * len(outs),
        scratch_shapes=scratch,
        input_output_aliases=aliases or {},
        compiler_params=pltpu.CompilerParams(vmem_limit_bytes=VMEM_LIMIT),
        cost_estimate=pl.CostEstimate(flops=1, bytes_accessed=1, transcendentals=0),
    )(*[pltpu.with_memory_space_constraint(a, pltpu.VMEM) for a in operands])


def ctf_table(defocus, radial):
    radius = (jnp.arange(radial, dtype=F32) + 1.0) / radial
    phase = 20.0 * defocus[:, None] * radius[None, :] ** 2
    return -(0.995 * jnp.sin(phase) + 0.1 * jnp.cos(phase))


def shards(ring, particles, refs, ctf_group, defocus, class_prior, cycle_weight):
    chips = ring.chips
    order = ring.order()
    opposite = chips // 2
    nl, _, q = particles.shape
    mp, k, _ = refs.shape
    kh = k // 2
    n2 = 2 * nl
    c = lax.rem(lax.axis_index("dp"), 2)

    send = lambda a, shift, cross: lax.ppermute(a, "dp", ring_perm(order, shift, cross))
    core_swap = lambda a: lax.ppermute(a, "dp", [(i, i ^ 1) for i in range(2 * chips)])
    tie = lax.optimization_barrier

    near = lax.dynamic_slice_in_dim(refs, c * kh, kh, axis=1)
    far = lax.dynamic_slice_in_dim(refs, (1 - c) * kh, kh, axis=1)
    group_x = core_swap(ctf_group)
    chunk = jnp.concatenate([near, core_swap(far)], axis=0)
    chunk, particles, defocus, cycle_weight, ctf_group = tie((chunk, particles, defocus, cycle_weight, ctf_group))
    from_left, from_right = send(chunk, 1, 0), send(chunk, -1, 0)
    particles_x = with_layout_constraint(core_swap(particles), Layout(major_to_minor=(0, 1, 2)))

    ctf = ctf_table(defocus, q // 2)
    gains = cycle_weight[None, :] * ctf
    gain_table = jnp.concatenate([gains, gains], axis=1)
    square_table = jnp.concatenate([gains * ctf, gains * ctf], axis=1)
    index = jnp.arange(defocus.shape[0], dtype=jnp.int32)[None, :]
    groups = jnp.concatenate([ctf_group, group_x])
    onehot = (groups[:, None] == index).astype(F32)
    both = jnp.dot(onehot, jnp.concatenate([gain_table, square_table], axis=1), precision=HIGHEST)
    gain, w2 = both[:, :q], both[:, q:]
    weigh = lambda a, g: jnp.transpose((a.astype(F32) * g[:, None, :]).astype(BF16), (1, 0, 2))
    wo = weigh(particles, gain[:nl])
    prior = lax.dynamic_slice_in_dim(class_prior, c * kh, kh, axis=0)[:, None]
    prior = jnp.broadcast_to(prior, (kh, n2))

    shape = jax.ShapeDtypeStruct
    acc_shapes = [shape((19, 2 * kh, n2), F32), shape((kh, q), F32)]
    pieces, where = [chunk], [(0, 0, (0, 0)), (0, mp, (0, 1))]
    acc = ws = None
    for step in range(1, opposite):
        for dist, got in ((-step, from_left), (step, from_right)):
            where += [(len(pieces), 0, (dist, 0)), (len(pieces), mp, (dist, 1))]
            pieces.append(got)
        if ws is None:
            from_left, from_right, wo, particles_x = tie((from_left, from_right, wo, particles_x))
            ws = weigh(particles_x, gain[nl:])
        elif acc is None:
            from_left, from_right, ws = tie((from_left, from_right, ws))
        else:
            from_left, from_right, acc = tie((from_left, from_right, acc))
        if step == opposite - 1:
            from_left, from_right = from_left[:mp], from_right[mp:]
        from_left, from_right = send(from_left, 1, 0), send(from_right, -1, 0)
        if step == 1 and opposite > 2:
            continue
        count = len(pieces)
        acc = _call(
            functools.partial(forward_kernel, ring, where, mp, acc is None),
            [wo, ws] + pieces + list(acc or []),
            acc_shapes,
            aliases={2 + count: 0, 3 + count: 1} if acc else None,
        )
        pieces, where = [], []

    where = [(0, 0, (opposite, 0)), (1, 0, (opposite, 1))]
    _, _, real, imag, stats = _call(
        functools.partial(score_kernel, ring, where, mp),
        [wo, ws, from_left, from_right, w2, prior] + list(acc),
        acc_shapes + [shape((19, kh, n2), F32), shape((17, kh, n2), F32), shape((2, n2), F32)],
        aliases={6: 0, 7: 1},
        scratch=[pltpu.VMEM((ROT, kh, n2), F32)],
    )
    stats_x = core_swap(stats)

    piece = shape((mp, kh, q), BF16)
    piece_d = shape((mp + 1, kh, q), BF16)
    pair = shape((2 * mp, kh, q), F32)
    pair_d = shape((2 * mp + 1, kh, q), BF16)
    dsum_shape = shape((kh, q), F32)
    table, evidence, dsum, to_right, to_left = _call(
        functools.partial(table_kernel, ring, [(opposite, 0), (opposite, 1)], mp),
        [wo, ws, real, imag, stats, stats_x, w2],
        [shape((19, 2 * kh, n2), BF16), shape((1, n2), F32), shape((kh, q), F32), piece_d, piece_d],
    )
    for dist in range(opposite - 1, -1, -1):
        got_r, got_l = send(to_right, 1, 0), send(to_left, -1, 0)
        spots = [(dist, 0), (dist, 1), (-dist, 0), (-dist, 1)] if dist else [(0, 0), (0, 1)]
        part = _call(functools.partial(numer_kernel, ring, spots, mp), [wo, ws, table], [pair] * (len(spots) // 2))
        if dist:
            to_right, to_left, dsum = _call(
                functools.partial(add_kernel, mp, dist == opposite - 1),
                [*part, got_r, got_l, dsum],
                [pair_d, pair_d, dsum_shape],
            )
    own, far = _call(own_kernel, [*part, got_r, got_l, dsum], [shape((mp, kh, q), F32), piece])
    new_refs = _call(
        functools.partial(final_kernel, ring), [own, core_swap(far)], [shape((mp, k, q), F32)], keep=False
    )[0]
    return new_refs, evidence[0, :nl]


def solution(mesh):
    in_specs = (
        P(("groups", "dp"), None, None),
        P("dp", "groups", None),
        P(("groups", "dp")),
        P("groups"),
        P("groups"),
        P(),
    )
    out_specs = (P("dp", "groups", None), P(("groups", "dp")))
    body = functools.partial(shards, Ring(mesh))
    return jax.shard_map(body, mesh=mesh, in_specs=in_specs, out_specs=out_specs, check_vma=False)
```

time: 94.2 us -> 76.4 us (0.81)
  waiting for transfers between devices: 12.6 us -> 39.7 us
  Pallas kernels: 28.8 us -> 8.6 us
  starting transfers between devices: 37.9 us -> 18.6 us
  between operations: 5.91 us -> 0.79 us
  other arithmetic: 5.15 us -> 6.52 us
    ppermute x37 -> x21, waiting for transfers between devices: 12.6 us -> 39.7 us  [the longest x16 35.8 us: shards(): lax.ppermute(a, 'dp', ring_perm(order, shift, cross))]
    pallas_call x15 -> x13, Pallas kernels: 28.8 us -> 8.6 us  [_call(): pl.pallas_call(kernel, out_shape=[pltpu.VMEM(o.shape, o.dtype) for o in o...]
    ppermute x37 -> x21, starting transfers between devices: 37.9 us -> 18.6 us  [the longest x16 17.4 us: shards(): lax.ppermute(a, 'dp', ring_perm(order, shift, cross))]
    transpose x1 -> x2, other arithmetic: 2.98 us -> 4.3 us  [shards(): jnp.transpose((a.astype(F32) * g[:, None, :]).astype(BF16), (1, 0, 2))]
  transfers between devices with their start and end apart: 37 -> 21, of which waited for: 6 -> 20; matrix products, arithmetic and copies ran while one was open for 3% -> 10% of each run, Pallas kernels for 24% -> 6%
where the time goes in v2:
time: 76.4 us; the launch traced here: 76.2 us
  waiting for transfers between devices  39.7 us (52%)
  starting transfers between devices  18.6 us (24%)
  Pallas kernels  8.6 us (11%)
  other arithmetic  6.52 us (9%)
  local copies, waits for them, and re-layouts  1.7 us (2%)
  between operations  0.79 us (1%)
    ppermute x16, waiting for transfers between devices, shards(): lax.ppermute(a, 'dp', ring_perm(order, shift, cross))  35.8 us
    ppermute x16, starting transfers between devices, shards(): lax.ppermute(a, 'dp', ring_perm(order, shift, cross))  17.4 us
    pallas_call x13, Pallas kernels, _call(): pl.pallas_call(kernel, out_shape=[pltpu.VMEM(o.shape, o.dtype) for o in o...  8.6 us
    transpose x2, other arithmetic, shards(): jnp.transpose((a.astype(F32) * g[:, None, :]).astype(BF16), (1, 0, 2))  4.3 us
    ppermute x5, waiting for transfers between devices, shards(): lax.ppermute(a, 'dp', [(i, i ^ 1) for i in range(2 * chips)])  3.85 us
  transfers between devices with their start and end apart: 21, of which 20 were waited for; matrix products, arithmetic and copies ran while one was open for 10% of the time, Pallas kernels for 6%

profile of v2, /device:TPU:0, one launch (start us, length us, event | category | flops | bytes accessed | tf_op | source)
XLA Modules:
  0.0 76.2 jit_solution(2931209219356156875)
XLA Ops:
  0.6 1.0 %constant_dynamic-slice_fusion.1 = (bf16[8,64,128]{2,1,0:T(8,128)(2,1)S(1)}, bf16[8,64,128]{2,1,0:T(8,128)(2,1)S(1)}) fusion(bf16[8,128,128]{2,1,0:T(8,128)(2,1)} %param.7, s32[]{:T(128)S(6)} %select_n.7, s32[]{:T(128)S(6)} %select_n.8), kind=kLoop, calls=%fused_computation.27 | loop fusion | bytes 524296 | tf_op jit(solution)/shard_map/dynamic_slice | solution.py:345
  2.2 1.0 %collective-permute-done = bf16[8,64,128]{2,1,0:T(8,128)(2,1)S(1)} collective-permute-done((bf16[8,64,128]{2,1,0:T(8,128)(2,1)S(1)}, bf16[8,64,128]{2,1,0:T(8,128)(2,1)S(1)}, u32[]{:S(2)}, u32[]{:S(2)}) %collective-permute-start) | collective-permute-done | bytes 131104 | tf_op jit(solution)/shard_map/ppermute | solution.py:342
  3.8 2.9 %collective-permute-start.2 = (bf16[16,64,128]{2,1,0:T(8,128)(2,1)S(1)}, bf16[16,64,128]{2,1,0:T(8,128)(2,1)S(1)}, u32[]{:S(2)}, u32[]{:S(2)}) collective-permute-start(bf16[16,64,128]{2,1,0:T(8,128)(2,1)S(1)} %pad_maximum_fusion.refs_0_), channel_id=1, source_target_pairs={{2,0},{3,1},{6,2},{7,3},{10,6},{11,7},{14,10},{15,11},{12,14},{13,... | collective-permute-start | bytes 786440 | tf_op jit(solution)/shard_map/ppermute | solution.py:341
  6.7 0.9 %collective-permute-done.3 = s32[64]{0:T(128)S(1)} collective-permute-done((s32[64]{0:T(128)}, s32[64]{0:T(128)S(1)}, u32[]{:S(2)}, u32[]{:S(2)}) %collective-permute-start.3) | collective-permute-done | bytes 288 | tf_op jit(solution)/shard_map/ppermute | solution.py:342
  10.1 2.9 %fusion.wo = bf16[128,64,128]{2,1,0:T(8,128)(2,1)S(1)} fusion(bf16[64,128,128]{2,1,0:T(8,128)(2,1)} %param.6, f32[64,128]{1,0:T(8,128)S(1)} %get-tuple-element.95), kind=kLoop, calls=%fused_computation.2 | loop fusion | flops 3145728 | bytes 4227072 | tf_op jit(solution)/shard_map/transpose | solution.py:362
  13.2 1.5 %collective-permute-done.1.refs_1_ = bf16[16,64,128]{2,1,0:T(8,128)(2,1)S(1)} collective-permute-done((bf16[16,64,128]{2,1,0:T(8,128)(2,1)S(1)}, bf16[16,64,128]{2,1,0:T(8,128)(2,1)S(1)}, u32[]{:S(2)}, u32[]{:S(2)}) %collective-permute-start.1) | collective-permute-done | bytes 262176 | tf_op jit(solution)/shard_map/ppermute | solution.py:341
  14.8 1.2 %collective-permute-start.5 = (bf16[16,64,128]{2,1,0:T(8,128)(2,1)S(1)}, bf16[16,64,128]{2,1,0:T(8,128)(2,1)S(1)}, u32[]{:S(2)}, u32[]{:S(2)}) collective-permute-start(bf16[16,64,128]{2,1,0:T(8,128)(2,1)S(1)} %collective-permute-done.1.refs_1_), channel_id=1, source_target_pairs={{2,6},{3,7},{6,10},{7,11},{10,14},{11,15},{14,12},{15,13},{12,8},{... | collective-permute-start | bytes 786440 | tf_op jit(solution)/shard_map/ppermute | solution.py:341
  16.0 0.8 %collective-permute-start.6 = (bf16[16,64,128]{2,1,0:T(8,128)(2,1)S(1)}, bf16[16,64,128]{2,1,0:T(8,128)(2,1)S(1)}, u32[]{:S(2)}, u32[]{:S(2)}) collective-permute-start(bf16[16,64,128]{2,1,0:T(8,128)(2,1)S(1)} %collective-permute-done.2.refs_2_), channel_id=1, source_target_pairs={{2,0},{3,1},{6,2},{7,3},{10,6},{11,7},{14,10},{15,11},{12,14},{13,... | collective-permute-start | bytes 786440 | tf_op jit(solution)/shard_map/ppermute | solution.py:341
  16.8 1.4 %fusion.1.ws = bf16[128,64,128]{2,1,0:T(8,128)(2,1)S(1)} fusion(bf16[64,128,128]{2,1,0:T(8,128)(2,1)S(1)} %collective-permute-done.4, f32[64,128]{1,0:T(8,128)S(1)} %get-tuple-element.94), kind=kLoop, calls=%fused_computation.3 | loop fusion | flops 3145728 | bytes 4227072 | tf_op jit(solution)/shard_map/transpose | solution.py:362
  18.2 4.5 %collective-permute-done.5.refs_3_ = bf16[16,64,128]{2,1,0:T(8,128)(2,1)S(1)} collective-permute-done((bf16[16,64,128]{2,1,0:T(8,128)(2,1)S(1)}, bf16[16,64,128]{2,1,0:T(8,128)(2,1)S(1)}, u32[]{:S(2)}, u32[]{:S(2)}) %collective-permute-start.5) | collective-permute-done | bytes 262176 | tf_op jit(solution)/shard_map/ppermute | solution.py:341
  22.7 1.4 %collective-permute-done.6.refs_4_ = bf16[16,64,128]{2,1,0:T(8,128)(2,1)S(1)} collective-permute-done((bf16[16,64,128]{2,1,0:T(8,128)(2,1)S(1)}, bf16[16,64,128]{2,1,0:T(8,128)(2,1)S(1)}, u32[]{:S(2)}, u32[]{:S(2)}) %collective-permute-start.6) | collective-permute-done | bytes 262176 | tf_op jit(solution)/shard_map/ppermute | solution.py:341
  24.1 1.6 %collective-permute-start.7 = (bf16[16,64,128]{2,1,0:T(8,128)(2,1)S(1)}, bf16[16,64,128]{2,1,0:T(8,128)(2,1)S(1)}, u32[]{:S(2)}, u32[]{:S(2)}) collective-permute-start(bf16[16,64,128]{2,1,0:T(8,128)(2,1)S(1)} %collective-permute-done.5.refs_3_), channel_id=1, source_target_pairs={{2,6},{3,7},{6,10},{7,11},{10,14},{11,15},{14,12},{15,13},{12,8},{... | collective-permute-start | bytes 786440 | tf_op jit(solution)/shard_map/ppermute | solution.py:341
  26.1 2.0 %shard_map.77 = (f32[19,128,128]{2,1,0:T(8,128)S(1)}, f32[64,128]{1,0:T(8,128)S(1)}) custom-call(bf16[128,64,128]{2,1,0:T(8,128)(2,1)S(1)} %fusion.wo, bf16[128,64,128]{2,1,0:T(8,128)(2,1)S(1)} %fusion.1.ws, bf16[16,64,128]{2,1,0:T(8,128)(2,1)S(1)} %pad_maximum_fusion.refs_0_, bf16[16,64,128]{2,1,0:T(8,128)(2,1)S(1)} %collective-permute-done.1.refs_1_, ...), custom_call_target="tpu_custom_call" | custom-call | flops 1 | bytes 1 | tf_op jit(solution)/shard_map/pallas_call | solution.py:313
  28.1 3.2 %collective-permute-done.7.refs_0_ = bf16[16,64,128]{2,1,0:T(8,128)(2,1)S(1)} collective-permute-done((bf16[16,64,128]{2,1,0:T(8,128)(2,1)S(1)}, bf16[16,64,128]{2,1,0:T(8,128)(2,1)S(1)}, u32[]{:S(2)}, u32[]{:S(2)}) %collective-permute-start.7) | collective-permute-done | bytes 262176 | tf_op jit(solution)/shard_map/ppermute | solution.py:341
  31.3 1.3 %collective-permute-done.8.refs_1_ = bf16[16,64,128]{2,1,0:T(8,128)(2,1)S(1)} collective-permute-done((bf16[16,64,128]{2,1,0:T(8,128)(2,1)S(1)}, bf16[16,64,128]{2,1,0:T(8,128)(2,1)S(1)}, u32[]{:S(2)}, u32[]{:S(2)}) %collective-permute-start.8) | collective-permute-done | bytes 262176 | tf_op jit(solution)/shard_map/ppermute | solution.py:341
  33.1 1.6 %collective-permute-start.9 = (bf16[8,64,128]{2,1,0:T(8,128)(2,1)S(1)}, bf16[8,64,128]{2,1,0:T(8,128)(2,1)S(1)}, u32[]{:S(2)}, u32[]{:S(2)}) collective-permute-start(bf16[8,64,128]{2,1,0:T(8,128)(2,1)S(1)} %slice.23), channel_id=1, source_target_pairs={{2,6},{3,7},{6,10},{7,11},{10,14},{11,15},{14,12},{15,13},{12,8},{... | collective-permute-start | bytes 393224 | tf_op jit(solution)/shard_map/ppermute | solution.py:341
  34.8 0.9 %shard_map.78 = (f32[19,128,128]{2,1,0:T(8,128)S(1)}, f32[64,128]{1,0:T(8,128)S(1)}) custom-call(bf16[128,64,128]{2,1,0:T(8,128)(2,1)S(1)} %fusion.wo, bf16[128,64,128]{2,1,0:T(8,128)(2,1)S(1)} %fusion.1.ws, bf16[16,64,128]{2,1,0:T(8,128)(2,1)S(1)} %collective-permute-done.7.refs_0_, ...), custom_call_target="tpu_custom_call", output_to_operand_aliasing={{0}: (4, {}), {1}: (5, {})} | custom-call | flops 1 | bytes 1 | tf_op jit(solution)/shard_map/pallas_call | solution.py:313
  35.7 2.0 %collective-permute-done.10.refs_1_ = bf16[8,64,128]{2,1,0:T(8,128)(2,1)S(1)} collective-permute-done((bf16[8,64,128]{2,1,0:T(8,128)(2,1)S(1)}, bf16[8,64,128]{2,1,0:T(8,128)(2,1)S(1)}, u32[]{:S(2)}, u32[]{:S(2)}) %collective-permute-start.10) | collective-permute-done | bytes 131104 | tf_op jit(solution)/shard_map/ppermute | solution.py:341
  38.1 1.8 %shard_map.79 = (f32[19,128,128]{2,1,0:T(8,128)S(1)}, f32[64,128]{1,0:T(8,128)S(1)}, f32[19,64,128]{2,1,0:T(8,128)S(1)}, f32[17,64,128]{2,1,0:T(8,128)S(1)}, f32[2,128]{1,0:T(2,128)S(1)}) custom-call(bf16[128,64,128]{2,1,0:T(8,128)(2,1)S(1)} %fusion.wo, bf16[128,64,128]{2,1,0:T(8,128)(2,1)S(1)} %fusion.1.ws, ...), custom_call_target="tpu_custom_call", output_to_operand_aliasing={{0}: (6, {}), {1}: (7, {})} | custom-call | flops 1 | bytes 1 | tf_op jit(solution)/shard_map/pallas_call | solution.py:313
  40.0 1.1 %collective-permute-done.11.other = f32[2,128]{1,0:T(2,128)S(1)} collective-permute-done((f32[2,128]{1,0:T(2,128)S(1)}, f32[2,128]{1,0:T(2,128)S(1)}, u32[]{:S(2)}, u32[]{:S(2)}) %collective-permute-start.11) | collective-permute-done | bytes 1056 | tf_op jit(solution)/shard_map/ppermute | solution.py:342
  41.7 1.6 %collective-permute-start.12 = (bf16[9,64,128]{2,1,0:T(8,128)(2,1)S(1)}, bf16[9,64,128]{2,1,0:T(8,128)(2,1)S(1)}, u32[]{:S(2)}, u32[]{:S(2)}) collective-permute-start(bf16[9,64,128]{2,1,0:T(8,128)(2,1)S(1)} %get-tuple-element.77), channel_id=1, source_target_pairs={{2,6},{3,7},{6,10},{7,11},{10,14},{11,15},{14,12},{15,13},{12,8},{... | collective-permute-start | bytes 442376 | tf_op jit(solution)/shard_map/ppermute | solution.py:341
  44.3 3.4 %collective-permute-done.12.got_r = bf16[9,64,128]{2,1,0:T(8,128)(2,1)S(1)} collective-permute-done((bf16[9,64,128]{2,1,0:T(8,128)(2,1)S(1)}, bf16[9,64,128]{2,1,0:T(8,128)(2,1)S(1)}, u32[]{:S(2)}, u32[]{:S(2)}) %collective-permute-start.12) | collective-permute-done | bytes 147488 | tf_op jit(solution)/shard_map/ppermute | solution.py:341
  47.7 1.3 %collective-permute-done.13.got_l = bf16[9,64,128]{2,1,0:T(8,128)(2,1)S(1)} collective-permute-done((bf16[9,64,128]{2,1,0:T(8,128)(2,1)S(1)}, bf16[9,64,128]{2,1,0:T(8,128)(2,1)S(1)}, u32[]{:S(2)}, u32[]{:S(2)}) %collective-permute-start.13) | collective-permute-done | bytes 147488 | tf_op jit(solution)/shard_map/ppermute | solution.py:341
  49.1 1.6 %collective-permute-start.14 = (bf16[17,64,128]{2,1,0:T(8,128)(2,1)S(1)}, bf16[17,64,128]{2,1,0:T(8,128)(2,1)S(1)}, u32[]{:S(2)}, u32[]{:S(2)}) collective-permute-start(bf16[17,64,128]{2,1,0:T(8,128)(2,1)S(1)} %get-tuple-element.80), channel_id=1, source_target_pairs={{2,6},{3,7},{6,10},{7,11},{10,14},{11,15},{14,12},{15,13},{12,8},{... | collective-permute-start | bytes 835592 | tf_op jit(solution)/shard_map/ppermute | solution.py:341
  51.7 5.1 %collective-permute-done.14.got_r = bf16[17,64,128]{2,1,0:T(8,128)(2,1)S(1)} collective-permute-done((bf16[17,64,128]{2,1,0:T(8,128)(2,1)S(1)}, bf16[17,64,128]{2,1,0:T(8,128)(2,1)S(1)}, u32[]{:S(2)}, u32[]{:S(2)}) %collective-permute-start.14) | collective-permute-done | bytes 278560 | tf_op jit(solution)/shard_map/ppermute | solution.py:341
  56.8 1.3 %collective-permute-done.15.got_l = bf16[17,64,128]{2,1,0:T(8,128)(2,1)S(1)} collective-permute-done((bf16[17,64,128]{2,1,0:T(8,128)(2,1)S(1)}, bf16[17,64,128]{2,1,0:T(8,128)(2,1)S(1)}, u32[]{:S(2)}, u32[]{:S(2)}) %collective-permute-start.15) | collective-permute-done | bytes 278560 | tf_op jit(solution)/shard_map/ppermute | solution.py:341
  58.2 1.6 %collective-permute-start.16 = (bf16[17,64,128]{2,1,0:T(8,128)(2,1)S(1)}, bf16[17,64,128]{2,1,0:T(8,128)(2,1)S(1)}, u32[]{:S(2)}, u32[]{:S(2)}) collective-permute-start(bf16[17,64,128]{2,1,0:T(8,128)(2,1)S(1)} %get-tuple-element.83), channel_id=1, source_target_pairs={{2,6},{3,7},{6,10},{7,11},{10,14},{11,15},{14,12},{15,13},{12,8},{... | collective-permute-start | bytes 835592 | tf_op jit(solution)/shard_map/ppermute | solution.py:341
  60.8 4.0 %collective-permute-done.16.got_r = bf16[17,64,128]{2,1,0:T(8,128)(2,1)S(1)} collective-permute-done((bf16[17,64,128]{2,1,0:T(8,128)(2,1)S(1)}, bf16[17,64,128]{2,1,0:T(8,128)(2,1)S(1)}, u32[]{:S(2)}, u32[]{:S(2)}) %collective-permute-start.16) | collective-permute-done | bytes 278560 | tf_op jit(solution)/shard_map/ppermute | solution.py:341
  64.8 1.7 %collective-permute-done.17.got_l = bf16[17,64,128]{2,1,0:T(8,128)(2,1)S(1)} collective-permute-done((bf16[17,64,128]{2,1,0:T(8,128)(2,1)S(1)}, bf16[17,64,128]{2,1,0:T(8,128)(2,1)S(1)}, u32[]{:S(2)}, u32[]{:S(2)}) %collective-permute-start.17) | collective-permute-done | bytes 278560 | tf_op jit(solution)/shard_map/ppermute | solution.py:341
  67.2 1.5 %collective-permute-start.19 = (bf16[17,64,128]{2,1,0:T(8,128)(2,1)S(1)}, bf16[17,64,128]{2,1,0:T(8,128)(2,1)S(1)}, u32[]{:S(2)}, u32[]{:S(2)}) collective-permute-start(bf16[17,64,128]{2,1,0:T(8,128)(2,1)S(1)} %get-tuple-element.87), channel_id=1, source_target_pairs={{2,0},{3,1},{6,2},{7,3},{10,6},{11,7},{14,10},{15,11},{12,14},{13,... | collective-permute-start | bytes 835592 | tf_op jit(solution)/shard_map/ppermute | solution.py:341
  69.1 4.1 %collective-permute-done.18.got_r = bf16[17,64,128]{2,1,0:T(8,128)(2,1)S(1)} collective-permute-done((bf16[17,64,128]{2,1,0:T(8,128)(2,1)S(1)}, bf16[17,64,128]{2,1,0:T(8,128)(2,1)S(1)}, u32[]{:S(2)}, u32[]{:S(2)}) %collective-permute-start.18) | collective-permute-done | bytes 278560 | tf_op jit(solution)/shard_map/ppermute | solution.py:341
  75.3 0.8 %shard_map.89 = f32[8,128,128]{2,1,0:T(8,128)} custom-call(f32[8,64,128]{2,1,0:T(8,128)S(1)} %get-tuple-element.89.own, bf16[8,64,128]{2,1,0:T(8,128)(2,1)S(1)} %collective-permute-done.20.own_x), custom_call_target="tpu_custom_call" | custom-call | flops 1 | bytes 1 | tf_op jit(solution)/shard_map/pallas_call | solution.py:313
  (41 shorter events, 12.3 us)
Async XLA Ops:
  1.6 1.5 %collective-permute-start = (bf16[8,64,128]{2,1,0:T(8,128)(2,1)S(1)}, bf16[8,64,128]{2,1,0:T(8,128)(2,1)S(1)}, u32[]{:S(2)}, u32[]{:S(2)}) collective-permute-start(bf16[8,64,128]{2,1,0:T(8,128)(2,1)S(1)} %get-tuple-element.93), channel_id=1, source_target_pairs={{0,1},{1,0},{2,3},{3,2},{4,5},{5,4},{6,7},{7,6},{8,9},{9,8},{10,11... | collective-permute-start | bytes 393224 | tf_op jit(solution)/shard_map/ppermute | solution.py:342
  3.2 11.6 %collective-permute-start.4 = (bf16[64,128,128]{2,1,0:T(8,128)(2,1)}, bf16[64,128,128]{2,1,0:T(8,128)(2,1)S(1)}, u32[]{:S(2)}, u32[]{:S(2)}) collective-permute-start(bf16[64,128,128]{2,1,0:T(8,128)(2,1)} %param.6), channel_id=1, source_target_pairs={{0,1},{1,0},{2,3},{3,2},{4,5},{5,4},{6,7},{7,6},{8,9},{9,8},{10,11... | collective-permute-start | bytes 6291464 | tf_op jit(solution)/shard_map/ppermute | solution.py:342
  3.6 4.0 %collective-permute-start.3 = (s32[64]{0:T(128)}, s32[64]{0:T(128)S(1)}, u32[]{:S(2)}, u32[]{:S(2)}) collective-permute-start(s32[64]{0:T(128)} %param.8), channel_id=1, source_target_pairs={{0,1},{1,0},{2,3},{3,2},{4,5},{5,4},{6,7},{7,6},{8,9},{9,8},{10,11... | collective-permute-start | bytes 776 | tf_op jit(solution)/shard_map/ppermute | solution.py:342
  3.8 9.5 %collective-permute-start.2 = (bf16[16,64,128]{2,1,0:T(8,128)(2,1)S(1)}, bf16[16,64,128]{2,1,0:T(8,128)(2,1)S(1)}, u32[]{:S(2)}, u32[]{:S(2)}) collective-permute-start(bf16[16,64,128]{2,1,0:T(8,128)(2,1)S(1)} %pad_maximum_fusion.refs_0_), channel_id=1, source_target_pairs={{2,0},{3,1},{6,2},{7,3},{10,6},{11,7},{14,10},{15,11},{12,14},{13,... | collective-permute-start | bytes 786440 | tf_op jit(solution)/shard_map/ppermute | solution.py:341
  6.7 8.1 %collective-permute-start.1 = (bf16[16,64,128]{2,1,0:T(8,128)(2,1)S(1)}, bf16[16,64,128]{2,1,0:T(8,128)(2,1)S(1)}, u32[]{:S(2)}, u32[]{:S(2)}) collective-permute-start(bf16[16,64,128]{2,1,0:T(8,128)(2,1)S(1)} %pad_maximum_fusion.refs_0_), channel_id=1, source_target_pairs={{2,6},{3,7},{6,10},{7,11},{10,14},{11,15},{14,12},{15,13},{12,8},{... | collective-permute-start | bytes 786440 | tf_op jit(solution)/shard_map/ppermute | solution.py:341
  14.8 7.9 %collective-permute-start.5 = (bf16[16,64,128]{2,1,0:T(8,128)(2,1)S(1)}, bf16[16,64,128]{2,1,0:T(8,128)(2,1)S(1)}, u32[]{:S(2)}, u32[]{:S(2)}) collective-permute-start(bf16[16,64,128]{2,1,0:T(8,128)(2,1)S(1)} %collective-permute-done.1.refs_1_), channel_id=1, source_target_pairs={{2,6},{3,7},{6,10},{7,11},{10,14},{11,15},{14,12},{15,13},{12,8},{... | collective-permute-start | bytes 786440 | tf_op jit(solution)/shard_map/ppermute | solution.py:341
  16.0 8.1 %collective-permute-start.6 = (bf16[16,64,128]{2,1,0:T(8,128)(2,1)S(1)}, bf16[16,64,128]{2,1,0:T(8,128)(2,1)S(1)}, u32[]{:S(2)}, u32[]{:S(2)}) collective-permute-start(bf16[16,64,128]{2,1,0:T(8,128)(2,1)S(1)} %collective-permute-done.2.refs_2_), channel_id=1, source_target_pairs={{2,0},{3,1},{6,2},{7,3},{10,6},{11,7},{14,10},{15,11},{12,14},{13,... | collective-permute-start | bytes 786440 | tf_op jit(solution)/shard_map/ppermute | solution.py:341
  18.2 16.5 %copy-start = (f32[128]{0:T(128)S(1)}, f32[128]{0:T(128)}, u32[]{:S(2)}) copy-start(f32[128]{0:T(128)} %param.10) | copy-start | bytes 1540
  24.1 7.2 %collective-permute-start.7 = (bf16[16,64,128]{2,1,0:T(8,128)(2,1)S(1)}, bf16[16,64,128]{2,1,0:T(8,128)(2,1)S(1)}, u32[]{:S(2)}, u32[]{:S(2)}) collective-permute-start(bf16[16,64,128]{2,1,0:T(8,128)(2,1)S(1)} %collective-permute-done.5.refs_3_), channel_id=1, source_target_pairs={{2,6},{3,7},{6,10},{7,11},{10,14},{11,15},{14,12},{15,13},{12,8},{... | collective-permute-start | bytes 786440 | tf_op jit(solution)/shard_map/ppermute | solution.py:341
  25.6 6.9 %collective-permute-start.8 = (bf16[16,64,128]{2,1,0:T(8,128)(2,1)S(1)}, bf16[16,64,128]{2,1,0:T(8,128)(2,1)S(1)}, u32[]{:S(2)}, u32[]{:S(2)}) collective-permute-start(bf16[16,64,128]{2,1,0:T(8,128)(2,1)S(1)} %collective-permute-done.6.refs_4_), channel_id=1, source_target_pairs={{2,0},{3,1},{6,2},{7,3},{10,6},{11,7},{14,10},{15,11},{12,14},{13,... | collective-permute-start | bytes 786440 | tf_op jit(solution)/shard_map/ppermute | solution.py:341
  32.6 5.0 %collective-permute-start.10 = (bf16[8,64,128]{2,1,0:T(8,128)(2,1)S(1)}, bf16[8,64,128]{2,1,0:T(8,128)(2,1)S(1)}, u32[]{:S(2)}, u32[]{:S(2)}) collective-permute-start(bf16[8,64,128]{2,1,0:T(8,128)(2,1)S(1)} %slice.24), channel_id=1, source_target_pairs={{2,0},{3,1},{6,2},{7,3},{10,6},{11,7},{14,10},{15,11},{12,14},{13,... | collective-permute-start | bytes 393224 | tf_op jit(solution)/shard_map/ppermute | solution.py:341
  33.1 5.0 %collective-permute-start.9 = (bf16[8,64,128]{2,1,0:T(8,128)(2,1)S(1)}, bf16[8,64,128]{2,1,0:T(8,128)(2,1)S(1)}, u32[]{:S(2)}, u32[]{:S(2)}) collective-permute-start(bf16[8,64,128]{2,1,0:T(8,128)(2,1)S(1)} %slice.23), channel_id=1, source_target_pairs={{2,6},{3,7},{6,10},{7,11},{10,14},{11,15},{14,12},{15,13},{12,8},{... | collective-permute-start | bytes 393224 | tf_op jit(solution)/shard_map/ppermute | solution.py:341
  39.9 1.2 %collective-permute-start.11 = (f32[2,128]{1,0:T(2,128)S(1)}, f32[2,128]{1,0:T(2,128)S(1)}, u32[]{:S(2)}, u32[]{:S(2)}) collective-permute-start(f32[2,128]{1,0:T(2,128)S(1)} %get-tuple-element.69.mine), channel_id=1, source_target_pairs={{0,1},{1,0},{2,3},{3,2},{4,5},{5,4},{6,7},{7,6},{8,9},{9,8},{10,11... | collective-permute-start | bytes 3080 | tf_op jit(solution)/shard_map/ppermute | solution.py:342
  41.7 6.0 %collective-permute-start.12 = (bf16[9,64,128]{2,1,0:T(8,128)(2,1)S(1)}, bf16[9,64,128]{2,1,0:T(8,128)(2,1)S(1)}, u32[]{:S(2)}, u32[]{:S(2)}) collective-permute-start(bf16[9,64,128]{2,1,0:T(8,128)(2,1)S(1)} %get-tuple-element.77), channel_id=1, source_target_pairs={{2,6},{3,7},{6,10},{7,11},{10,14},{11,15},{14,12},{15,13},{12,8},{... | collective-permute-start | bytes 442376 | tf_op jit(solution)/shard_map/ppermute | solution.py:341
  43.3 5.7 %collective-permute-start.13 = (bf16[9,64,128]{2,1,0:T(8,128)(2,1)S(1)}, bf16[9,64,128]{2,1,0:T(8,128)(2,1)S(1)}, u32[]{:S(2)}, u32[]{:S(2)}) collective-permute-start(bf16[9,64,128]{2,1,0:T(8,128)(2,1)S(1)} %get-tuple-element.78), channel_id=1, source_target_pairs={{2,0},{3,1},{6,2},{7,3},{10,6},{11,7},{14,10},{15,11},{12,14},{13,... | collective-permute-start | bytes 442376 | tf_op jit(solution)/shard_map/ppermute | solution.py:341
  49.1 7.6 %collective-permute-start.14 = (bf16[17,64,128]{2,1,0:T(8,128)(2,1)S(1)}, bf16[17,64,128]{2,1,0:T(8,128)(2,1)S(1)}, u32[]{:S(2)}, u32[]{:S(2)}) collective-permute-start(bf16[17,64,128]{2,1,0:T(8,128)(2,1)S(1)} %get-tuple-element.80), channel_id=1, source_target_pairs={{2,6},{3,7},{6,10},{7,11},{10,14},{11,15},{14,12},{15,13},{12,8},{... | collective-permute-start | bytes 835592 | tf_op jit(solution)/shard_map/ppermute | solution.py:341
  50.7 7.3 %collective-permute-start.15 = (bf16[17,64,128]{2,1,0:T(8,128)(2,1)S(1)}, bf16[17,64,128]{2,1,0:T(8,128)(2,1)S(1)}, u32[]{:S(2)}, u32[]{:S(2)}) collective-permute-start(bf16[17,64,128]{2,1,0:T(8,128)(2,1)S(1)} %get-tuple-element.81), channel_id=1, source_target_pairs={{2,0},{3,1},{6,2},{7,3},{10,6},{11,7},{14,10},{15,11},{12,14},{13,... | collective-permute-start | bytes 835592 | tf_op jit(solution)/shard_map/ppermute | solution.py:341
  58.2 6.6 %collective-permute-start.16 = (bf16[17,64,128]{2,1,0:T(8,128)(2,1)S(1)}, bf16[17,64,128]{2,1,0:T(8,128)(2,1)S(1)}, u32[]{:S(2)}, u32[]{:S(2)}) collective-permute-start(bf16[17,64,128]{2,1,0:T(8,128)(2,1)S(1)} %get-tuple-element.83), channel_id=1, source_target_pairs={{2,6},{3,7},{6,10},{7,11},{10,14},{11,15},{14,12},{15,13},{12,8},{... | collective-permute-start | bytes 835592 | tf_op jit(solution)/shard_map/ppermute | solution.py:341
  59.8 6.6 %collective-permute-start.17 = (bf16[17,64,128]{2,1,0:T(8,128)(2,1)S(1)}, bf16[17,64,128]{2,1,0:T(8,128)(2,1)S(1)}, u32[]{:S(2)}, u32[]{:S(2)}) collective-permute-start(bf16[17,64,128]{2,1,0:T(8,128)(2,1)S(1)} %get-tuple-element.84), channel_id=1, source_target_pairs={{2,0},{3,1},{6,2},{7,3},{10,6},{11,7},{14,10},{15,11},{12,14},{13,... | collective-permute-start | bytes 835592 | tf_op jit(solution)/shard_map/ppermute | solution.py:341
  66.6 6.6 %collective-permute-start.18 = (bf16[17,64,128]{2,1,0:T(8,128)(2,1)S(1)}, bf16[17,64,128]{2,1,0:T(8,128)(2,1)S(1)}, u32[]{:S(2)}, u32[]{:S(2)}) collective-permute-start(bf16[17,64,128]{2,1,0:T(8,128)(2,1)S(1)} %get-tuple-element.86), channel_id=1, source_target_pairs={{2,6},{3,7},{6,10},{7,11},{10,14},{11,15},{14,12},{15,13},{12,8},{... | collective-permute-start | bytes 835592 | tf_op jit(solution)/shard_map/ppermute | solution.py:341
  67.2 6.5 %collective-permute-start.19 = (bf16[17,64,128]{2,1,0:T(8,128)(2,1)S(1)}, bf16[17,64,128]{2,1,0:T(8,128)(2,1)S(1)}, u32[]{:S(2)}, u32[]{:S(2)}) collective-permute-start(bf16[17,64,128]{2,1,0:T(8,128)(2,1)S(1)} %get-tuple-element.87), channel_id=1, source_target_pairs={{2,0},{3,1},{6,2},{7,3},{10,6},{11,7},{14,10},{15,11},{12,14},{13,... | collective-permute-start | bytes 835592 | tf_op jit(solution)/shard_map/ppermute | solution.py:341
  73.9 1.4 %collective-permute-start.20 = (bf16[8,64,128]{2,1,0:T(8,128)(2,1)S(1)}, bf16[8,64,128]{2,1,0:T(8,128)(2,1)S(1)}, u32[]{:S(2)}, u32[]{:S(2)}) collective-permute-start(bf16[8,64,128]{2,1,0:T(8,128)(2,1)S(1)} %get-tuple-element.90), channel_id=1, source_target_pairs={{0,1},{1,0},{2,3},{3,2},{4,5},{5,4},{6,7},{7,6},{8,9},{9,8},{10,11... | collective-permute-start | bytes 393224 | tf_op jit(solution)/shard_map/ppermute | solution.py:342

commit v3 on v2

--- a/solution.py
+++ b/solution.py
@@ -163,6 +163,14 @@
     energy[...] += squares
 
 
+def _forward_all(ring, spots, mp, wo, ws, pieces, acc, energy):
+    at, _ = ring.devices(spots)
+    for piece in pieces:
+        for row in range(0, piece.shape[0], mp):
+            if at:
+                _forward(at.pop(0), mp, piece, row, wo, ws, acc, energy)
+
+
 def _backward(m, table, wo, ws):
     t, s = _residue(m)
     w = jnp.concatenate([wo[m], ws[m]], axis=0)
@@ -172,21 +180,23 @@
     return y[:kh] + turned
 
 
+def split_kernel(from_left, from_right, p_x, p_y, q_x, q_y):
+    mp = p_x.shape[0]
+    p_x[...], q_y[...] = from_left[:mp], from_left[mp:]
+    q_x[...], p_y[...] = from_right[:mp], from_right[mp:]
+
+
 def forward_kernel(ring, spots, mp, first, wo, ws, *refs):
     acc, energy = refs[-2:]
     if first:
         acc[...] = jnp.zeros_like(acc)
         energy[...] = jnp.zeros_like(energy)
-    at, _ = ring.devices([place for _, _, place in spots])
-    for base, (operand, row, _) in zip(at, spots):
-        _forward(base, mp, refs[operand], row, wo, ws, acc, energy)
+    _forward_all(ring, spots, mp, wo, ws, refs, acc, energy)
 
 
 def score_kernel(ring, spots, mp, wo, ws, *refs):
-    at, _ = ring.devices([place for _, _, place in spots])
     w2, prior, _, _, acc, energy, real_out, imag_out, stats, scores = refs[2:]
-    for base, (operand, row, _) in zip(at, spots):
-        _forward(base, mp, refs[operand], row, wo, ws, acc, energy)
+    _forward_all(ring, spots, mp, wo, ws, refs, acc, energy)
     kh, n = scores.shape[1:]
     norm = lax.dot_general(
         energy[...], w2[...], (((1,), (1,)), ((), ())), precision=HIGHEST, preferred_element_type=F32
@@ -254,14 +264,15 @@
     for base, out in zip(at, outs):
         for j in range(mp):
             out[j] = _backward(base * mp + j, table, wo, ws).astype(out.dtype)
+    for out in outs[:2]:
         out[mp] = _split(dpart[...])
 
 
 def numer_kernel(ring, spots, mp, wo, ws, table, *outs):
     at, _ = ring.devices(spots)
-    for i, base in enumerate(at):
+    for base, out in zip(at, outs):
         for j in range(mp):
-            outs[i // 2][i % 2 * mp + j] = _backward(base * mp + j, table, wo, ws)
+            out[j] = _backward(base * mp + j, table, wo, ws)
 
 
 def _split(x):
@@ -276,30 +287,24 @@
     return wide + pltpu.roll(wide, row.shape[1] // 2, 1)
 
 
-def add_kernel(mp, half, part_r, part_l, got_r, got_l, dsum, out_r, out_l, total):
-    for side, (part, got, out) in enumerate(((part_r, got_r, out_r), (part_l, got_l, out_l))):
-        for i in (0, 1):
-            rows = slice(i * mp, (i + 1) * mp)
-            y = part[rows]
-            if not half:
-                y = y + got[rows].astype(F32)
-            elif i == side:
-                y = y + got[:mp].astype(F32)
-            out[rows] = y.astype(BF16)
-        out[2 * mp] = got[got.shape[0] - 1]
-    total[...] = dsum[...] + (_join(got_r[got_r.shape[0] - 1]) + _join(got_l[got_l.shape[0] - 1]))
-
-
-def own_kernel(part, got_r, got_l, dsum, own, far):
+def add_kernel(part_x, part_y, got_x, got_y, *refs):
+    n = part_x.shape[0]
+    tails = got_x.shape[0] > n
+    out_x, out_y = refs[1:3] if tails else refs
+    for part, got, out in ((part_x, got_x, out_x), (part_y, got_y, out_y)):
+        out[:n] = (part[...] + got[:n].astype(F32)).astype(BF16)
+        if tails:
+            out[n] = got[n]
+    if tails:
+        refs[3][...] = refs[0][...] + (_join(got_x[n]) + _join(got_y[n]))
+
+
+def own_kernel(part_x, part_y, p_x, p_y, q_x, q_y, dsum, own, far):
     mp = own.shape[0]
-    denom = 1.0 + dsum[...] + _join(got_r[2 * mp])
-    inv = 1.0 / denom
-    for j in range(2 * mp):
-        y = (part[j] + got_r[j].astype(F32) + got_l[j].astype(F32)) * inv
-        if j < mp:
-            own[j] = y
-        else:
-            far[j - mp] = y.astype(BF16)
+    inv = 1.0 / (1.0 + dsum[...] + _join(p_x[mp]))
+    for j in range(mp):
+        own[j] = (part_x[j] + p_x[j].astype(F32) + q_x[j].astype(F32)) * inv
+        far[j] = ((part_y[j] + p_y[j].astype(F32) + q_y[j].astype(F32)) * inv).astype(BF16)
 
 
 def final_kernel(ring, own, own_x, out):
@@ -366,22 +371,22 @@
 
     shape = jax.ShapeDtypeStruct
     acc_shapes = [shape((19, 2 * kh, n2), F32), shape((kh, q), F32)]
-    pieces, where = [chunk], [(0, 0, (0, 0)), (0, mp, (0, 1))]
+    from_left, from_right, wo, particles_x = tie((from_left, from_right, wo, particles_x))
+    p_x, p_y, q_x, q_y = _call(split_kernel, [from_left, from_right], [shape((mp, kh, q), BF16)] * 4)
+    pieces, where = [chunk], [(0, 0), (0, 1)]
     acc = ws = None
     for step in range(1, opposite):
-        for dist, got in ((-step, from_left), (step, from_right)):
-            where += [(len(pieces), 0, (dist, 0)), (len(pieces), mp, (dist, 1))]
-            pieces.append(got)
+        pieces = pieces + [p_x, p_y, q_x, q_y]
+        where = where + [(-step, 0), (step, 1), (step, 0), (-step, 1)]
         if ws is None:
-            from_left, from_right, wo, particles_x = tie((from_left, from_right, wo, particles_x))
             ws = weigh(particles_x, gain[nl:])
         elif acc is None:
-            from_left, from_right, ws = tie((from_left, from_right, ws))
+            p_x, p_y, ws = tie((p_x, p_y, ws))
         else:
-            from_left, from_right, acc = tie((from_left, from_right, acc))
-        if step == opposite - 1:
-            from_left, from_right = from_left[:mp], from_right[mp:]
-        from_left, from_right = send(from_left, 1, 0), send(from_right, -1, 0)
+            p_x, p_y, acc = tie((p_x, p_y, acc))
+        p_x, p_y = send(p_x, 1, 0), send(p_y, -1, 0)
+        if step < opposite - 1:
+            q_x, q_y = send(q_x, -1, 0), send(q_y, 1, 0)
         if step == 1 and opposite > 2:
             continue
         count = len(pieces)
@@ -393,10 +398,10 @@
         )
         pieces, where = [], []
 
-    where = [(0, 0, (opposite, 0)), (1, 0, (opposite, 1))]
+    where = [(opposite, 0), (opposite, 1)]
     _, _, real, imag, stats = _call(
         functools.partial(score_kernel, ring, where, mp),
-        [wo, ws, from_left, from_right, w2, prior] + list(acc),
+        [wo, ws, p_x, p_y, w2, prior] + list(acc),
         acc_shapes + [shape((19, kh, n2), F32), shape((17, kh, n2), F32), shape((2, n2), F32)],
         aliases={6: 0, 7: 1},
         scratch=[pltpu.VMEM((ROT, kh, n2), F32)],
@@ -405,25 +410,24 @@
 
     piece = shape((mp, kh, q), BF16)
     piece_d = shape((mp + 1, kh, q), BF16)
-    pair = shape((2 * mp, kh, q), F32)
-    pair_d = shape((2 * mp + 1, kh, q), BF16)
+    wide = shape((mp, kh, q), F32)
     dsum_shape = shape((kh, q), F32)
-    table, evidence, dsum, to_right, to_left = _call(
-        functools.partial(table_kernel, ring, [(opposite, 0), (opposite, 1)], mp),
+    far = opposite - 1
+    table, evidence, dsum, p_x, p_y, q_x, q_y = _call(
+        functools.partial(table_kernel, ring, [(opposite, 0), (opposite, 1), (-far, 0), (far, 1)], mp),
         [wo, ws, real, imag, stats, stats_x, w2],
-        [shape((19, 2 * kh, n2), BF16), shape((1, n2), F32), shape((kh, q), F32), piece_d, piece_d],
+        [shape((19, 2 * kh, n2), BF16), shape((1, n2), F32), dsum_shape, piece_d, piece_d, piece, piece],
     )
-    for dist in range(opposite - 1, -1, -1):
-        got_r, got_l = send(to_right, 1, 0), send(to_left, -1, 0)
-        spots = [(dist, 0), (dist, 1), (-dist, 0), (-dist, 1)] if dist else [(0, 0), (0, 1)]
-        part = _call(functools.partial(numer_kernel, ring, spots, mp), [wo, ws, table], [pair] * (len(spots) // 2))
+    for dist in range(far, -1, -1):
+        p_x, p_y = send(p_x, 1, 0), send(p_y, -1, 0)
         if dist:
-            to_right, to_left, dsum = _call(
-                functools.partial(add_kernel, mp, dist == opposite - 1),
-                [*part, got_r, got_l, dsum],
-                [pair_d, pair_d, dsum_shape],
-            )
-    own, far = _call(own_kernel, [*part, got_r, got_l, dsum], [shape((mp, kh, q), F32), piece])
+            q_x, q_y = send(q_x, -1, 0), send(q_y, 1, 0)
+            spots = [(dist, 0), (-dist, 1), (-(dist - 1), 0), (dist - 1, 1)]
+            px, py, qx, qy = _call(functools.partial(numer_kernel, ring, spots, mp), [wo, ws, table], [wide] * 4)
+            p_x, p_y, dsum = _call(add_kernel, [px, py, p_x, p_y, dsum], [piece_d, piece_d, dsum_shape])
+            if dist > 1:
+                q_x, q_y = _call(add_kernel, [qx, qy, q_x, q_y], [piece, piece])
+    own, far = _call(own_kernel, [qx, qy, p_x, p_y, q_x, q_y, dsum], [shape((mp, kh, q), F32), piece])
     new_refs = _call(
         functools.partial(final_kernel, ring), [own, core_swap(far)], [shape((mp, k, q), F32)], keep=False
     )[0]

time: 76.4 us -> 72.1 us (0.944)
  waiting for transfers between devices: 39.7 us -> 25.4 us
  starting transfers between devices: 18.6 us -> 28.8 us
    ppermute x16 -> x26, waiting for transfers between devices: 35.8 us -> 21.6 us  [shards(): lax.ppermute(a, 'dp', ring_perm(order, shift, cross))]
    ppermute x16 -> x26, starting transfers between devices: 17.4 us -> 27.5 us  [shards(): lax.ppermute(a, 'dp', ring_perm(order, shift, cross))]
    pallas_call x13 -> x15, Pallas kernels: 8.6 us -> 8.47 us  [_call(): pl.pallas_call(kernel, out_shape=[pltpu.VMEM(o.shape, o.dtype) for o in o...]
  transfers between devices with their start and end apart: 21 -> 31, of which waited for: 20 -> 22; matrix products, arithmetic and copies ran while one was open for 10% -> 10% of each run, Pallas kernels for 6% -> 7%
where the time goes in v3:
time: 72.1 us; the launch traced here: 71.9 us
  starting transfers between devices  28.8 us (40%)
  waiting for transfers between devices  25.4 us (35%)
  Pallas kernels  8.47 us (12%)
  other arithmetic  6.52 us (9%)
  local copies, waits for them, and re-layouts  1.68 us (2%)
  between operations  0.8 us (1%)
    ppermute x26, starting transfers between devices, shards(): lax.ppermute(a, 'dp', ring_perm(order, shift, cross))  27.5 us
    ppermute x26, waiting for transfers between devices, shards(): lax.ppermute(a, 'dp', ring_perm(order, shift, cross))  21.6 us
    pallas_call x15, Pallas kernels, _call(): pl.pallas_call(kernel, out_shape=[pltpu.VMEM(o.shape, o.dtype) for o in o...  8.47 us
    transpose x2, other arithmetic, shards(): jnp.transpose((a.astype(F32) * g[:, None, :]).astype(BF16), (1, 0, 2))  4.3 us
    ppermute x5, waiting for transfers between devices, shards(): lax.ppermute(a, 'dp', [(i, i ^ 1) for i in range(2 * chips)])  3.85 us
  transfers between devices with their start and end apart: 31, of which 22 were waited for; matrix products, arithmetic and copies ran while one was open for 10% of the time, Pallas kernels for 7%

profile of v3, /device:TPU:0, one launch (start us, length us, event | category | flops | bytes accessed | tf_op | source)
XLA Modules:
  0.0 71.9 jit_solution(14911001156852546405)
XLA Ops:
  0.6 1.0 %constant_dynamic-slice_fusion.1 = (bf16[8,64,128]{2,1,0:T(8,128)(2,1)S(1)}, bf16[8,64,128]{2,1,0:T(8,128)(2,1)S(1)}) fusion(bf16[8,128,128]{2,1,0:T(8,128)(2,1)} %param.7, s32[]{:T(128)S(6)} %select_n.7, s32[]{:T(128)S(6)} %select_n.8), kind=kLoop, calls=%fused_computation.27 | loop fusion | bytes 524296 | tf_op jit(solution)/shard_map/dynamic_slice | solution.py:350
  2.2 1.0 %collective-permute-done = bf16[8,64,128]{2,1,0:T(8,128)(2,1)S(1)} collective-permute-done((bf16[8,64,128]{2,1,0:T(8,128)(2,1)S(1)}, bf16[8,64,128]{2,1,0:T(8,128)(2,1)S(1)}, u32[]{:S(2)}, u32[]{:S(2)}) %collective-permute-start) | collective-permute-done | bytes 131104 | tf_op jit(solution)/shard_map/ppermute | solution.py:347
  3.8 2.9 %collective-permute-start.2 = (bf16[16,64,128]{2,1,0:T(8,128)(2,1)S(1)}, bf16[16,64,128]{2,1,0:T(8,128)(2,1)S(1)}, u32[]{:S(2)}, u32[]{:S(2)}) collective-permute-start(bf16[16,64,128]{2,1,0:T(8,128)(2,1)S(1)} %pad_maximum_fusion.refs_0_), channel_id=1, source_target_pairs={{2,0},{3,1},{6,2},{7,3},{10,6},{11,7},{14,10},{15,11},{12,14},{13,... | collective-permute-start | bytes 786440 | tf_op jit(solution)/shard_map/ppermute | solution.py:346
  6.7 0.9 %collective-permute-done.3 = s32[64]{0:T(128)S(1)} collective-permute-done((s32[64]{0:T(128)}, s32[64]{0:T(128)S(1)}, u32[]{:S(2)}, u32[]{:S(2)}) %collective-permute-start.3) | collective-permute-done | bytes 288 | tf_op jit(solution)/shard_map/ppermute | solution.py:347
  10.1 2.9 %fusion.wo = bf16[128,64,128]{2,1,0:T(8,128)(2,1)S(1)} fusion(bf16[64,128,128]{2,1,0:T(8,128)(2,1)} %param.6, f32[64,128]{1,0:T(8,128)S(1)} %get-tuple-element.127), kind=kLoop, calls=%fused_computation.2 | loop fusion | flops 3145728 | bytes 4227072 | tf_op jit(solution)/shard_map/transpose | solution.py:367
  13.2 1.5 %collective-permute-done.1.from_left = bf16[16,64,128]{2,1,0:T(8,128)(2,1)S(1)} collective-permute-done((bf16[16,64,128]{2,1,0:T(8,128)(2,1)S(1)}, bf16[16,64,128]{2,1,0:T(8,128)(2,1)S(1)}, u32[]{:S(2)}, u32[]{:S(2)}) %collective-permute-start.1) | collective-permute-done | bytes 262176 | tf_op jit(solution)/shard_map/ppermute | solution.py:346
  14.8 1.2 %collective-permute-start.5 = (bf16[8,64,128]{2,1,0:T(8,128)(2,1)S(1)}, bf16[8,64,128]{2,1,0:T(8,128)(2,1)S(1)}, u32[]{:S(2)}, u32[]{:S(2)}) collective-permute-start(bf16[8,64,128]{2,1,0:T(8,128)(2,1)S(1)} %get-tuple-element.71.refs_1_), channel_id=1, source_target_pairs={{2,6},{3,7},{6,10},{7,11},{10,14},{11,15},{14,12},{15,13},{12,8},{... | collective-permute-start | bytes 393224 | tf_op jit(solution)/shard_map/ppermute | solution.py:346
  16.9 1.6 %collective-permute-start.9 = (bf16[8,64,128]{2,1,0:T(8,128)(2,1)S(1)}, bf16[8,64,128]{2,1,0:T(8,128)(2,1)S(1)}, u32[]{:S(2)}, u32[]{:S(2)}) collective-permute-start(bf16[8,64,128]{2,1,0:T(8,128)(2,1)S(1)} %get-tuple-element.77.refs_3_), channel_id=1, source_target_pairs={{2,0},{3,1},{6,2},{7,3},{10,6},{11,7},{14,10},{15,11},{12,14},{13,... | collective-permute-start | bytes 393224 | tf_op jit(solution)/shard_map/ppermute | solution.py:346
  18.9 1.4 %fusion.1.ws = bf16[128,64,128]{2,1,0:T(8,128)(2,1)S(1)} fusion(bf16[64,128,128]{2,1,0:T(8,128)(2,1)S(1)} %collective-permute-done.4, f32[64,128]{1,0:T(8,128)S(1)} %get-tuple-element.126), kind=kLoop, calls=%fused_computation.3 | loop fusion | flops 3145728 | bytes 4227072 | tf_op jit(solution)/shard_map/transpose | solution.py:367
  20.3 2.1 %collective-permute-done.6.refs_6_ = bf16[8,64,128]{2,1,0:T(8,128)(2,1)S(1)} collective-permute-done((bf16[8,64,128]{2,1,0:T(8,128)(2,1)S(1)}, bf16[8,64,128]{2,1,0:T(8,128)(2,1)S(1)}, u32[]{:S(2)}, u32[]{:S(2)}) %collective-permute-start.6) | collective-permute-done | bytes 131104 | tf_op jit(solution)/shard_map/ppermute | solution.py:346
  22.4 1.6 %collective-permute-start.7 = (bf16[8,64,128]{2,1,0:T(8,128)(2,1)S(1)}, bf16[8,64,128]{2,1,0:T(8,128)(2,1)S(1)}, u32[]{:S(2)}, u32[]{:S(2)}) collective-permute-start(bf16[8,64,128]{2,1,0:T(8,128)(2,1)S(1)} %collective-permute-done.5.refs_5_), channel_id=1, source_target_pairs={{2,6},{3,7},{6,10},{7,11},{10,14},{11,15},{14,12},{15,13},{12,8},{... | collective-permute-start | bytes 393224 | tf_op jit(solution)/shard_map/ppermute | solution.py:346
  25.2 1.3 %collective-permute-start.14 = (bf16[8,64,128]{2,1,0:T(8,128)(2,1)S(1)}, bf16[8,64,128]{2,1,0:T(8,128)(2,1)S(1)}, u32[]{:S(2)}, u32[]{:S(2)}) collective-permute-start(bf16[8,64,128]{2,1,0:T(8,128)(2,1)S(1)} %collective-permute-done.10.refs_8_), channel_id=1, source_target_pairs={{2,6},{3,7},{6,10},{7,11},{10,14},{11,15},{14,12},{15,13},{12,8},{... | collective-permute-start | bytes 393224 | tf_op jit(solution)/shard_map/ppermute | solution.py:346
  26.5 2.0 %shard_map.78 = (f32[19,128,128]{2,1,0:T(8,128)S(1)}, f32[64,128]{1,0:T(8,128)S(1)}) custom-call(bf16[128,64,128]{2,1,0:T(8,128)(2,1)S(1)} %fusion.wo, bf16[128,64,128]{2,1,0:T(8,128)(2,1)S(1)} %fusion.1.ws, bf16[16,64,128]{2,1,0:T(8,128)(2,1)S(1)} %pad_maximum_fusion.refs_0_, bf16[8,64,128]{2,1,0:T(8,128)(2,1)S(1)} %get-tuple-element.71.refs_1_, ...), custom_call_target="tpu_custom_call" | custom-call | flops 1 | bytes 1 | tf_op jit(solution)/shard_map/pallas_call | solution.py:318
  29.0 1.6 %collective-permute-start.11 = (bf16[8,64,128]{2,1,0:T(8,128)(2,1)S(1)}, bf16[8,64,128]{2,1,0:T(8,128)(2,1)S(1)}, u32[]{:S(2)}, u32[]{:S(2)}) collective-permute-start(bf16[8,64,128]{2,1,0:T(8,128)(2,1)S(1)} %collective-permute-done.7.refs_0_), channel_id=1, source_target_pairs={{2,6},{3,7},{6,10},{7,11},{10,14},{11,15},{14,12},{15,13},{12,8},{... | collective-permute-start | bytes 393224 | tf_op jit(solution)/shard_map/ppermute | solution.py:346
  32.3 1.6 %collective-permute-done.11.refs_0_ = bf16[8,64,128]{2,1,0:T(8,128)(2,1)S(1)} collective-permute-done((bf16[8,64,128]{2,1,0:T(8,128)(2,1)S(1)}, bf16[8,64,128]{2,1,0:T(8,128)(2,1)S(1)}, u32[]{:S(2)}, u32[]{:S(2)}) %collective-permute-start.11) | collective-permute-done | bytes 131104 | tf_op jit(solution)/shard_map/ppermute | solution.py:346
  33.9 1.6 %collective-permute-done.12.refs_1_ = bf16[8,64,128]{2,1,0:T(8,128)(2,1)S(1)} collective-permute-done((bf16[8,64,128]{2,1,0:T(8,128)(2,1)S(1)}, bf16[8,64,128]{2,1,0:T(8,128)(2,1)S(1)}, u32[]{:S(2)}, u32[]{:S(2)}) %collective-permute-start.12) | collective-permute-done | bytes 131104 | tf_op jit(solution)/shard_map/ppermute | solution.py:346
  35.6 1.8 %shard_map.80 = (f32[19,128,128]{2,1,0:T(8,128)S(1)}, f32[64,128]{1,0:T(8,128)S(1)}, f32[19,64,128]{2,1,0:T(8,128)S(1)}, f32[17,64,128]{2,1,0:T(8,128)S(1)}, f32[2,128]{1,0:T(2,128)S(1)}) custom-call(bf16[128,64,128]{2,1,0:T(8,128)(2,1)S(1)} %fusion.wo, bf16[128,64,128]{2,1,0:T(8,128)(2,1)S(1)} %fusion.1.ws, ...), custom_call_target="tpu_custom_call", output_to_operand_aliasing={{0}: (6, {}), {1}: (7, {})} | custom-call | flops 1 | bytes 1 | tf_op jit(solution)/shard_map/pallas_call | solution.py:318
  37.4 1.1 %collective-permute-done.15.other = f32[2,128]{1,0:T(2,128)S(1)} collective-permute-done((f32[2,128]{1,0:T(2,128)S(1)}, f32[2,128]{1,0:T(2,128)S(1)}, u32[]{:S(2)}, u32[]{:S(2)}) %collective-permute-start.15) | collective-permute-done | bytes 1056 | tf_op jit(solution)/shard_map/ppermute | solution.py:347
  39.3 1.6 %collective-permute-start.16 = (bf16[9,64,128]{2,1,0:T(8,128)(2,1)S(1)}, bf16[9,64,128]{2,1,0:T(8,128)(2,1)S(1)}, u32[]{:S(2)}, u32[]{:S(2)}) collective-permute-start(bf16[9,64,128]{2,1,0:T(8,128)(2,1)S(1)} %get-tuple-element.99), channel_id=1, source_target_pairs={{2,6},{3,7},{6,10},{7,11},{10,14},{11,15},{14,12},{15,13},{12,8},{... | collective-permute-start | bytes 442376 | tf_op jit(solution)/shard_map/ppermute | solution.py:346
  41.9 3.4 %collective-permute-done.16.got_x = bf16[9,64,128]{2,1,0:T(8,128)(2,1)S(1)} collective-permute-done((bf16[9,64,128]{2,1,0:T(8,128)(2,1)S(1)}, bf16[9,64,128]{2,1,0:T(8,128)(2,1)S(1)}, u32[]{:S(2)}, u32[]{:S(2)}) %collective-permute-start.16) | collective-permute-done | bytes 147488 | tf_op jit(solution)/shard_map/ppermute | solution.py:346
  45.3 1.3 %collective-permute-done.17.got_y = bf16[9,64,128]{2,1,0:T(8,128)(2,1)S(1)} collective-permute-done((bf16[9,64,128]{2,1,0:T(8,128)(2,1)S(1)}, bf16[9,64,128]{2,1,0:T(8,128)(2,1)S(1)}, u32[]{:S(2)}, u32[]{:S(2)}) %collective-permute-start.17) | collective-permute-done | bytes 147488 | tf_op jit(solution)/shard_map/ppermute | solution.py:346
  46.7 1.7 %collective-permute-start.18 = (bf16[9,64,128]{2,1,0:T(8,128)(2,1)S(1)}, bf16[9,64,128]{2,1,0:T(8,128)(2,1)S(1)}, u32[]{:S(2)}, u32[]{:S(2)}) collective-permute-start(bf16[9,64,128]{2,1,0:T(8,128)(2,1)S(1)} %get-tuple-element.102), channel_id=1, source_target_pairs={{2,6},{3,7},{6,10},{7,11},{10,14},{11,15},{14,12},{15,13},{12,8},{... | collective-permute-start | bytes 442376 | tf_op jit(solution)/shard_map/ppermute | solution.py:346
  49.2 1.6 %collective-permute-start.25 = (bf16[8,64,128]{2,1,0:T(8,128)(2,1)S(1)}, bf16[8,64,128]{2,1,0:T(8,128)(2,1)S(1)}, u32[]{:S(2)}, u32[]{:S(2)}) collective-permute-start(bf16[8,64,128]{2,1,0:T(8,128)(2,1)S(1)} %get-tuple-element.115), channel_id=1, source_target_pairs={{2,6},{3,7},{6,10},{7,11},{10,14},{11,15},{14,12},{15,13},{12,8},{... | collective-permute-start | bytes 393224 | tf_op jit(solution)/shard_map/ppermute | solution.py:346
  51.3 1.7 %collective-permute-done.18.got_x = bf16[9,64,128]{2,1,0:T(8,128)(2,1)S(1)} collective-permute-done((bf16[9,64,128]{2,1,0:T(8,128)(2,1)S(1)}, bf16[9,64,128]{2,1,0:T(8,128)(2,1)S(1)}, u32[]{:S(2)}, u32[]{:S(2)}) %collective-permute-start.18) | collective-permute-done | bytes 147488 | tf_op jit(solution)/shard_map/ppermute | solution.py:346
  53.0 1.3 %collective-permute-done.19.got_y = bf16[9,64,128]{2,1,0:T(8,128)(2,1)S(1)} collective-permute-done((bf16[9,64,128]{2,1,0:T(8,128)(2,1)S(1)}, bf16[9,64,128]{2,1,0:T(8,128)(2,1)S(1)}, u32[]{:S(2)}, u32[]{:S(2)}) %collective-permute-start.19) | collective-permute-done | bytes 147488 | tf_op jit(solution)/shard_map/ppermute | solution.py:346
  55.3 1.2 %collective-permute-start.21 = (bf16[9,64,128]{2,1,0:T(8,128)(2,1)S(1)}, bf16[9,64,128]{2,1,0:T(8,128)(2,1)S(1)}, u32[]{:S(2)}, u32[]{:S(2)}) collective-permute-start(bf16[9,64,128]{2,1,0:T(8,128)(2,1)S(1)} %get-tuple-element.106), channel_id=1, source_target_pairs={{2,0},{3,1},{6,2},{7,3},{10,6},{11,7},{14,10},{15,11},{12,14},{13,... | collective-permute-start | bytes 442376 | tf_op jit(solution)/shard_map/ppermute | solution.py:346
  57.0 1.8 %collective-permute-start.27 = (bf16[8,64,128]{2,1,0:T(8,128)(2,1)S(1)}, bf16[8,64,128]{2,1,0:T(8,128)(2,1)S(1)}, u32[]{:S(2)}, u32[]{:S(2)}) collective-permute-start(bf16[8,64,128]{2,1,0:T(8,128)(2,1)S(1)} %get-tuple-element.117), channel_id=1, source_target_pairs={{2,6},{3,7},{6,10},{7,11},{10,14},{11,15},{14,12},{15,13},{12,8},{... | collective-permute-start | bytes 393224 | tf_op jit(solution)/shard_map/ppermute | solution.py:346
  61.3 1.3 %collective-permute-start.23 = (bf16[9,64,128]{2,1,0:T(8,128)(2,1)S(1)}, bf16[9,64,128]{2,1,0:T(8,128)(2,1)S(1)}, u32[]{:S(2)}, u32[]{:S(2)}) collective-permute-start(bf16[9,64,128]{2,1,0:T(8,128)(2,1)S(1)} %get-tuple-element.109), channel_id=1, source_target_pairs={{2,0},{3,1},{6,2},{7,3},{10,6},{11,7},{14,10},{15,11},{12,14},{13,... | collective-permute-start | bytes 442376 | tf_op jit(solution)/shard_map/ppermute | solution.py:346
  63.4 1.2 %collective-permute-start.28 = (bf16[8,64,128]{2,1,0:T(8,128)(2,1)S(1)}, bf16[8,64,128]{2,1,0:T(8,128)(2,1)S(1)}, u32[]{:S(2)}, u32[]{:S(2)}) collective-permute-start(bf16[8,64,128]{2,1,0:T(8,128)(2,1)S(1)} %get-tuple-element.118), channel_id=1, source_target_pairs={{2,0},{3,1},{6,2},{7,3},{10,6},{11,7},{14,10},{15,11},{12,14},{13,... | collective-permute-start | bytes 393224 | tf_op jit(solution)/shard_map/ppermute | solution.py:346
  64.5 0.9 %collective-permute-start.29 = (bf16[8,64,128]{2,1,0:T(8,128)(2,1)S(1)}, bf16[8,64,128]{2,1,0:T(8,128)(2,1)S(1)}, u32[]{:S(2)}, u32[]{:S(2)}) collective-permute-start(bf16[8,64,128]{2,1,0:T(8,128)(2,1)S(1)} %get-tuple-element.119), channel_id=1, source_target_pairs={{2,6},{3,7},{6,10},{7,11},{10,14},{11,15},{14,12},{15,13},{12,8},{... | collective-permute-start | bytes 393224 | tf_op jit(solution)/shard_map/ppermute | solution.py:346
  65.4 2.9 %collective-permute-done.28.q_x = bf16[8,64,128]{2,1,0:T(8,128)(2,1)S(1)} collective-permute-done((bf16[8,64,128]{2,1,0:T(8,128)(2,1)S(1)}, bf16[8,64,128]{2,1,0:T(8,128)(2,1)S(1)}, u32[]{:S(2)}, u32[]{:S(2)}) %collective-permute-start.28) | collective-permute-done | bytes 131104 | tf_op jit(solution)/shard_map/ppermute | solution.py:346
  68.4 1.1 %collective-permute-done.29.q_y = bf16[8,64,128]{2,1,0:T(8,128)(2,1)S(1)} collective-permute-done((bf16[8,64,128]{2,1,0:T(8,128)(2,1)S(1)}, bf16[8,64,128]{2,1,0:T(8,128)(2,1)S(1)}, u32[]{:S(2)}, u32[]{:S(2)}) %collective-permute-start.29) | collective-permute-done | bytes 131104 | tf_op jit(solution)/shard_map/ppermute | solution.py:346
  (61 shorter events, 18.9 us)
Async XLA Ops:
  1.6 1.5 %collective-permute-start = (bf16[8,64,128]{2,1,0:T(8,128)(2,1)S(1)}, bf16[8,64,128]{2,1,0:T(8,128)(2,1)S(1)}, u32[]{:S(2)}, u32[]{:S(2)}) collective-permute-start(bf16[8,64,128]{2,1,0:T(8,128)(2,1)S(1)} %get-tuple-element.125), channel_id=1, source_target_pairs={{0,1},{1,0},{2,3},{3,2},{4,5},{5,4},{6,7},{7,6},{8,9},{9,8},{10,11... | collective-permute-start | bytes 393224 | tf_op jit(solution)/shard_map/ppermute | solution.py:347
  3.2 11.6 %collective-permute-start.4 = (bf16[64,128,128]{2,1,0:T(8,128)(2,1)}, bf16[64,128,128]{2,1,0:T(8,128)(2,1)S(1)}, u32[]{:S(2)}, u32[]{:S(2)}) collective-permute-start(bf16[64,128,128]{2,1,0:T(8,128)(2,1)} %param.6), channel_id=1, source_target_pairs={{0,1},{1,0},{2,3},{3,2},{4,5},{5,4},{6,7},{7,6},{8,9},{9,8},{10,11... | collective-permute-start | bytes 6291464 | tf_op jit(solution)/shard_map/ppermute | solution.py:347
  3.6 4.0 %collective-permute-start.3 = (s32[64]{0:T(128)}, s32[64]{0:T(128)S(1)}, u32[]{:S(2)}, u32[]{:S(2)}) collective-permute-start(s32[64]{0:T(128)} %param.8), channel_id=1, source_target_pairs={{0,1},{1,0},{2,3},{3,2},{4,5},{5,4},{6,7},{7,6},{8,9},{9,8},{10,11... | collective-permute-start | bytes 776 | tf_op jit(solution)/shard_map/ppermute | solution.py:347
  3.8 9.5 %collective-permute-start.2 = (bf16[16,64,128]{2,1,0:T(8,128)(2,1)S(1)}, bf16[16,64,128]{2,1,0:T(8,128)(2,1)S(1)}, u32[]{:S(2)}, u32[]{:S(2)}) collective-permute-start(bf16[16,64,128]{2,1,0:T(8,128)(2,1)S(1)} %pad_maximum_fusion.refs_0_), channel_id=1, source_target_pairs={{2,0},{3,1},{6,2},{7,3},{10,6},{11,7},{14,10},{15,11},{12,14},{13,... | collective-permute-start | bytes 786440 | tf_op jit(solution)/shard_map/ppermute | solution.py:346
  6.7 8.1 %collective-permute-start.1 = (bf16[16,64,128]{2,1,0:T(8,128)(2,1)S(1)}, bf16[16,64,128]{2,1,0:T(8,128)(2,1)S(1)}, u32[]{:S(2)}, u32[]{:S(2)}) collective-permute-start(bf16[16,64,128]{2,1,0:T(8,128)(2,1)S(1)} %pad_maximum_fusion.refs_0_), channel_id=1, source_target_pairs={{2,6},{3,7},{6,10},{7,11},{10,14},{11,15},{14,12},{15,13},{12,8},{... | collective-permute-start | bytes 786440 | tf_op jit(solution)/shard_map/ppermute | solution.py:346
  14.8 5.5 %collective-permute-start.5 = (bf16[8,64,128]{2,1,0:T(8,128)(2,1)S(1)}, bf16[8,64,128]{2,1,0:T(8,128)(2,1)S(1)}, u32[]{:S(2)}, u32[]{:S(2)}) collective-permute-start(bf16[8,64,128]{2,1,0:T(8,128)(2,1)S(1)} %get-tuple-element.71.refs_1_), channel_id=1, source_target_pairs={{2,6},{3,7},{6,10},{7,11},{10,14},{11,15},{14,12},{15,13},{12,8},{... | collective-permute-start | bytes 393224 | tf_op jit(solution)/shard_map/ppermute | solution.py:346
  16.0 6.4 %collective-permute-start.6 = (bf16[8,64,128]{2,1,0:T(8,128)(2,1)S(1)}, bf16[8,64,128]{2,1,0:T(8,128)(2,1)S(1)}, u32[]{:S(2)}, u32[]{:S(2)}) collective-permute-start(bf16[8,64,128]{2,1,0:T(8,128)(2,1)S(1)} %get-tuple-element.72.refs_2_), channel_id=1, source_target_pairs={{2,0},{3,1},{6,2},{7,3},{10,6},{11,7},{14,10},{15,11},{12,14},{13,... | collective-permute-start | bytes 393224 | tf_op jit(solution)/shard_map/ppermute | solution.py:346
  16.9 7.5 %collective-permute-start.9 = (bf16[8,64,128]{2,1,0:T(8,128)(2,1)S(1)}, bf16[8,64,128]{2,1,0:T(8,128)(2,1)S(1)}, u32[]{:S(2)}, u32[]{:S(2)}) collective-permute-start(bf16[8,64,128]{2,1,0:T(8,128)(2,1)S(1)} %get-tuple-element.77.refs_3_), channel_id=1, source_target_pairs={{2,0},{3,1},{6,2},{7,3},{10,6},{11,7},{14,10},{15,11},{12,14},{13,... | collective-permute-start | bytes 393224 | tf_op jit(solution)/shard_map/ppermute | solution.py:346
  18.5 6.7 %collective-permute-start.10 = (bf16[8,64,128]{2,1,0:T(8,128)(2,1)S(1)}, bf16[8,64,128]{2,1,0:T(8,128)(2,1)S(1)}, u32[]{:S(2)}, u32[]{:S(2)}) collective-permute-start(bf16[8,64,128]{2,1,0:T(8,128)(2,1)S(1)} %get-tuple-element.78.refs_4_), channel_id=1, source_target_pairs={{2,6},{3,7},{6,10},{7,11},{10,14},{11,15},{14,12},{15,13},{12,8},{... | collective-permute-start | bytes 393224 | tf_op jit(solution)/shard_map/ppermute | solution.py:346
  20.3 10.7 %copy-start = (f32[128]{0:T(128)S(1)}, f32[128]{0:T(128)}, u32[]{:S(2)}) copy-start(f32[128]{0:T(128)} %param.10) | copy-start | bytes 1540
  22.4 6.1 %collective-permute-start.7 = (bf16[8,64,128]{2,1,0:T(8,128)(2,1)S(1)}, bf16[8,64,128]{2,1,0:T(8,128)(2,1)S(1)}, u32[]{:S(2)}, u32[]{:S(2)}) collective-permute-start(bf16[8,64,128]{2,1,0:T(8,128)(2,1)S(1)} %collective-permute-done.5.refs_5_), channel_id=1, source_target_pairs={{2,6},{3,7},{6,10},{7,11},{10,14},{11,15},{14,12},{15,13},{12,8},{... | collective-permute-start | bytes 393224 | tf_op jit(solution)/shard_map/ppermute | solution.py:346
  24.0 5.0 %collective-permute-start.8 = (bf16[8,64,128]{2,1,0:T(8,128)(2,1)S(1)}, bf16[8,64,128]{2,1,0:T(8,128)(2,1)S(1)}, u32[]{:S(2)}, u32[]{:S(2)}) collective-permute-start(bf16[8,64,128]{2,1,0:T(8,128)(2,1)S(1)} %collective-permute-done.6.refs_6_), channel_id=1, source_target_pairs={{2,0},{3,1},{6,2},{7,3},{10,6},{11,7},{14,10},{15,11},{12,14},{13,... | collective-permute-start | bytes 393224 | tf_op jit(solution)/shard_map/ppermute | solution.py:346
  24.4 6.6 %collective-permute-start.13 = (bf16[8,64,128]{2,1,0:T(8,128)(2,1)S(1)}, bf16[8,64,128]{2,1,0:T(8,128)(2,1)S(1)}, u32[]{:S(2)}, u32[]{:S(2)}) collective-permute-start(bf16[8,64,128]{2,1,0:T(8,128)(2,1)S(1)} %collective-permute-done.9.refs_7_), channel_id=1, source_target_pairs={{2,0},{3,1},{6,2},{7,3},{10,6},{11,7},{14,10},{15,11},{12,14},{13,... | collective-permute-start | bytes 393224 | tf_op jit(solution)/shard_map/ppermute | solution.py:346
  25.2 6.2 %collective-permute-start.14 = (bf16[8,64,128]{2,1,0:T(8,128)(2,1)S(1)}, bf16[8,64,128]{2,1,0:T(8,128)(2,1)S(1)}, u32[]{:S(2)}, u32[]{:S(2)}) collective-permute-start(bf16[8,64,128]{2,1,0:T(8,128)(2,1)S(1)} %collective-permute-done.10.refs_8_), channel_id=1, source_target_pairs={{2,6},{3,7},{6,10},{7,11},{10,14},{11,15},{14,12},{15,13},{12,8},{... | collective-permute-start | bytes 393224 | tf_op jit(solution)/shard_map/ppermute | solution.py:346
  29.0 5.0 %collective-permute-start.11 = (bf16[8,64,128]{2,1,0:T(8,128)(2,1)S(1)}, bf16[8,64,128]{2,1,0:T(8,128)(2,1)S(1)}, u32[]{:S(2)}, u32[]{:S(2)}) collective-permute-start(bf16[8,64,128]{2,1,0:T(8,128)(2,1)S(1)} %collective-permute-done.7.refs_0_), channel_id=1, source_target_pairs={{2,6},{3,7},{6,10},{7,11},{10,14},{11,15},{14,12},{15,13},{12,8},{... | collective-permute-start | bytes 393224 | tf_op jit(solution)/shard_map/ppermute | solution.py:346
  30.5 5.0 %collective-permute-start.12 = (bf16[8,64,128]{2,1,0:T(8,128)(2,1)S(1)}, bf16[8,64,128]{2,1,0:T(8,128)(2,1)S(1)}, u32[]{:S(2)}, u32[]{:S(2)}) collective-permute-start(bf16[8,64,128]{2,1,0:T(8,128)(2,1)S(1)} %collective-permute-done.8.refs_1_), channel_id=1, source_target_pairs={{2,0},{3,1},{6,2},{7,3},{10,6},{11,7},{14,10},{15,11},{12,14},{13,... | collective-permute-start | bytes 393224 | tf_op jit(solution)/shard_map/ppermute | solution.py:346
  37.4 1.2 %collective-permute-start.15 = (f32[2,128]{1,0:T(2,128)S(1)}, f32[2,128]{1,0:T(2,128)S(1)}, u32[]{:S(2)}, u32[]{:S(2)}) collective-permute-start(f32[2,128]{1,0:T(2,128)S(1)} %get-tuple-element.89.mine), channel_id=1, source_target_pairs={{0,1},{1,0},{2,3},{3,2},{4,5},{5,4},{6,7},{7,6},{8,9},{9,8},{10,11... | collective-permute-start | bytes 3080 | tf_op jit(solution)/shard_map/ppermute | solution.py:347
  39.3 6.0 %collective-permute-start.16 = (bf16[9,64,128]{2,1,0:T(8,128)(2,1)S(1)}, bf16[9,64,128]{2,1,0:T(8,128)(2,1)S(1)}, u32[]{:S(2)}, u32[]{:S(2)}) collective-permute-start(bf16[9,64,128]{2,1,0:T(8,128)(2,1)S(1)} %get-tuple-element.99), channel_id=1, source_target_pairs={{2,6},{3,7},{6,10},{7,11},{10,14},{11,15},{14,12},{15,13},{12,8},{... | collective-permute-start | bytes 442376 | tf_op jit(solution)/shard_map/ppermute | solution.py:346
  40.9 5.7 %collective-permute-start.17 = (bf16[9,64,128]{2,1,0:T(8,128)(2,1)S(1)}, bf16[9,64,128]{2,1,0:T(8,128)(2,1)S(1)}, u32[]{:S(2)}, u32[]{:S(2)}) collective-permute-start(bf16[9,64,128]{2,1,0:T(8,128)(2,1)S(1)} %get-tuple-element.100), channel_id=1, source_target_pairs={{2,0},{3,1},{6,2},{7,3},{10,6},{11,7},{14,10},{15,11},{12,14},{13,... | collective-permute-start | bytes 442376 | tf_op jit(solution)/shard_map/ppermute | solution.py:346
  46.7 6.3 %collective-permute-start.18 = (bf16[9,64,128]{2,1,0:T(8,128)(2,1)S(1)}, bf16[9,64,128]{2,1,0:T(8,128)(2,1)S(1)}, u32[]{:S(2)}, u32[]{:S(2)}) collective-permute-start(bf16[9,64,128]{2,1,0:T(8,128)(2,1)S(1)} %get-tuple-element.102), channel_id=1, source_target_pairs={{2,6},{3,7},{6,10},{7,11},{10,14},{11,15},{14,12},{15,13},{12,8},{... | collective-permute-start | bytes 442376 | tf_op jit(solution)/shard_map/ppermute | solution.py:346
  48.4 5.9 %collective-permute-start.19 = (bf16[9,64,128]{2,1,0:T(8,128)(2,1)S(1)}, bf16[9,64,128]{2,1,0:T(8,128)(2,1)S(1)}, u32[]{:S(2)}, u32[]{:S(2)}) collective-permute-start(bf16[9,64,128]{2,1,0:T(8,128)(2,1)S(1)} %get-tuple-element.103), channel_id=1, source_target_pairs={{2,0},{3,1},{6,2},{7,3},{10,6},{11,7},{14,10},{15,11},{12,14},{13,... | collective-permute-start | bytes 442376 | tf_op jit(solution)/shard_map/ppermute | solution.py:346
  48.8 7.9 %collective-permute-start.24 = (bf16[8,64,128]{2,1,0:T(8,128)(2,1)S(1)}, bf16[8,64,128]{2,1,0:T(8,128)(2,1)S(1)}, u32[]{:S(2)}, u32[]{:S(2)}) collective-permute-start(bf16[8,64,128]{2,1,0:T(8,128)(2,1)S(1)} %get-tuple-element.114), channel_id=1, source_target_pairs={{2,0},{3,1},{6,2},{7,3},{10,6},{11,7},{14,10},{15,11},{12,14},{13,... | collective-permute-start | bytes 393224 | tf_op jit(solution)/shard_map/ppermute | solution.py:346
  49.2 7.5 %collective-permute-start.25 = (bf16[8,64,128]{2,1,0:T(8,128)(2,1)S(1)}, bf16[8,64,128]{2,1,0:T(8,128)(2,1)S(1)}, u32[]{:S(2)}, u32[]{:S(2)}) collective-permute-start(bf16[8,64,128]{2,1,0:T(8,128)(2,1)S(1)} %get-tuple-element.115), channel_id=1, source_target_pairs={{2,6},{3,7},{6,10},{7,11},{10,14},{11,15},{14,12},{15,13},{12,8},{... | collective-permute-start | bytes 393224 | tf_op jit(solution)/shard_map/ppermute | solution.py:346
  54.5 5.2 %collective-permute-start.20 = (bf16[9,64,128]{2,1,0:T(8,128)(2,1)S(1)}, bf16[9,64,128]{2,1,0:T(8,128)(2,1)S(1)}, u32[]{:S(2)}, u32[]{:S(2)}) collective-permute-start(bf16[9,64,128]{2,1,0:T(8,128)(2,1)S(1)} %get-tuple-element.105), channel_id=1, source_target_pairs={{2,6},{3,7},{6,10},{7,11},{10,14},{11,15},{14,12},{15,13},{12,8},{... | collective-permute-start | bytes 442376 | tf_op jit(solution)/shard_map/ppermute | solution.py:346
  55.3 5.1 %collective-permute-start.21 = (bf16[9,64,128]{2,1,0:T(8,128)(2,1)S(1)}, bf16[9,64,128]{2,1,0:T(8,128)(2,1)S(1)}, u32[]{:S(2)}, u32[]{:S(2)}) collective-permute-start(bf16[9,64,128]{2,1,0:T(8,128)(2,1)S(1)} %get-tuple-element.106), channel_id=1, source_target_pairs={{2,0},{3,1},{6,2},{7,3},{10,6},{11,7},{14,10},{15,11},{12,14},{13,... | collective-permute-start | bytes 442376 | tf_op jit(solution)/shard_map/ppermute | solution.py:346
  56.7 6.4 %collective-permute-start.26 = (bf16[8,64,128]{2,1,0:T(8,128)(2,1)S(1)}, bf16[8,64,128]{2,1,0:T(8,128)(2,1)S(1)}, u32[]{:S(2)}, u32[]{:S(2)}) collective-permute-start(bf16[8,64,128]{2,1,0:T(8,128)(2,1)S(1)} %get-tuple-element.116), channel_id=1, source_target_pairs={{2,0},{3,1},{6,2},{7,3},{10,6},{11,7},{14,10},{15,11},{12,14},{13,... | collective-permute-start | bytes 393224 | tf_op jit(solution)/shard_map/ppermute | solution.py:346
  57.0 6.3 %collective-permute-start.27 = (bf16[8,64,128]{2,1,0:T(8,128)(2,1)S(1)}, bf16[8,64,128]{2,1,0:T(8,128)(2,1)S(1)}, u32[]{:S(2)}, u32[]{:S(2)}) collective-permute-start(bf16[8,64,128]{2,1,0:T(8,128)(2,1)S(1)} %get-tuple-element.117), channel_id=1, source_target_pairs={{2,6},{3,7},{6,10},{7,11},{10,14},{11,15},{14,12},{15,13},{12,8},{... | collective-permute-start | bytes 393224 | tf_op jit(solution)/shard_map/ppermute | solution.py:346
  60.6 8.9 %collective-permute-start.22 = (bf16[9,64,128]{2,1,0:T(8,128)(2,1)S(1)}, bf16[9,64,128]{2,1,0:T(8,128)(2,1)S(1)}, u32[]{:S(2)}, u32[]{:S(2)}) collective-permute-start(bf16[9,64,128]{2,1,0:T(8,128)(2,1)S(1)} %get-tuple-element.108), channel_id=1, source_target_pairs={{2,6},{3,7},{6,10},{7,11},{10,14},{11,15},{14,12},{15,13},{12,8},{... | collective-permute-start | bytes 442376 | tf_op jit(solution)/shard_map/ppermute | solution.py:346
  61.3 8.2 %collective-permute-start.23 = (bf16[9,64,128]{2,1,0:T(8,128)(2,1)S(1)}, bf16[9,64,128]{2,1,0:T(8,128)(2,1)S(1)}, u32[]{:S(2)}, u32[]{:S(2)}) collective-permute-start(bf16[9,64,128]{2,1,0:T(8,128)(2,1)S(1)} %get-tuple-element.109), channel_id=1, source_target_pairs={{2,0},{3,1},{6,2},{7,3},{10,6},{11,7},{14,10},{15,11},{12,14},{13,... | collective-permute-start | bytes 442376 | tf_op jit(solution)/shard_map/ppermute | solution.py:346
  63.4 5.0 %collective-permute-start.28 = (bf16[8,64,128]{2,1,0:T(8,128)(2,1)S(1)}, bf16[8,64,128]{2,1,0:T(8,128)(2,1)S(1)}, u32[]{:S(2)}, u32[]{:S(2)}) collective-permute-start(bf16[8,64,128]{2,1,0:T(8,128)(2,1)S(1)} %get-tuple-element.118), channel_id=1, source_target_pairs={{2,0},{3,1},{6,2},{7,3},{10,6},{11,7},{14,10},{15,11},{12,14},{13,... | collective-permute-start | bytes 393224 | tf_op jit(solution)/shard_map/ppermute | solution.py:346
  64.5 5.0 %collective-permute-start.29 = (bf16[8,64,128]{2,1,0:T(8,128)(2,1)S(1)}, bf16[8,64,128]{2,1,0:T(8,128)(2,1)S(1)}, u32[]{:S(2)}, u32[]{:S(2)}) collective-permute-start(bf16[8,64,128]{2,1,0:T(8,128)(2,1)S(1)} %get-tuple-element.119), channel_id=1, source_target_pairs={{2,6},{3,7},{6,10},{7,11},{10,14},{11,15},{14,12},{15,13},{12,8},{... | collective-permute-start | bytes 393224 | tf_op jit(solution)/shard_map/ppermute | solution.py:346
  69.7 1.4 %collective-permute-start.30 = (bf16[8,64,128]{2,1,0:T(8,128)(2,1)S(1)}, bf16[8,64,128]{2,1,0:T(8,128)(2,1)S(1)}, u32[]{:S(2)}, u32[]{:S(2)}) collective-permute-start(bf16[8,64,128]{2,1,0:T(8,128)(2,1)S(1)} %get-tuple-element.122), channel_id=1, source_target_pairs={{0,1},{1,0},{2,3},{3,2},{4,5},{5,4},{6,7},{7,6},{8,9},{9,8},{10,11... | collective-permute-start | bytes 393224 | tf_op jit(solution)/shard_map/ppermute | solution.py:347

commit v4 on v3

--- a/solution.py
+++ b/solution.py
@@ -266,6 +266,8 @@
             out[j] = _backward(base * mp + j, table, wo, ws).astype(out.dtype)
     for out in outs[:2]:
         out[mp] = _split(dpart[...])
+    for out in outs[2:]:
+        out[mp:] = jnp.zeros_like(out[mp:])
 
 
 def numer_kernel(ring, spots, mp, wo, ws, table, *outs):
@@ -289,12 +291,11 @@
 
 def add_kernel(part_x, part_y, got_x, got_y, *refs):
     n = part_x.shape[0]
-    tails = got_x.shape[0] > n
+    tails = len(refs) == 4
     out_x, out_y = refs[1:3] if tails else refs
     for part, got, out in ((part_x, got_x, out_x), (part_y, got_y, out_y)):
         out[:n] = (part[...] + got[:n].astype(F32)).astype(BF16)
-        if tails:
-            out[n] = got[n]
+        out[n:] = got[n:]
     if tails:
         refs[3][...] = refs[0][...] + (_join(got_x[n]) + _join(got_y[n]))
 
@@ -411,12 +412,13 @@
     piece = shape((mp, kh, q), BF16)
     piece_d = shape((mp + 1, kh, q), BF16)
     wide = shape((mp, kh, q), F32)
+    piece_q = shape((mp + 1, kh, q), BF16)
     dsum_shape = shape((kh, q), F32)
     far = opposite - 1
     table, evidence, dsum, p_x, p_y, q_x, q_y = _call(
         functools.partial(table_kernel, ring, [(opposite, 0), (opposite, 1), (-far, 0), (far, 1)], mp),
         [wo, ws, real, imag, stats, stats_x, w2],
-        [shape((19, 2 * kh, n2), BF16), shape((1, n2), F32), dsum_shape, piece_d, piece_d, piece, piece],
+        [shape((19, 2 * kh, n2), BF16), shape((1, n2), F32), dsum_shape, piece_d, piece_d, piece_q, piece_q],
     )
     for dist in range(far, -1, -1):
         p_x, p_y = send(p_x, 1, 0), send(p_y, -1, 0)
@@ -426,7 +428,7 @@
             px, py, qx, qy = _call(functools.partial(numer_kernel, ring, spots, mp), [wo, ws, table], [wide] * 4)
             p_x, p_y, dsum = _call(add_kernel, [px, py, p_x, p_y, dsum], [piece_d, piece_d, dsum_shape])
             if dist > 1:
-                q_x, q_y = _call(add_kernel, [qx, qy, q_x, q_y], [piece, piece])
+                q_x, q_y = _call(add_kernel, [qx, qy, q_x, q_y], [piece_q, piece_q])
     own, far = _call(own_kernel, [qx, qy, p_x, p_y, q_x, q_y, dsum], [shape((mp, kh, q), F32), piece])
     new_refs = _call(
         functools.partial(final_kernel, ring), [own, core_swap(far)], [shape((mp, k, q), F32)], keep=False

time: 72.1 us -> 70.9 us (0.983)
  waiting for transfers between devices: 25.4 us -> 24.1 us
    ppermute x26, waiting for transfers between devices: 21.6 us -> 20.3 us  [shards(): lax.ppermute(a, 'dp', ring_perm(order, shift, cross))]
  transfers between devices with their start and end apart: 31 -> 31, of which waited for: 22 -> 21; matrix products, arithmetic and copies ran while one was open for 10% -> 10% of each run, Pallas kernels for 7% -> 7%
where the time goes in v4:
time: 70.9 us; the launch traced here: 70.7 us
  starting transfers between devices  28.8 us (41%)
  waiting for transfers between devices  24.1 us (34%)
  Pallas kernels  8.46 us (12%)
  other arithmetic  6.52 us (9%)
  local copies, waits for them, and re-layouts  1.68 us (2%)
  between operations  0.83 us (1%)
    ppermute x26, starting transfers between devices, shards(): lax.ppermute(a, 'dp', ring_perm(order, shift, cross))  27.5 us
    ppermute x26, waiting for transfers between devices, shards(): lax.ppermute(a, 'dp', ring_perm(order, shift, cross))  20.3 us
    pallas_call x15, Pallas kernels, _call(): pl.pallas_call(kernel, out_shape=[pltpu.VMEM(o.shape, o.dtype) for o in o...  8.46 us
    transpose x2, other arithmetic, shards(): jnp.transpose((a.astype(F32) * g[:, None, :]).astype(BF16), (1, 0, 2))  4.3 us
    ppermute x5, waiting for transfers between devices, shards(): lax.ppermute(a, 'dp', [(i, i ^ 1) for i in range(2 * chips)])  3.85 us
  transfers between devices with their start and end apart: 31, of which 21 were waited for; matrix products, arithmetic and copies ran while one was open for 10% of the time, Pallas kernels for 7%

profile of v4, /device:TPU:0, one launch (start us, length us, event | category | flops | bytes accessed | tf_op | source)
XLA Modules:
  0.0 70.7 jit_solution(783794037213700762)
XLA Ops:
  0.6 1.0 %constant_dynamic-slice_fusion.1 = (bf16[8,64,128]{2,1,0:T(8,128)(2,1)S(1)}, bf16[8,64,128]{2,1,0:T(8,128)(2,1)S(1)}) fusion(bf16[8,128,128]{2,1,0:T(8,128)(2,1)} %param.7, s32[]{:T(128)S(6)} %select_n.7, s32[]{:T(128)S(6)} %select_n.8), kind=kLoop, calls=%fused_computation.27 | loop fusion | bytes 524296 | tf_op jit(solution)/shard_map/dynamic_slice | solution.py:351
  2.2 1.0 %collective-permute-done = bf16[8,64,128]{2,1,0:T(8,128)(2,1)S(1)} collective-permute-done((bf16[8,64,128]{2,1,0:T(8,128)(2,1)S(1)}, bf16[8,64,128]{2,1,0:T(8,128)(2,1)S(1)}, u32[]{:S(2)}, u32[]{:S(2)}) %collective-permute-start) | collective-permute-done | bytes 131104 | tf_op jit(solution)/shard_map/ppermute | solution.py:348
  3.8 2.9 %collective-permute-start.2 = (bf16[16,64,128]{2,1,0:T(8,128)(2,1)S(1)}, bf16[16,64,128]{2,1,0:T(8,128)(2,1)S(1)}, u32[]{:S(2)}, u32[]{:S(2)}) collective-permute-start(bf16[16,64,128]{2,1,0:T(8,128)(2,1)S(1)} %pad_maximum_fusion.refs_0_), channel_id=1, source_target_pairs={{2,0},{3,1},{6,2},{7,3},{10,6},{11,7},{14,10},{15,11},{12,14},{13,... | collective-permute-start | bytes 786440 | tf_op jit(solution)/shard_map/ppermute | solution.py:347
  6.7 0.9 %collective-permute-done.3 = s32[64]{0:T(128)S(1)} collective-permute-done((s32[64]{0:T(128)}, s32[64]{0:T(128)S(1)}, u32[]{:S(2)}, u32[]{:S(2)}) %collective-permute-start.3) | collective-permute-done | bytes 288 | tf_op jit(solution)/shard_map/ppermute | solution.py:348
  10.1 2.9 %fusion.wo = bf16[128,64,128]{2,1,0:T(8,128)(2,1)S(1)} fusion(bf16[64,128,128]{2,1,0:T(8,128)(2,1)} %param.6, f32[64,128]{1,0:T(8,128)S(1)} %get-tuple-element.127), kind=kLoop, calls=%fused_computation.2 | loop fusion | flops 3145728 | bytes 4227072 | tf_op jit(solution)/shard_map/transpose | solution.py:368
  13.2 1.5 %collective-permute-done.1.from_left = bf16[16,64,128]{2,1,0:T(8,128)(2,1)S(1)} collective-permute-done((bf16[16,64,128]{2,1,0:T(8,128)(2,1)S(1)}, bf16[16,64,128]{2,1,0:T(8,128)(2,1)S(1)}, u32[]{:S(2)}, u32[]{:S(2)}) %collective-permute-start.1) | collective-permute-done | bytes 262176 | tf_op jit(solution)/shard_map/ppermute | solution.py:347
  14.8 1.2 %collective-permute-start.5 = (bf16[8,64,128]{2,1,0:T(8,128)(2,1)S(1)}, bf16[8,64,128]{2,1,0:T(8,128)(2,1)S(1)}, u32[]{:S(2)}, u32[]{:S(2)}) collective-permute-start(bf16[8,64,128]{2,1,0:T(8,128)(2,1)S(1)} %get-tuple-element.71.refs_1_), channel_id=1, source_target_pairs={{2,6},{3,7},{6,10},{7,11},{10,14},{11,15},{14,12},{15,13},{12,8},{... | collective-permute-start | bytes 393224 | tf_op jit(solution)/shard_map/ppermute | solution.py:347
  16.9 1.6 %collective-permute-start.9 = (bf16[8,64,128]{2,1,0:T(8,128)(2,1)S(1)}, bf16[8,64,128]{2,1,0:T(8,128)(2,1)S(1)}, u32[]{:S(2)}, u32[]{:S(2)}) collective-permute-start(bf16[8,64,128]{2,1,0:T(8,128)(2,1)S(1)} %get-tuple-element.77.refs_3_), channel_id=1, source_target_pairs={{2,0},{3,1},{6,2},{7,3},{10,6},{11,7},{14,10},{15,11},{12,14},{13,... | collective-permute-start | bytes 393224 | tf_op jit(solution)/shard_map/ppermute | solution.py:347
  18.9 1.4 %fusion.1.ws = bf16[128,64,128]{2,1,0:T(8,128)(2,1)S(1)} fusion(bf16[64,128,128]{2,1,0:T(8,128)(2,1)S(1)} %collective-permute-done.4, f32[64,128]{1,0:T(8,128)S(1)} %get-tuple-element.126), kind=kLoop, calls=%fused_computation.3 | loop fusion | flops 3145728 | bytes 4227072 | tf_op jit(solution)/shard_map/transpose | solution.py:368
  20.3 2.1 %collective-permute-done.6.refs_6_ = bf16[8,64,128]{2,1,0:T(8,128)(2,1)S(1)} collective-permute-done((bf16[8,64,128]{2,1,0:T(8,128)(2,1)S(1)}, bf16[8,64,128]{2,1,0:T(8,128)(2,1)S(1)}, u32[]{:S(2)}, u32[]{:S(2)}) %collective-permute-start.6) | collective-permute-done | bytes 131104 | tf_op jit(solution)/shard_map/ppermute | solution.py:347
  22.4 1.6 %collective-permute-start.7 = (bf16[8,64,128]{2,1,0:T(8,128)(2,1)S(1)}, bf16[8,64,128]{2,1,0:T(8,128)(2,1)S(1)}, u32[]{:S(2)}, u32[]{:S(2)}) collective-permute-start(bf16[8,64,128]{2,1,0:T(8,128)(2,1)S(1)} %collective-permute-done.5.refs_5_), channel_id=1, source_target_pairs={{2,6},{3,7},{6,10},{7,11},{10,14},{11,15},{14,12},{15,13},{12,8},{... | collective-permute-start | bytes 393224 | tf_op jit(solution)/shard_map/ppermute | solution.py:347
  25.2 1.3 %collective-permute-start.14 = (bf16[8,64,128]{2,1,0:T(8,128)(2,1)S(1)}, bf16[8,64,128]{2,1,0:T(8,128)(2,1)S(1)}, u32[]{:S(2)}, u32[]{:S(2)}) collective-permute-start(bf16[8,64,128]{2,1,0:T(8,128)(2,1)S(1)} %collective-permute-done.10.refs_8_), channel_id=1, source_target_pairs={{2,6},{3,7},{6,10},{7,11},{10,14},{11,15},{14,12},{15,13},{12,8},{... | collective-permute-start | bytes 393224 | tf_op jit(solution)/shard_map/ppermute | solution.py:347
  26.5 2.0 %shard_map.78 = (f32[19,128,128]{2,1,0:T(8,128)S(1)}, f32[64,128]{1,0:T(8,128)S(1)}) custom-call(bf16[128,64,128]{2,1,0:T(8,128)(2,1)S(1)} %fusion.wo, bf16[128,64,128]{2,1,0:T(8,128)(2,1)S(1)} %fusion.1.ws, bf16[16,64,128]{2,1,0:T(8,128)(2,1)S(1)} %pad_maximum_fusion.refs_0_, bf16[8,64,128]{2,1,0:T(8,128)(2,1)S(1)} %get-tuple-element.71.refs_1_, ...), custom_call_target="tpu_custom_call" | custom-call | flops 1 | bytes 1 | tf_op jit(solution)/shard_map/pallas_call | solution.py:319
  29.0 1.6 %collective-permute-start.11 = (bf16[8,64,128]{2,1,0:T(8,128)(2,1)S(1)}, bf16[8,64,128]{2,1,0:T(8,128)(2,1)S(1)}, u32[]{:S(2)}, u32[]{:S(2)}) collective-permute-start(bf16[8,64,128]{2,1,0:T(8,128)(2,1)S(1)} %collective-permute-done.7.refs_0_), channel_id=1, source_target_pairs={{2,6},{3,7},{6,10},{7,11},{10,14},{11,15},{14,12},{15,13},{12,8},{... | collective-permute-start | bytes 393224 | tf_op jit(solution)/shard_map/ppermute | solution.py:347
  31.4 0.9 %shard_map.79 = (f32[19,128,128]{2,1,0:T(8,128)S(1)}, f32[64,128]{1,0:T(8,128)S(1)}) custom-call(bf16[128,64,128]{2,1,0:T(8,128)(2,1)S(1)} %fusion.wo, bf16[128,64,128]{2,1,0:T(8,128)(2,1)S(1)} %fusion.1.ws, bf16[8,64,128]{2,1,0:T(8,128)(2,1)S(1)} %collective-permute-done.7.refs_0_, ...), custom_call_target="tpu_custom_call", output_to_operand_aliasing={{0}: (6, {}), {1}: (7, {})} | custom-call | flops 1 | bytes 1 | tf_op jit(solution)/shard_map/pallas_call | solution.py:319
  32.3 1.6 %collective-permute-done.11.refs_0_ = bf16[8,64,128]{2,1,0:T(8,128)(2,1)S(1)} collective-permute-done((bf16[8,64,128]{2,1,0:T(8,128)(2,1)S(1)}, bf16[8,64,128]{2,1,0:T(8,128)(2,1)S(1)}, u32[]{:S(2)}, u32[]{:S(2)}) %collective-permute-start.11) | collective-permute-done | bytes 131104 | tf_op jit(solution)/shard_map/ppermute | solution.py:347
  33.9 1.6 %collective-permute-done.12.refs_1_ = bf16[8,64,128]{2,1,0:T(8,128)(2,1)S(1)} collective-permute-done((bf16[8,64,128]{2,1,0:T(8,128)(2,1)S(1)}, bf16[8,64,128]{2,1,0:T(8,128)(2,1)S(1)}, u32[]{:S(2)}, u32[]{:S(2)}) %collective-permute-start.12) | collective-permute-done | bytes 131104 | tf_op jit(solution)/shard_map/ppermute | solution.py:347
  35.6 1.8 %shard_map.80 = (f32[19,128,128]{2,1,0:T(8,128)S(1)}, f32[64,128]{1,0:T(8,128)S(1)}, f32[19,64,128]{2,1,0:T(8,128)S(1)}, f32[17,64,128]{2,1,0:T(8,128)S(1)}, f32[2,128]{1,0:T(2,128)S(1)}) custom-call(bf16[128,64,128]{2,1,0:T(8,128)(2,1)S(1)} %fusion.wo, bf16[128,64,128]{2,1,0:T(8,128)(2,1)S(1)} %fusion.1.ws, ...), custom_call_target="tpu_custom_call", output_to_operand_aliasing={{0}: (6, {}), {1}: (7, {})} | custom-call | flops 1 | bytes 1 | tf_op jit(solution)/shard_map/pallas_call | solution.py:319
  37.4 1.1 %collective-permute-done.15.other = f32[2,128]{1,0:T(2,128)S(1)} collective-permute-done((f32[2,128]{1,0:T(2,128)S(1)}, f32[2,128]{1,0:T(2,128)S(1)}, u32[]{:S(2)}, u32[]{:S(2)}) %collective-permute-start.15) | collective-permute-done | bytes 1056 | tf_op jit(solution)/shard_map/ppermute | solution.py:348
  39.3 1.6 %collective-permute-start.16 = (bf16[9,64,128]{2,1,0:T(8,128)(2,1)S(1)}, bf16[9,64,128]{2,1,0:T(8,128)(2,1)S(1)}, u32[]{:S(2)}, u32[]{:S(2)}) collective-permute-start(bf16[9,64,128]{2,1,0:T(8,128)(2,1)S(1)} %get-tuple-element.99), channel_id=1, source_target_pairs={{2,6},{3,7},{6,10},{7,11},{10,14},{11,15},{14,12},{15,13},{12,8},{... | collective-permute-start | bytes 442376 | tf_op jit(solution)/shard_map/ppermute | solution.py:347
  41.8 1.6 %collective-permute-start.25 = (bf16[9,64,128]{2,1,0:T(8,128)(2,1)S(1)}, bf16[9,64,128]{2,1,0:T(8,128)(2,1)S(1)}, u32[]{:S(2)}, u32[]{:S(2)}) collective-permute-start(bf16[9,64,128]{2,1,0:T(8,128)(2,1)S(1)} %get-tuple-element.115), channel_id=1, source_target_pairs={{2,6},{3,7},{6,10},{7,11},{10,14},{11,15},{14,12},{15,13},{12,8},{... | collective-permute-start | bytes 442376 | tf_op jit(solution)/shard_map/ppermute | solution.py:347
  43.9 2.1 %collective-permute-done.16.got_x = bf16[9,64,128]{2,1,0:T(8,128)(2,1)S(1)} collective-permute-done((bf16[9,64,128]{2,1,0:T(8,128)(2,1)S(1)}, bf16[9,64,128]{2,1,0:T(8,128)(2,1)S(1)}, u32[]{:S(2)}, u32[]{:S(2)}) %collective-permute-start.16) | collective-permute-done | bytes 147488 | tf_op jit(solution)/shard_map/ppermute | solution.py:347
  46.0 1.6 %collective-permute-done.17.got_y = bf16[9,64,128]{2,1,0:T(8,128)(2,1)S(1)} collective-permute-done((bf16[9,64,128]{2,1,0:T(8,128)(2,1)S(1)}, bf16[9,64,128]{2,1,0:T(8,128)(2,1)S(1)}, u32[]{:S(2)}, u32[]{:S(2)}) %collective-permute-start.17) | collective-permute-done | bytes 147488 | tf_op jit(solution)/shard_map/ppermute | solution.py:347
  47.8 1.7 %collective-permute-start.18 = (bf16[9,64,128]{2,1,0:T(8,128)(2,1)S(1)}, bf16[9,64,128]{2,1,0:T(8,128)(2,1)S(1)}, u32[]{:S(2)}, u32[]{:S(2)}) collective-permute-start(bf16[9,64,128]{2,1,0:T(8,128)(2,1)S(1)} %get-tuple-element.102), channel_id=1, source_target_pairs={{2,6},{3,7},{6,10},{7,11},{10,14},{11,15},{14,12},{15,13},{12,8},{... | collective-permute-start | bytes 442376 | tf_op jit(solution)/shard_map/ppermute | solution.py:347
  50.9 1.6 %collective-permute-start.27 = (bf16[9,64,128]{2,1,0:T(8,128)(2,1)S(1)}, bf16[9,64,128]{2,1,0:T(8,128)(2,1)S(1)}, u32[]{:S(2)}, u32[]{:S(2)}) collective-permute-start(bf16[9,64,128]{2,1,0:T(8,128)(2,1)S(1)} %get-tuple-element.117), channel_id=1, source_target_pairs={{2,6},{3,7},{6,10},{7,11},{10,14},{11,15},{14,12},{15,13},{12,8},{... | collective-permute-start | bytes 442376 | tf_op jit(solution)/shard_map/ppermute | solution.py:347
  52.5 1.7 %collective-permute-done.18.got_x = bf16[9,64,128]{2,1,0:T(8,128)(2,1)S(1)} collective-permute-done((bf16[9,64,128]{2,1,0:T(8,128)(2,1)S(1)}, bf16[9,64,128]{2,1,0:T(8,128)(2,1)S(1)}, u32[]{:S(2)}, u32[]{:S(2)}) %collective-permute-start.18) | collective-permute-done | bytes 147488 | tf_op jit(solution)/shard_map/ppermute | solution.py:347
  54.8 1.9 %collective-permute-start.20 = (bf16[9,64,128]{2,1,0:T(8,128)(2,1)S(1)}, bf16[9,64,128]{2,1,0:T(8,128)(2,1)S(1)}, u32[]{:S(2)}, u32[]{:S(2)}) collective-permute-start(bf16[9,64,128]{2,1,0:T(8,128)(2,1)S(1)} %get-tuple-element.105), channel_id=1, source_target_pairs={{2,6},{3,7},{6,10},{7,11},{10,14},{11,15},{14,12},{15,13},{12,8},{... | collective-permute-start | bytes 442376 | tf_op jit(solution)/shard_map/ppermute | solution.py:347
  58.3 1.6 %collective-permute-start.29 = (bf16[9,64,128]{2,1,0:T(8,128)(2,1)S(1)}, bf16[9,64,128]{2,1,0:T(8,128)(2,1)S(1)}, u32[]{:S(2)}, u32[]{:S(2)}) collective-permute-start(bf16[9,64,128]{2,1,0:T(8,128)(2,1)S(1)} %get-tuple-element.119), channel_id=1, source_target_pairs={{2,6},{3,7},{6,10},{7,11},{10,14},{11,15},{14,12},{15,13},{12,8},{... | collective-permute-start | bytes 442376 | tf_op jit(solution)/shard_map/ppermute | solution.py:347
  59.9 1.2 %collective-permute-done.20.got_x = bf16[9,64,128]{2,1,0:T(8,128)(2,1)S(1)} collective-permute-done((bf16[9,64,128]{2,1,0:T(8,128)(2,1)S(1)}, bf16[9,64,128]{2,1,0:T(8,128)(2,1)S(1)}, u32[]{:S(2)}, u32[]{:S(2)}) %collective-permute-start.20) | collective-permute-done | bytes 147488 | tf_op jit(solution)/shard_map/ppermute | solution.py:347
  61.9 1.2 %collective-permute-start.22 = (bf16[9,64,128]{2,1,0:T(8,128)(2,1)S(1)}, bf16[9,64,128]{2,1,0:T(8,128)(2,1)S(1)}, u32[]{:S(2)}, u32[]{:S(2)}) collective-permute-start(bf16[9,64,128]{2,1,0:T(8,128)(2,1)S(1)} %get-tuple-element.108), channel_id=1, source_target_pairs={{2,6},{3,7},{6,10},{7,11},{10,14},{11,15},{14,12},{15,13},{12,8},{... | collective-permute-start | bytes 442376 | tf_op jit(solution)/shard_map/ppermute | solution.py:347
  64.7 2.4 %collective-permute-done.22.p_x = bf16[9,64,128]{2,1,0:T(8,128)(2,1)S(1)} collective-permute-done((bf16[9,64,128]{2,1,0:T(8,128)(2,1)S(1)}, bf16[9,64,128]{2,1,0:T(8,128)(2,1)S(1)}, u32[]{:S(2)}, u32[]{:S(2)}) %collective-permute-start.22) | collective-permute-done | bytes 147488 | tf_op jit(solution)/shard_map/ppermute | solution.py:347
  67.1 1.2 %collective-permute-done.23.p_y = bf16[9,64,128]{2,1,0:T(8,128)(2,1)S(1)} collective-permute-done((bf16[9,64,128]{2,1,0:T(8,128)(2,1)S(1)}, bf16[9,64,128]{2,1,0:T(8,128)(2,1)S(1)}, u32[]{:S(2)}, u32[]{:S(2)}) %collective-permute-start.23) | collective-permute-done | bytes 147488 | tf_op jit(solution)/shard_map/ppermute | solution.py:347
  (61 shorter events, 18.5 us)
Async XLA Ops:
  1.6 1.5 %collective-permute-start = (bf16[8,64,128]{2,1,0:T(8,128)(2,1)S(1)}, bf16[8,64,128]{2,1,0:T(8,128)(2,1)S(1)}, u32[]{:S(2)}, u32[]{:S(2)}) collective-permute-start(bf16[8,64,128]{2,1,0:T(8,128)(2,1)S(1)} %get-tuple-element.125), channel_id=1, source_target_pairs={{0,1},{1,0},{2,3},{3,2},{4,5},{5,4},{6,7},{7,6},{8,9},{9,8},{10,11... | collective-permute-start | bytes 393224 | tf_op jit(solution)/shard_map/ppermute | solution.py:348
  3.2 11.6 %collective-permute-start.4 = (bf16[64,128,128]{2,1,0:T(8,128)(2,1)}, bf16[64,128,128]{2,1,0:T(8,128)(2,1)S(1)}, u32[]{:S(2)}, u32[]{:S(2)}) collective-permute-start(bf16[64,128,128]{2,1,0:T(8,128)(2,1)} %param.6), channel_id=1, source_target_pairs={{0,1},{1,0},{2,3},{3,2},{4,5},{5,4},{6,7},{7,6},{8,9},{9,8},{10,11... | collective-permute-start | bytes 6291464 | tf_op jit(solution)/shard_map/ppermute | solution.py:348
  3.6 4.0 %collective-permute-start.3 = (s32[64]{0:T(128)}, s32[64]{0:T(128)S(1)}, u32[]{:S(2)}, u32[]{:S(2)}) collective-permute-start(s32[64]{0:T(128)} %param.8), channel_id=1, source_target_pairs={{0,1},{1,0},{2,3},{3,2},{4,5},{5,4},{6,7},{7,6},{8,9},{9,8},{10,11... | collective-permute-start | bytes 776 | tf_op jit(solution)/shard_map/ppermute | solution.py:348
  3.8 9.5 %collective-permute-start.2 = (bf16[16,64,128]{2,1,0:T(8,128)(2,1)S(1)}, bf16[16,64,128]{2,1,0:T(8,128)(2,1)S(1)}, u32[]{:S(2)}, u32[]{:S(2)}) collective-permute-start(bf16[16,64,128]{2,1,0:T(8,128)(2,1)S(1)} %pad_maximum_fusion.refs_0_), channel_id=1, source_target_pairs={{2,0},{3,1},{6,2},{7,3},{10,6},{11,7},{14,10},{15,11},{12,14},{13,... | collective-permute-start | bytes 786440 | tf_op jit(solution)/shard_map/ppermute | solution.py:347
  6.7 8.1 %collective-permute-start.1 = (bf16[16,64,128]{2,1,0:T(8,128)(2,1)S(1)}, bf16[16,64,128]{2,1,0:T(8,128)(2,1)S(1)}, u32[]{:S(2)}, u32[]{:S(2)}) collective-permute-start(bf16[16,64,128]{2,1,0:T(8,128)(2,1)S(1)} %pad_maximum_fusion.refs_0_), channel_id=1, source_target_pairs={{2,6},{3,7},{6,10},{7,11},{10,14},{11,15},{14,12},{15,13},{12,8},{... | collective-permute-start | bytes 786440 | tf_op jit(solution)/shard_map/ppermute | solution.py:347
  14.8 5.5 %collective-permute-start.5 = (bf16[8,64,128]{2,1,0:T(8,128)(2,1)S(1)}, bf16[8,64,128]{2,1,0:T(8,128)(2,1)S(1)}, u32[]{:S(2)}, u32[]{:S(2)}) collective-permute-start(bf16[8,64,128]{2,1,0:T(8,128)(2,1)S(1)} %get-tuple-element.71.refs_1_), channel_id=1, source_target_pairs={{2,6},{3,7},{6,10},{7,11},{10,14},{11,15},{14,12},{15,13},{12,8},{... | collective-permute-start | bytes 393224 | tf_op jit(solution)/shard_map/ppermute | solution.py:347
  16.0 6.4 %collective-permute-start.6 = (bf16[8,64,128]{2,1,0:T(8,128)(2,1)S(1)}, bf16[8,64,128]{2,1,0:T(8,128)(2,1)S(1)}, u32[]{:S(2)}, u32[]{:S(2)}) collective-permute-start(bf16[8,64,128]{2,1,0:T(8,128)(2,1)S(1)} %get-tuple-element.72.refs_2_), channel_id=1, source_target_pairs={{2,0},{3,1},{6,2},{7,3},{10,6},{11,7},{14,10},{15,11},{12,14},{13,... | collective-permute-start | bytes 393224 | tf_op jit(solution)/shard_map/ppermute | solution.py:347
  16.9 7.5 %collective-permute-start.9 = (bf16[8,64,128]{2,1,0:T(8,128)(2,1)S(1)}, bf16[8,64,128]{2,1,0:T(8,128)(2,1)S(1)}, u32[]{:S(2)}, u32[]{:S(2)}) collective-permute-start(bf16[8,64,128]{2,1,0:T(8,128)(2,1)S(1)} %get-tuple-element.77.refs_3_), channel_id=1, source_target_pairs={{2,0},{3,1},{6,2},{7,3},{10,6},{11,7},{14,10},{15,11},{12,14},{13,... | collective-permute-start | bytes 393224 | tf_op jit(solution)/shard_map/ppermute | solution.py:347
  18.5 6.7 %collective-permute-start.10 = (bf16[8,64,128]{2,1,0:T(8,128)(2,1)S(1)}, bf16[8,64,128]{2,1,0:T(8,128)(2,1)S(1)}, u32[]{:S(2)}, u32[]{:S(2)}) collective-permute-start(bf16[8,64,128]{2,1,0:T(8,128)(2,1)S(1)} %get-tuple-element.78.refs_4_), channel_id=1, source_target_pairs={{2,6},{3,7},{6,10},{7,11},{10,14},{11,15},{14,12},{15,13},{12,8},{... | collective-permute-start | bytes 393224 | tf_op jit(solution)/shard_map/ppermute | solution.py:347
  20.3 10.7 %copy-start = (f32[128]{0:T(128)S(1)}, f32[128]{0:T(128)}, u32[]{:S(2)}) copy-start(f32[128]{0:T(128)} %param.10) | copy-start | bytes 1540
  22.4 6.1 %collective-permute-start.7 = (bf16[8,64,128]{2,1,0:T(8,128)(2,1)S(1)}, bf16[8,64,128]{2,1,0:T(8,128)(2,1)S(1)}, u32[]{:S(2)}, u32[]{:S(2)}) collective-permute-start(bf16[8,64,128]{2,1,0:T(8,128)(2,1)S(1)} %collective-permute-done.5.refs_5_), channel_id=1, source_target_pairs={{2,6},{3,7},{6,10},{7,11},{10,14},{11,15},{14,12},{15,13},{12,8},{... | collective-permute-start | bytes 393224 | tf_op jit(solution)/shard_map/ppermute | solution.py:347
  24.0 5.0 %collective-permute-start.8 = (bf16[8,64,128]{2,1,0:T(8,128)(2,1)S(1)}, bf16[8,64,128]{2,1,0:T(8,128)(2,1)S(1)}, u32[]{:S(2)}, u32[]{:S(2)}) collective-permute-start(bf16[8,64,128]{2,1,0:T(8,128)(2,1)S(1)} %collective-permute-done.6.refs_6_), channel_id=1, source_target_pairs={{2,0},{3,1},{6,2},{7,3},{10,6},{11,7},{14,10},{15,11},{12,14},{13,... | collective-permute-start | bytes 393224 | tf_op jit(solution)/shard_map/ppermute | solution.py:347
  24.4 6.6 %collective-permute-start.13 = (bf16[8,64,128]{2,1,0:T(8,128)(2,1)S(1)}, bf16[8,64,128]{2,1,0:T(8,128)(2,1)S(1)}, u32[]{:S(2)}, u32[]{:S(2)}) collective-permute-start(bf16[8,64,128]{2,1,0:T(8,128)(2,1)S(1)} %collective-permute-done.9.refs_7_), channel_id=1, source_target_pairs={{2,0},{3,1},{6,2},{7,3},{10,6},{11,7},{14,10},{15,11},{12,14},{13,... | collective-permute-start | bytes 393224 | tf_op jit(solution)/shard_map/ppermute | solution.py:347
  25.2 6.2 %collective-permute-start.14 = (bf16[8,64,128]{2,1,0:T(8,128)(2,1)S(1)}, bf16[8,64,128]{2,1,0:T(8,128)(2,1)S(1)}, u32[]{:S(2)}, u32[]{:S(2)}) collective-permute-start(bf16[8,64,128]{2,1,0:T(8,128)(2,1)S(1)} %collective-permute-done.10.refs_8_), channel_id=1, source_target_pairs={{2,6},{3,7},{6,10},{7,11},{10,14},{11,15},{14,12},{15,13},{12,8},{... | collective-permute-start | bytes 393224 | tf_op jit(solution)/shard_map/ppermute | solution.py:347
  29.0 5.0 %collective-permute-start.11 = (bf16[8,64,128]{2,1,0:T(8,128)(2,1)S(1)}, bf16[8,64,128]{2,1,0:T(8,128)(2,1)S(1)}, u32[]{:S(2)}, u32[]{:S(2)}) collective-permute-start(bf16[8,64,128]{2,1,0:T(8,128)(2,1)S(1)} %collective-permute-done.7.refs_0_), channel_id=1, source_target_pairs={{2,6},{3,7},{6,10},{7,11},{10,14},{11,15},{14,12},{15,13},{12,8},{... | collective-permute-start | bytes 393224 | tf_op jit(solution)/shard_map/ppermute | solution.py:347
  30.5 5.0 %collective-permute-start.12 = (bf16[8,64,128]{2,1,0:T(8,128)(2,1)S(1)}, bf16[8,64,128]{2,1,0:T(8,128)(2,1)S(1)}, u32[]{:S(2)}, u32[]{:S(2)}) collective-permute-start(bf16[8,64,128]{2,1,0:T(8,128)(2,1)S(1)} %collective-permute-done.8.refs_1_), channel_id=1, source_target_pairs={{2,0},{3,1},{6,2},{7,3},{10,6},{11,7},{14,10},{15,11},{12,14},{13,... | collective-permute-start | bytes 393224 | tf_op jit(solution)/shard_map/ppermute | solution.py:347
  37.4 1.2 %collective-permute-start.15 = (f32[2,128]{1,0:T(2,128)S(1)}, f32[2,128]{1,0:T(2,128)S(1)}, u32[]{:S(2)}, u32[]{:S(2)}) collective-permute-start(f32[2,128]{1,0:T(2,128)S(1)} %get-tuple-element.89.mine), channel_id=1, source_target_pairs={{0,1},{1,0},{2,3},{3,2},{4,5},{5,4},{6,7},{7,6},{8,9},{9,8},{10,11... | collective-permute-start | bytes 3080 | tf_op jit(solution)/shard_map/ppermute | solution.py:348
  39.3 6.7 %collective-permute-start.16 = (bf16[9,64,128]{2,1,0:T(8,128)(2,1)S(1)}, bf16[9,64,128]{2,1,0:T(8,128)(2,1)S(1)}, u32[]{:S(2)}, u32[]{:S(2)}) collective-permute-start(bf16[9,64,128]{2,1,0:T(8,128)(2,1)S(1)} %get-tuple-element.99), channel_id=1, source_target_pairs={{2,6},{3,7},{6,10},{7,11},{10,14},{11,15},{14,12},{15,13},{12,8},{... | collective-permute-start | bytes 442376 | tf_op jit(solution)/shard_map/ppermute | solution.py:347
  40.9 6.7 %collective-permute-start.17 = (bf16[9,64,128]{2,1,0:T(8,128)(2,1)S(1)}, bf16[9,64,128]{2,1,0:T(8,128)(2,1)S(1)}, u32[]{:S(2)}, u32[]{:S(2)}) collective-permute-start(bf16[9,64,128]{2,1,0:T(8,128)(2,1)S(1)} %get-tuple-element.100), channel_id=1, source_target_pairs={{2,0},{3,1},{6,2},{7,3},{10,6},{11,7},{14,10},{15,11},{12,14},{13,... | collective-permute-start | bytes 442376 | tf_op jit(solution)/shard_map/ppermute | solution.py:347
  41.4 9.0 %collective-permute-start.24 = (bf16[9,64,128]{2,1,0:T(8,128)(2,1)S(1)}, bf16[9,64,128]{2,1,0:T(8,128)(2,1)S(1)}, u32[]{:S(2)}, u32[]{:S(2)}) collective-permute-start(bf16[9,64,128]{2,1,0:T(8,128)(2,1)S(1)} %get-tuple-element.114), channel_id=1, source_target_pairs={{2,0},{3,1},{6,2},{7,3},{10,6},{11,7},{14,10},{15,11},{12,14},{13,... | collective-permute-start | bytes 442376 | tf_op jit(solution)/shard_map/ppermute | solution.py:347
  41.8 8.6 %collective-permute-start.25 = (bf16[9,64,128]{2,1,0:T(8,128)(2,1)S(1)}, bf16[9,64,128]{2,1,0:T(8,128)(2,1)S(1)}, u32[]{:S(2)}, u32[]{:S(2)}) collective-permute-start(bf16[9,64,128]{2,1,0:T(8,128)(2,1)S(1)} %get-tuple-element.115), channel_id=1, source_target_pairs={{2,6},{3,7},{6,10},{7,11},{10,14},{11,15},{14,12},{15,13},{12,8},{... | collective-permute-start | bytes 442376 | tf_op jit(solution)/shard_map/ppermute | solution.py:347
  47.8 6.5 %collective-permute-start.18 = (bf16[9,64,128]{2,1,0:T(8,128)(2,1)S(1)}, bf16[9,64,128]{2,1,0:T(8,128)(2,1)S(1)}, u32[]{:S(2)}, u32[]{:S(2)}) collective-permute-start(bf16[9,64,128]{2,1,0:T(8,128)(2,1)S(1)} %get-tuple-element.102), channel_id=1, source_target_pairs={{2,6},{3,7},{6,10},{7,11},{10,14},{11,15},{14,12},{15,13},{12,8},{... | collective-permute-start | bytes 442376 | tf_op jit(solution)/shard_map/ppermute | solution.py:347
  49.5 5.2 %collective-permute-start.19 = (bf16[9,64,128]{2,1,0:T(8,128)(2,1)S(1)}, bf16[9,64,128]{2,1,0:T(8,128)(2,1)S(1)}, u32[]{:S(2)}, u32[]{:S(2)}) collective-permute-start(bf16[9,64,128]{2,1,0:T(8,128)(2,1)S(1)} %get-tuple-element.103), channel_id=1, source_target_pairs={{2,0},{3,1},{6,2},{7,3},{10,6},{11,7},{14,10},{15,11},{12,14},{13,... | collective-permute-start | bytes 442376 | tf_op jit(solution)/shard_map/ppermute | solution.py:347
  50.4 6.9 %collective-permute-start.26 = (bf16[9,64,128]{2,1,0:T(8,128)(2,1)S(1)}, bf16[9,64,128]{2,1,0:T(8,128)(2,1)S(1)}, u32[]{:S(2)}, u32[]{:S(2)}) collective-permute-start(bf16[9,64,128]{2,1,0:T(8,128)(2,1)S(1)} %get-tuple-element.116), channel_id=1, source_target_pairs={{2,0},{3,1},{6,2},{7,3},{10,6},{11,7},{14,10},{15,11},{12,14},{13,... | collective-permute-start | bytes 442376 | tf_op jit(solution)/shard_map/ppermute | solution.py:347
  50.9 6.8 %collective-permute-start.27 = (bf16[9,64,128]{2,1,0:T(8,128)(2,1)S(1)}, bf16[9,64,128]{2,1,0:T(8,128)(2,1)S(1)}, u32[]{:S(2)}, u32[]{:S(2)}) collective-permute-start(bf16[9,64,128]{2,1,0:T(8,128)(2,1)S(1)} %get-tuple-element.117), channel_id=1, source_target_pairs={{2,6},{3,7},{6,10},{7,11},{10,14},{11,15},{14,12},{15,13},{12,8},{... | collective-permute-start | bytes 442376 | tf_op jit(solution)/shard_map/ppermute | solution.py:347
  54.8 6.3 %collective-permute-start.20 = (bf16[9,64,128]{2,1,0:T(8,128)(2,1)S(1)}, bf16[9,64,128]{2,1,0:T(8,128)(2,1)S(1)}, u32[]{:S(2)}, u32[]{:S(2)}) collective-permute-start(bf16[9,64,128]{2,1,0:T(8,128)(2,1)S(1)} %get-tuple-element.105), channel_id=1, source_target_pairs={{2,6},{3,7},{6,10},{7,11},{10,14},{11,15},{14,12},{15,13},{12,8},{... | collective-permute-start | bytes 442376 | tf_op jit(solution)/shard_map/ppermute | solution.py:347
  56.6 5.1 %collective-permute-start.21 = (bf16[9,64,128]{2,1,0:T(8,128)(2,1)S(1)}, bf16[9,64,128]{2,1,0:T(8,128)(2,1)S(1)}, u32[]{:S(2)}, u32[]{:S(2)}) collective-permute-start(bf16[9,64,128]{2,1,0:T(8,128)(2,1)S(1)} %get-tuple-element.106), channel_id=1, source_target_pairs={{2,0},{3,1},{6,2},{7,3},{10,6},{11,7},{14,10},{15,11},{12,14},{13,... | collective-permute-start | bytes 442376 | tf_op jit(solution)/shard_map/ppermute | solution.py:347
  57.8 6.9 %collective-permute-start.28 = (bf16[9,64,128]{2,1,0:T(8,128)(2,1)S(1)}, bf16[9,64,128]{2,1,0:T(8,128)(2,1)S(1)}, u32[]{:S(2)}, u32[]{:S(2)}) collective-permute-start(bf16[9,64,128]{2,1,0:T(8,128)(2,1)S(1)} %get-tuple-element.118), channel_id=1, source_target_pairs={{2,0},{3,1},{6,2},{7,3},{10,6},{11,7},{14,10},{15,11},{12,14},{13,... | collective-permute-start | bytes 442376 | tf_op jit(solution)/shard_map/ppermute | solution.py:347
  58.3 6.4 %collective-permute-start.29 = (bf16[9,64,128]{2,1,0:T(8,128)(2,1)S(1)}, bf16[9,64,128]{2,1,0:T(8,128)(2,1)S(1)}, u32[]{:S(2)}, u32[]{:S(2)}) collective-permute-start(bf16[9,64,128]{2,1,0:T(8,128)(2,1)S(1)} %get-tuple-element.119), channel_id=1, source_target_pairs={{2,6},{3,7},{6,10},{7,11},{10,14},{11,15},{14,12},{15,13},{12,8},{... | collective-permute-start | bytes 442376 | tf_op jit(solution)/shard_map/ppermute | solution.py:347
  61.9 5.2 %collective-permute-start.22 = (bf16[9,64,128]{2,1,0:T(8,128)(2,1)S(1)}, bf16[9,64,128]{2,1,0:T(8,128)(2,1)S(1)}, u32[]{:S(2)}, u32[]{:S(2)}) collective-permute-start(bf16[9,64,128]{2,1,0:T(8,128)(2,1)S(1)} %get-tuple-element.108), channel_id=1, source_target_pairs={{2,6},{3,7},{6,10},{7,11},{10,14},{11,15},{14,12},{15,13},{12,8},{... | collective-permute-start | bytes 442376 | tf_op jit(solution)/shard_map/ppermute | solution.py:347
  63.1 5.1 %collective-permute-start.23 = (bf16[9,64,128]{2,1,0:T(8,128)(2,1)S(1)}, bf16[9,64,128]{2,1,0:T(8,128)(2,1)S(1)}, u32[]{:S(2)}, u32[]{:S(2)}) collective-permute-start(bf16[9,64,128]{2,1,0:T(8,128)(2,1)S(1)} %get-tuple-element.109), channel_id=1, source_target_pairs={{2,0},{3,1},{6,2},{7,3},{10,6},{11,7},{14,10},{15,11},{12,14},{13,... | collective-permute-start | bytes 442376 | tf_op jit(solution)/shard_map/ppermute | solution.py:347
  68.4 1.4 %collective-permute-start.30 = (bf16[8,64,128]{2,1,0:T(8,128)(2,1)S(1)}, bf16[8,64,128]{2,1,0:T(8,128)(2,1)S(1)}, u32[]{:S(2)}, u32[]{:S(2)}) collective-permute-start(bf16[8,64,128]{2,1,0:T(8,128)(2,1)S(1)} %get-tuple-element.122), channel_id=1, source_target_pairs={{0,1},{1,0},{2,3},{3,2},{4,5},{5,4},{6,7},{7,6},{8,9},{9,8},{10,11... | collective-permute-start | bytes 393224 | tf_op jit(solution)/shard_map/ppermute | solution.py:348
